TPU v7x, 512 devices: a whole 4x4x16 slice. The times are simulated.
512 devices in a mesh: dp: 32 (over y, z_lo, core), expert: 16 (over z_hi, x).
Axes of the slice: x: 4, y: 4, z: 16 (z_hi: 4, z_lo: 4; z = z_hi * 4 + z_lo), core: 2. Of those that a mesh axis runs over, the one named last changes fastest.
Arguments:
- tokens: bfloat16 [2048, 4096], P('expert', 'dp'), may hold values from -6 to 6
- out_grad: bfloat16 [2048, 4096], P('expert', 'dp'), may hold values from -0.29882812 to 0.29882812
- expert_ids: int32 [2048, 2], P('expert'), may hold values from 0 to 15, all different within a row; in each aligned block of 128 rows (0 to 127, 128 to 255, ...) at most 30 rows name the same one
- gate_weights: float32 [2048, 2], P('expert'), may hold values from 0.1 to 1
- w_in: bfloat16 [16, 4096, 4096], P('expert', None, 'dp'), may hold values from -0.09375 to 0.09375
- w_out: bfloat16 [16, 4096, 4096], P('expert', 'dp'), may hold values from -0.09375 to 0.09375
Outputs:
- tokens_grad: bfloat16 [2048, 4096], P('expert', 'dp')
- w_in_grad: bfloat16 [16, 4096, 4096], P('expert', None, 'dp')
- w_out_grad: bfloat16 [16, 4096, 4096], P('expert', 'dp')
Inputs may be any that keep to these rules, and one draw needn't show every extreme that they name: `expert_ids`: in each row the two ids differ. In the rows of one block no expert is named by more than 30 rows, and in some blocks one expert is named by exactly 30.
All inputs are finite; a program needn't handle non-finite values.
Results may differ from a plain program's by a relative error of at most 0.03.
Values may be sent and summed in bfloat16 or wider, within the bound.
No kernel may reach another device: no remote copies, remote signals or barrier semaphores. Data moves between devices by JAX's collectives and lax.ppermute only.
A program may use at most 64 MiB of HBM per device.

v0:
```python
import jax
import jax.numpy as jnp
from jax import lax
from jax.sharding import PartitionSpec as P


def activate(value):
    return jax.nn.gelu(value, approximate=True)


def on_device(tokens, out_grad, expert_ids, gate_weights, w_in, w_out):
    tok_rows = tokens.shape[0]
    experts_all = lax.axis_size("expert")
    capacity = (5 * tok_rows + 2 * experts_all - 1) // (2 * experts_all)
    slots_all = experts_all * capacity
    onehot = (
        expert_ids[:, :, None] == jnp.arange(experts_all, dtype=jnp.int32)[None, None, :]
    ).astype(jnp.int32)
    counts = onehot.sum(1)
    prior = jnp.cumsum(counts, axis=0) - counts
    slot = jnp.sum(onehot * prior[:, None, :], axis=-1)
    kept = slot < capacity
    target = expert_ids * capacity + jnp.minimum(slot, capacity - 1)
    table = (target[:, :, None] == jnp.arange(slots_all, dtype=jnp.int32)[None, None, :]) & kept[
        :, :, None
    ]
    dispatch = jnp.sum(table.astype(jnp.float32), axis=1).astype(jnp.bfloat16)
    gate_slot = jnp.sum(jnp.where(table, gate_weights[:, :, None], 0.0), axis=(0, 1))
    contract_first = (((0,), (0,)), ((), ()))
    contract_last = (((1,), (1,)), ((), ()))
    whole_tok, whole_dy = (
        lax.all_gather(tokens, "dp", axis=1, tiled=True),
        lax.all_gather(out_grad, "dp", axis=1, tiled=True),
    )
    send_in = lax.dot_general(
        dispatch, whole_tok, contract_first, preferred_element_type=jnp.float32
    )
    send_in = send_in.astype(jnp.bfloat16).reshape(experts_all, capacity, -1)
    send_dy = lax.dot_general(
        dispatch, whole_dy, contract_first, preferred_element_type=jnp.float32
    )
    send_dy = (gate_slot[:, None] * send_dy).astype(jnp.bfloat16).reshape(experts_all, capacity, -1)
    send_in, send_dy = (send_in, send_dy)
    recv_in, recv_dy = (
        lax.all_to_all(send_in, "expert", split_axis=0, concat_axis=0, tiled=True),
        lax.all_to_all(send_dy, "expert", split_axis=0, concat_axis=0, tiled=True),
    )
    width = recv_in.shape[2]
    rows_in = recv_in.reshape(-1, width)
    rows_dy = recv_dy.reshape(-1, width)
    pre = jnp.dot(rows_in, w_in[0], preferred_element_type=jnp.float32)
    act_grad = lax.dot_general(rows_dy, w_out[0], contract_last, preferred_element_type=jnp.float32)
    act, pullback = jax.vjp(activate, pre)
    pre_grad = pullback(act_grad)[0].astype(jnp.bfloat16)
    act_low = act.astype(jnp.bfloat16)
    w_in_grad = lax.dot_general(
        rows_in, pre_grad, contract_first, preferred_element_type=jnp.float32
    )
    w_out_grad = lax.dot_general(
        act_low, rows_dy, contract_first, preferred_element_type=jnp.float32
    )
    partial_value = lax.dot_general(
        pre_grad, w_in[0], contract_last, preferred_element_type=jnp.float32
    )
    summed = lax.psum_scatter(
        partial_value.astype(jnp.bfloat16), "dp", scatter_dimension=1, tiled=True
    ).astype(jnp.float32)
    block_width = summed.shape[1]
    back = summed.astype(jnp.bfloat16).reshape(experts_all, capacity, block_width)
    returned = lax.all_to_all(back, "expert", split_axis=0, concat_axis=0, tiled=True)
    tokens_grad = jnp.dot(
        dispatch, returned.reshape(slots_all, block_width), preferred_element_type=jnp.float32
    )
    return (
        tokens_grad.astype(jnp.bfloat16),
        w_in_grad.astype(jnp.bfloat16)[None],
        w_out_grad.astype(jnp.bfloat16)[None],
    )


def solution(mesh):
    placed = (
        P("expert", "dp"),
        P("expert", "dp"),
        P("expert", None),
        P("expert", None),
        P("expert", None, "dp"),
        P("expert", "dp", None),
    )
    return jax.shard_map(
        on_device,
        mesh=mesh,
        in_specs=placed,
        out_specs=(P("expert", "dp"), P("expert", None, "dp"), P("expert", "dp", None)),
        check_vma=False,
    )
```

profile of v0, /device:TPU:2, one launch (start us, length us, event | category | flops | bytes accessed | tf_op | source)
XLA Modules:
  0.0 634.9 jit_solution(13675690546611767337)
XLA Ops:
  7.2 0.0 copy-start
  7.2 0.0 all-gather.5.cloned.1.call-start
  7.2 0.7 all-gather.5.cloned.1.call-update
  7.9 0.7 convert_reduce_fusion.1
  8.6 0.1 copy.21
  8.7 0.2 reduce_window_sum.11
  8.9 0.1 copy.23
  8.9 0.7 select_reduce_fusion.1
  9.7 0.7 minimum_add_fusion
  10.4 0.9 select_reduce_fusion
  11.2 69.1 %all-gather.5.cloned.1.call-done = bf16[128,4096]{1,0:T(8,128)(2,1)} async-done(((bf16[128,128]{1,0:T(8,128)(2,1)}), bf16[128,4096]{1,0:T(8,128)(2,1)}) %all-gather.5.cloned.1.call-update) | async-done | bytes 1048592 | tf_op jit(solution)/shard_map/all_gather | solution.py:32
  80.3 3.6 convolution_convert_fusion.1
  83.9 4.3 reshape.42
  88.1 13.9 %all-to-all-start.1 = ((bf16[16,20,4096]{2,1,0:T(8,128)(2,1)}), bf16[16,20,4096]{2,1,0:T(8,128)(2,1)}, u32[]{:S(2)}, u32[]{:S(2)}) async-start(bf16[16,20,4096]{2,1,0:T(8,128)(2,1)} %reshape.42), calls=%async_computation.1 | async-start | bytes 6291456 | tf_op jit(solution)/shard_map/all_to_all | solution.py:45
  102.0 0.0 all-gather.3.cloned.1.call-start
  102.1 0.7 all-gather.3.cloned.1.call-update
  102.8 158.4 %all-gather.3.cloned.1.call-done = bf16[128,4096]{1,0:T(8,128)(2,1)} async-done(((bf16[128,128]{1,0:T(8,128)(2,1)}), bf16[128,4096]{1,0:T(8,128)(2,1)}) %all-gather.3.cloned.1.call-update) | async-done | bytes 1048592 | tf_op jit(solution)/shard_map/all_gather | solution.py:33
  261.2 3.5 fusion
  264.7 4.3 reshape.40
  269.1 0.0 all-to-all-done.1
  269.1 17.1 %all-to-all-start = ((bf16[16,20,4096]{2,1,0:T(8,128)(2,1)}), bf16[16,20,4096]{2,1,0:T(8,128)(2,1)}, u32[]{:S(2)}, u32[]{:S(2)}) async-start(bf16[16,20,4096]{2,1,0:T(8,128)(2,1)} %reshape.40), calls=%async_computation | async-start | bytes 6291456 | tf_op jit(solution)/shard_map/all_to_all | solution.py:46
  286.2 0.0 reduce-scatter.4.cloned.1.call-start
  286.2 4.3 reshape.43
  290.5 0.0 copy-done
  290.5 2.6 fusion.4
  293.1 0.0 copy-start.2
  293.1 131.1 %all-to-all-done = bf16[16,20,4096]{2,1,0:T(8,128)(2,1)} async-done(((bf16[16,20,4096]{2,1,0:T(8,128)(2,1)}), bf16[16,20,4096]{2,1,0:T(8,128)(2,1)}, u32[]{:S(2)}, u32[]{:S(2)}) %all-to-all-start) | async-done | bytes 2621472 | tf_op jit(solution)/shard_map/all_to_all | solution.py:46
  424.2 4.4 reshape.41
  428.6 0.0 copy-done.2
  428.6 2.6 fusion.15
  431.2 2.4 convolution_convert_fusion
  433.6 4.5 copy.24
  438.1 0.0 reduce-scatter.4.cloned.1.call-update
  438.1 162.1 %reduce-scatter.4.cloned.1.call-done = bf16[128,320]{1,0:T(8,128)(2,1)} async-done(((bf16[4096,320]{1,0:T(8,128)(2,1)}), bf16[128,320]{1,0:T(8,128)(2,1)}) %reduce-scatter.4.cloned.1.call-update) | async-done | bytes 81936
  600.2 1.0 copy.25
  601.2 0.7 reshape.44
  601.9 12.0 %all-to-all-start.2 = ((bf16[16,20,128]{2,1,0:T(8,128)(2,1)}), bf16[16,20,128]{2,1,0:T(8,128)(2,1)S(1)}, u32[]{:S(2)}, u32[]{:S(2)}) async-start(bf16[16,20,128]{2,1,0:T(8,128)(2,1)} %reshape.44), calls=%async_computation.2 | async-start | bytes 196608 | tf_op jit(solution)/shard_map/all_to_all | solution.py:70
  613.9 0.0 copy-start.1
  613.9 3.6 fusion.2
  617.6 0.0 copy-done.1
  617.6 2.0 fusion.1
  619.6 7.9 %all-to-all-done.2 = bf16[16,20,128]{2,1,0:T(8,128)(2,1)S(1)} async-done(((bf16[16,20,128]{2,1,0:T(8,128)(2,1)}), bf16[16,20,128]{2,1,0:T(8,128)(2,1)S(1)}, u32[]{:S(2)}, u32[]{:S(2)}) %all-to-all-start.2) | async-done | bytes 81952 | tf_op jit(solution)/shard_map/all_to_all | solution.py:70
  627.5 0.8 convolution_convert_fusion.4
  (3 shorter events, 0.0 us)
Async XLA Ops:
  7.2 283.3 %copy-start = (bf16[1,4096,128]{2,1,0:T(8,128)(2,1)S(1)}, bf16[1,4096,128]{2,1,0:T(8,128)(2,1)}, u32[]{:S(2)}) copy-start(bf16[1,4096,128]{2,1,0:T(8,128)(2,1)} %param.10) | copy-start | bytes 3145732
  7.2 73.1 %all-gather.5.cloned.1.call-start = ((), (), s32[]{:S(2)}) async-start(), calls=%async_computation.5 | async-start | bytes 1081344 | tf_op jit(solution)/shard_map/all_gather | solution.py:32
  88.1 180.9 %all-to-all-start.1 = ((bf16[16,20,4096]{2,1,0:T(8,128)(2,1)}), bf16[16,20,4096]{2,1,0:T(8,128)(2,1)}, u32[]{:S(2)}, u32[]{:S(2)}) async-start(bf16[16,20,4096]{2,1,0:T(8,128)(2,1)} %reshape.42), calls=%async_computation.1 | async-start | bytes 6291456 | tf_op jit(solution)/shard_map/all_to_all | solution.py:45
  102.0 159.2 %all-gather.3.cloned.1.call-start = ((), (), s32[]{:S(2)}) async-start(), calls=%async_computation.4 | async-start | bytes 1081344 | tf_op jit(solution)/shard_map/all_gather | solution.py:33
  269.1 155.1 %all-to-all-start = ((bf16[16,20,4096]{2,1,0:T(8,128)(2,1)}), bf16[16,20,4096]{2,1,0:T(8,128)(2,1)}, u32[]{:S(2)}, u32[]{:S(2)}) async-start(bf16[16,20,4096]{2,1,0:T(8,128)(2,1)} %reshape.40), calls=%async_computation | async-start | bytes 6291456 | tf_op jit(solution)/shard_map/all_to_all | solution.py:46
  286.2 314.1 %reduce-scatter.4.cloned.1.call-start = ((), (), s32[]{:S(2)}) async-start(), calls=%async_computation.6 | async-start | bytes 3244032
  293.1 135.5 %copy-start.2 = (bf16[1,128,4096]{2,1,0:T(8,128)(2,1)S(1)}, bf16[1,128,4096]{2,1,0:T(8,128)(2,1)}, u32[]{:S(2)}) copy-start(bf16[1,128,4096]{2,1,0:T(8,128)(2,1)} %param.11) | copy-start | bytes 3145732
  601.9 25.6 %all-to-all-start.2 = ((bf16[16,20,128]{2,1,0:T(8,128)(2,1)}), bf16[16,20,128]{2,1,0:T(8,128)(2,1)S(1)}, u32[]{:S(2)}, u32[]{:S(2)}) async-start(bf16[16,20,128]{2,1,0:T(8,128)(2,1)} %reshape.44), calls=%async_computation.2 | async-start | bytes 196608 | tf_op jit(solution)/shard_map/all_to_all | solution.py:70
  613.9 3.6 copy-start.1
Sparse Core Ops, SparseCore 0:
  10.1 70.1 all-gather.4
  104.9 156.2 all-gather.2
  438.2 161.9 reduce-scatter.3
where the time goes:
time: 636 us; the launch traced here: 635 us
  waiting for transfers between devices  530 us (83%)
  starting transfers between devices  43.1 us (7%)
  local copies, waits for them, and re-layouts  23.7 us (4%)
  matrix products  21.2 us (3%)
  between operations  13.8 us (2%)
    unnamed x4, waiting for transfers between devices  164 us
    all_gather x1, waiting for transfers between devices, on_device(): lax.all_gather(out_grad, 'dp', axis=1, tiled=True)  158 us
    all_to_all x1, waiting for transfers between devices, on_device(): lax.all_to_all(send_dy, 'expert', split_axis=0, concat_axis=0, tiled=True)  131 us
    all_gather x1, waiting for transfers between devices, on_device(): lax.all_gather(tokens, 'dp', axis=1, tiled=True)  69.1 us
    all_to_all x1, starting transfers between devices, on_device(): lax.all_to_all(send_dy, 'expert', split_axis=0, concat_axis=0, tiled=True)  17.1 us
    all_to_all x1, starting transfers between devices, on_device(): lax.all_to_all(send_in, 'expert', split_axis=0, concat_axis=0, tiled=True)  13.9 us
  transfers between devices with their start and end apart: 6, of which 5 were waited for; matrix products, arithmetic and copies ran while one was open for 4% of the time, Pallas kernels for 0%

commit v1 on v0

v1 whole, which is shorter than its diff:
```python
import jax
import jax.numpy as jnp
from jax import lax
from jax.experimental import pallas as pl
from jax.experimental.pallas import tpu as pltpu
from jax.sharding import Mesh, PartitionSpec as P

NY, NZ, NC, NH, NX = 4, 4, 2, 4, 4
EXPERTS = NH * NX
TOK = 128
CAP = 20
MSG = 2 * CAP
COLS = 128
HID = 128
ROWS = EXPERTS * MSG
KEPT = EXPERTS * CAP
BF16 = jnp.bfloat16
F32 = jnp.float32
VMEM = pltpu.CompilerParams(vmem_limit_bytes=56 * 1024 * 1024)
CONTRACT_LAST = (((1,), (1,)), ((), ()))
CONTRACT_FIRST = (((0,), (0,)), ((), ()))


def slot_table(ids, rows_each, slot_of):
    experts = lax.broadcasted_iota(jnp.int32, (EXPERTS, TOK), 0)
    named = (experts == ids[0:1, :]) | (experts == ids[1:2, :])
    earlier = lax.broadcasted_iota(jnp.int32, (TOK, TOK), 0) < lax.broadcasted_iota(jnp.int32, (TOK, TOK), 1)
    prior = jnp.dot(named.astype(BF16), earlier.astype(BF16), preferred_element_type=F32)
    place = jnp.where(named, prior, -1.0).astype(BF16)
    shape = (EXPERTS, rows_each, TOK)
    expert = lax.broadcasted_iota(jnp.int32, shape, 0).reshape(EXPERTS * rows_each, TOK)
    row = lax.broadcasted_iota(jnp.int32, shape, 1).reshape(EXPERTS * rows_each, TOK)
    spread = (expert[:, :EXPERTS] == lax.broadcasted_iota(jnp.int32, (EXPERTS * rows_each, EXPERTS), 1)).astype(BF16)
    place_of_row = jnp.dot(spread, place, preferred_element_type=F32)
    return place_of_row == slot_of(row).astype(F32), expert, row


def dispatch_kernel(ids_ref, gate_ref, tok_ref, dy_ref, out_ref):
    ids = ids_ref[...]
    table, expert, row = slot_table(ids, MSG, lambda q: jnp.where(q >= CAP, q - CAP, q))
    gate = jnp.where(expert == ids[0:1, :], gate_ref[0:1, :], gate_ref[1:2, :])
    scale = jnp.sum(jnp.where(table, gate, 0.0), axis=1, keepdims=True)
    pick = table.astype(BF16)
    rows_in = jnp.dot(pick, tok_ref[...], preferred_element_type=F32)
    rows_dy = jnp.dot(pick, dy_ref[...], preferred_element_type=F32)
    out = jnp.where(row < CAP, rows_in, scale * rows_dy)
    out_ref[...] = out.astype(BF16).reshape(EXPERTS, MSG, COLS)


def forward_kernel(pos_ref, w_in_ref, w_out_ref, *refs):
    xs, (pgact_t_ref, pg_ref) = refs[:-2], refs[-2:]
    pre = jnp.zeros((ROWS, HID), F32)
    act_grad = jnp.zeros((ROWS, HID), F32)
    for own, sib, mine, other in pairs(pos_ref, xs):
        x = jnp.concatenate([own(), sib()], axis=1)
        w = jnp.concatenate([w_in_ref[pl.ds(mine, COLS), :], w_in_ref[pl.ds(other, COLS), :]], axis=0)
        v = jnp.concatenate([w_out_ref[:, pl.ds(mine, COLS)], w_out_ref[:, pl.ds(other, COLS)]], axis=1)
        pre = pre + jnp.dot(x, w, preferred_element_type=F32)
        act_grad = act_grad + lax.dot_general(x, v, CONTRACT_LAST, preferred_element_type=F32)
    act_grad = jnp.concatenate([act_grad[CAP:], act_grad[:CAP]], axis=0)
    act, pullback = jax.vjp(lambda v: jax.nn.gelu(v, approximate=True), pre)
    pre_grad = pullback(act_grad)[0]
    act = jnp.concatenate([act[ROWS - CAP:], act[:ROWS - CAP]], axis=0)
    row = lax.broadcasted_iota(jnp.int32, (EXPERTS, MSG, HID), 1).reshape(ROWS, HID)
    pre_grad = jnp.where(row < CAP, pre_grad, 0.0).astype(BF16)
    act = jnp.where(row < CAP, 0.0, act).astype(BF16)
    pgact_t_ref[...] = jnp.concatenate([pre_grad, act], axis=1).T
    block = lax.broadcasted_iota(jnp.int32, (EXPERTS, CAP, ROWS), 0).reshape(KEPT, ROWS)
    within = lax.broadcasted_iota(jnp.int32, (EXPERTS, CAP, ROWS), 1).reshape(KEPT, ROWS)
    keep = (lax.broadcasted_iota(jnp.int32, (KEPT, ROWS), 1) == block * MSG + within).astype(BF16)
    pg_ref[...] = jnp.dot(keep, pre_grad, preferred_element_type=F32).astype(BF16)


def pairs(pos_ref, xs):
    half = len(xs) // 2
    y, c = pos_ref[0], pos_ref[1]
    steps = (0, NY - 1, 1, 2)
    for i, step in enumerate(steps):
        at = lax.rem(y + step, NY)
        for zl in range(NZ):
            if i < 3:
                own, sib, k = xs[i], xs[half + i], zl
            else:
                own, sib, k = xs[3 + zl // 2], xs[half + 3 + zl // 2], zl % 2
            first = (at * NZ + zl) * NC
            mine = pl.multiple_of((first + c) * COLS, COLS)
            other = pl.multiple_of((first + 1 - c) * COLS, COLS)

            def reader(ref, k=k):
                return lambda: ref[k * EXPERTS:(k + 1) * EXPERTS].reshape(ROWS, COLS)

            yield reader(own), reader(sib), mine, other


def partial_kernel(pos_ref, w_in_ref, pg_ref, far_ref, near_ref):
    y, c = pos_ref[0], pos_ref[1]
    pg = pg_ref[...]
    for place, step in enumerate((2, 0, 1, 3)):
        at = lax.rem(y + step, NY)
        for zl in range(NZ):
            first = (at * NZ + zl) * NC
            mine = pl.multiple_of((first + c) * COLS, COLS)
            other = pl.multiple_of((first + 1 - c) * COLS, COLS)
            w = jnp.concatenate([w_in_ref[pl.ds(mine, COLS), :], w_in_ref[pl.ds(other, COLS), :]], axis=0)
            out = lax.dot_general(pg, w, CONTRACT_LAST, preferred_element_type=F32).astype(BF16)
            for core in range(NC):
                block = out[:, core * COLS:(core + 1) * COLS]
                if place == 0:
                    far_ref[core, zl] = block
                else:
                    near_ref[core, place - 1, zl] = block


def grads_kernel(pos_ref, pgact_t_ref, *refs):
    xs, (w_in_grad_ref, w_out_grad_ref) = refs[:-2], refs[-2:]
    left = pgact_t_ref[...]
    for own, sib, mine, other in pairs(pos_ref, xs):
        x = jnp.concatenate([own(), sib()], axis=1)
        both = jnp.dot(left, x, preferred_element_type=F32)
        grad_in = both[:HID].T.astype(BF16)
        grad_out = both[HID:].astype(BF16)
        w_in_grad_ref[pl.ds(mine, COLS), :] = grad_in[:COLS]
        w_in_grad_ref[pl.ds(other, COLS), :] = grad_in[COLS:]
        w_out_grad_ref[:, pl.ds(mine, COLS)] = grad_out[:, :COLS]
        w_out_grad_ref[:, pl.ds(other, COLS)] = grad_out[:, COLS:]


def combine_kernel(ids_ref, back_ref, out_ref):
    table, _, _ = slot_table(ids_ref[...], CAP, lambda q: q)
    total = back_ref[0:EXPERTS].astype(F32)
    for z in range(1, NZ):
        total = total + back_ref[z * EXPERTS:(z + 1) * EXPERTS].astype(F32)
    rows = total.reshape(KEPT, COLS).astype(BF16)
    out_ref[...] = lax.dot_general(
        table.astype(BF16), rows, CONTRACT_FIRST, preferred_element_type=F32
    ).astype(BF16)


def shape(*dims, kind=BF16):
    return jax.ShapeDtypeStruct(dims, kind)


SMEM = pl.BlockSpec(memory_space=pltpu.SMEM)
WHOLE = pl.BlockSpec(memory_space=pltpu.VMEM)


def run(kernel, outs, scalars, *args):
    specs = [SMEM] * scalars + [WHOLE] * (len(args) - scalars)
    out_specs = jax.tree.map(lambda _: WHOLE, outs)
    return pl.pallas_call(kernel, out_shape=outs, in_specs=specs, out_specs=out_specs, compiler_params=VMEM)(*args)


def ring(value, step):
    return lax.ppermute(value, "y", [(i, (i + step) % NY) for i in range(NY)])


def across(value):
    return lax.ppermute(value, "c", [(0, 1), (1, 0)])


def add(*parts):
    total = parts[0].astype(F32)
    for part in parts[1:]:
        total = total + part.astype(F32)
    return total.astype(BF16)


def on_device(tokens, out_grad, expert_ids, gate_weights, w_in, w_out):
    pos = jnp.stack([lax.axis_index("y"), lax.axis_index("c")]).astype(jnp.int32)
    ids, gate = expert_ids.T, gate_weights.T
    send = run(dispatch_kernel, shape(EXPERTS, MSG, COLS), 0, ids, gate, tokens, out_grad)
    received = lax.all_to_all(send, ("zh", "x"), 0, 0, tiled=True)
    own = lax.all_gather(received, "zl", axis=0, tiled=True)
    prev, after = ring(own, 1), ring(own, -1)
    cut = NZ // 2 * EXPERTS
    far_a, far_b = ring(prev[:cut], 1), ring(after[cut:], -1)
    mine = [own, prev, after, far_a, far_b]
    xs = mine + [across(x) for x in mine]
    w_in, w_out = w_in[0], w_out[0]
    pgact_t, pg = run(
        forward_kernel, (shape(2 * HID, ROWS), shape(KEPT, HID)), 1, pos, w_in, w_out, *xs
    )
    far, near = run(
        partial_kernel,
        (shape(NC, NZ, KEPT, COLS), shape(NC, NY - 1, NZ, KEPT, COLS)),
        1, pos, w_in, pg,
    )
    far = add(far[0], across(far[1]))
    near = add(near[0], across(near[1]))
    half = NZ // 2
    from_prev, from_after = ring(far[:half], 1), ring(far[half:], -1)
    up = jnp.concatenate([add(near[1, :half], from_prev), near[1, half:]])
    down = jnp.concatenate([near[2, :half], add(near[2, half:], from_after)])
    summed = add(near[0], ring(up, 1), ring(down, -1))
    back = lax.all_to_all(summed.reshape(NZ * EXPERTS, CAP, COLS), ("zl", "zh", "x"), 0, 0, tiled=True)
    tokens_grad = run(combine_kernel, shape(TOK, COLS), 0, ids, back)
    w_in_grad, w_out_grad = run(
        grads_kernel, (shape(*w_in.shape), shape(*w_out.shape)), 1, pos, pgact_t, *xs
    )
    return tokens_grad, w_in_grad[None], w_out_grad[None]


def solution(mesh):
    fine = Mesh(mesh.devices.reshape(NY, NZ, NC, NH, NX), ("y", "zl", "c", "zh", "x"))
    dp, expert = ("y", "zl", "c"), ("zh", "x")
    placed = (
        P(expert, dp),
        P(expert, dp),
        P(expert, None),
        P(expert, None),
        P(expert, None, dp),
        P(expert, dp, None),
    )
    return jax.shard_map(
        on_device,
        mesh=fine,
        in_specs=placed,
        out_specs=(P(expert, dp), P(expert, None, dp), P(expert, dp, None)),
        check_vma=False,
    )
```

time: 636 us -> 173 us (0.27)
  the two profiles are of different devices: /device:TPU:2 before, /device:TPU:32 now
where the time goes in v1:
time: 173 us; the launch traced here: 172 us
  starting transfers between devices  51.4 us (30%)
  blocking collectives  51 us (29%)
  waiting for transfers between devices  43.8 us (25%)
  Pallas kernels  20.2 us (12%)
  local copies, waits for them, and re-layouts  3.15 us (2%)
    all_to_all x1, blocking collectives, on_device(): received = lax.all_to_all(send, ('zh', 'x'), 0, 0, tiled=True)  36 us
    ppermute x8, starting transfers between devices, ring(): return lax.ppermute(value, 'y', [(i, (i + step) % NY) for i in range(NY)])  28.9 us
    ppermute x8, waiting for transfers between devices, ring(): return lax.ppermute(value, 'y', [(i, (i + step) % NY) for i in range(NY)])  20.7 us
    all_to_all x1, waiting for transfers between devices, on_device(): lax.all_to_all(summed.reshape(NZ * EXPERTS, CAP, COLS), ('zl', 'zh', 'x')...  20.5 us
    pallas_call x5, Pallas kernels, run(): pl.pallas_call(kernel, out_shape=outs, in_specs=specs, out_specs=out_spec...  20.2 us
    all_gather x1, blocking collectives, on_device(): own = lax.all_gather(received, 'zl', axis=0, tiled=True)  15.1 us
    ppermute x7, starting transfers between devices, across(): return lax.ppermute(value, 'c', [(0, 1), (1, 0)])  14.4 us
    all_to_all x1, starting transfers between devices, on_device(): lax.all_to_all(summed.reshape(NZ * EXPERTS, CAP, COLS), ('zl', 'zh', 'x')...  8.08 us
  transfers between devices with their start and end apart: 16, of which 9 were waited for; matrix products, arithmetic and copies ran while one was open for 1% of the time, Pallas kernels for 3%

profile of v1, /device:TPU:32, one launch (start us, length us, event | category | flops | bytes accessed | tf_op | source)
XLA Modules:
  0.0 171.9 jit_solution(12137093524377118544)
XLA Ops:
  0.6 2.0 %shard_map.85 = bf16[16,40,128]{2,1,0:T(8,128)(2,1)} custom-call(s32[2,128]{1,0:T(2,128)} %bitcast.40, f32[2,128]{1,0:T(2,128)} %bitcast.42, bf16[128,128]{1,0:T(8,128)(2,1)} %tok_ref.1, bf16[128,128]{1,0:T(8,128)(2,1)} %dy_ref.1), custom_call_target="tpu_custom_call" | custom-call | tf_op jit(solution)/shard_map/pallas_call | solution.py:150
  2.6 36.0 %all_to_all.10 = bf16[16,40,128]{2,1,0:T(8,128)(2,1)S(1)} all-to-all(bf16[16,40,128]{2,1,0:T(8,128)(2,1)} %shard_map.85), channel_id=1, replica_groups=mesh['y'=4,'zl'=4,'c'=2,'zh'=4,'x'=4] {'zh','x'}, dimensions={0} | all-to-all | bytes 327680 | tf_op jit(solution)/shard_map/all_to_all | solution.py:172
  38.6 15.1 %all_gather.3.refs_0_ = bf16[64,40,128]{2,1,0:T(8,128)(2,1)S(1)} all-gather(bf16[16,40,128]{2,1,0:T(8,128)(2,1)S(1)} %all_to_all.10), channel_id=1, replica_groups=mesh['y'=4,'zl'=4,'c'=2,'zh'=4,'x'=4] {'zl'}, dimensions={0}, use_global_device_ids=true | all-gather | bytes 819200 | tf_op jit(solution)/shard_map/all_gather | solution.py:173
  53.6 4.9 %collective-permute-start.1 = (bf16[64,40,128]{2,1,0:T(8,128)(2,1)S(1)}, bf16[64,40,128]{2,1,0:T(8,128)(2,1)S(1)}, u32[]{:S(2)}, u32[]{:S(2)}) collective-permute-start(bf16[64,40,128]{2,1,0:T(8,128)(2,1)S(1)} %all_gather.3.refs_0_), channel_id=1, source_target_pairs={{0,384},{128,0},{256,128},{384,256},{1,385},{129,1},{257,129},{385... | collective-permute-start | bytes 1966088 | tf_op jit(solution)/shard_map/ppermute | solution.py:154
  58.6 1.9 %collective-permute-start = (bf16[64,40,128]{2,1,0:T(8,128)(2,1)S(1)}, bf16[64,40,128]{2,1,0:T(8,128)(2,1)S(1)}, u32[]{:S(2)}, u32[]{:S(2)}) collective-permute-start(bf16[64,40,128]{2,1,0:T(8,128)(2,1)S(1)} %all_gather.3.refs_0_), channel_id=1, source_target_pairs={{0,128},{128,256},{256,384},{384,0},{1,129},{129,257},{257,385},{3... | collective-permute-start | bytes 1966088 | tf_op jit(solution)/shard_map/ppermute | solution.py:154
  60.5 1.9 %collective-permute-start.4 = (bf16[64,40,128]{2,1,0:T(8,128)(2,1)S(1)}, bf16[64,40,128]{2,1,0:T(8,128)(2,1)S(1)}, u32[]{:S(2)}, u32[]{:S(2)}) collective-permute-start(bf16[64,40,128]{2,1,0:T(8,128)(2,1)S(1)} %all_gather.3.refs_0_), channel_id=1, source_target_pairs={{0,16},{16,0},{1,17},{17,1},{2,18},{18,2},{3,19},{19,3},{4,20},{20... | collective-permute-start | bytes 1966088 | tf_op jit(solution)/shard_map/ppermute | solution.py:158
  62.4 5.7 %collective-permute-done.1.refs_2_ = bf16[64,40,128]{2,1,0:T(8,128)(2,1)S(1)} collective-permute-done((bf16[64,40,128]{2,1,0:T(8,128)(2,1)S(1)}, bf16[64,40,128]{2,1,0:T(8,128)(2,1)S(1)}, u32[]{:S(2)}, u32[]{:S(2)}) %collective-permute-start.1) | collective-permute-done | bytes 655392 | tf_op jit(solution)/shard_map/ppermute | solution.py:154
  68.2 5.6 %collective-permute-start.3 = (bf16[32,40,128]{2,1,0:T(8,128)(2,1)S(1)}, bf16[32,40,128]{2,1,0:T(8,128)(2,1)}, u32[]{:S(2)}, u32[]{:S(2)}) collective-permute-start(bf16[32,40,128]{2,1,0:T(8,128)(2,1)S(1)} %slice.53), channel_id=1, source_target_pairs={{0,384},{128,0},{256,128},{384,256},{1,385},{129,1},{257,129},{385... | collective-permute-start | bytes 983048 | tf_op jit(solution)/shard_map/ppermute | solution.py:154
  73.8 0.0 collective-permute-done.refs_1_
  73.8 0.0 copy-start.2
  73.9 1.9 %collective-permute-start.2 = (bf16[32,40,128]{2,1,0:T(8,128)(2,1)S(1)}, bf16[32,40,128]{2,1,0:T(8,128)(2,1)}, u32[]{:S(2)}, u32[]{:S(2)}) collective-permute-start(bf16[32,40,128]{2,1,0:T(8,128)(2,1)S(1)} %slice.52), channel_id=1, source_target_pairs={{0,128},{128,256},{256,384},{384,0},{1,129},{129,257},{257,385},{3... | collective-permute-start | bytes 983048 | tf_op jit(solution)/shard_map/ppermute | solution.py:154
  75.8 1.9 %collective-permute-start.6 = (bf16[64,40,128]{2,1,0:T(8,128)(2,1)S(1)}, bf16[64,40,128]{2,1,0:T(8,128)(2,1)S(1)}, u32[]{:S(2)}, u32[]{:S(2)}) collective-permute-start(bf16[64,40,128]{2,1,0:T(8,128)(2,1)S(1)} %collective-permute-done.1.refs_2_), channel_id=1, source_target_pairs={{0,16},{16,0},{1,17},{17,1},{2,18},{18,2},{3,19},{19,3},{4,20},{20... | collective-permute-start | bytes 1966088 | tf_op jit(solution)/shard_map/ppermute | solution.py:158
  77.7 2.4 %collective-permute-start.5 = (bf16[64,40,128]{2,1,0:T(8,128)(2,1)S(1)}, bf16[64,40,128]{2,1,0:T(8,128)(2,1)}, u32[]{:S(2)}, u32[]{:S(2)}) collective-permute-start(bf16[64,40,128]{2,1,0:T(8,128)(2,1)S(1)} %collective-permute-done.refs_1_), channel_id=1, source_target_pairs={{0,16},{16,0},{1,17},{17,1},{2,18},{18,2},{3,19},{19,3},{4,20},{20... | collective-permute-start | bytes 1966088 | tf_op jit(solution)/shard_map/ppermute | solution.py:158
  80.1 0.0 collective-permute-done.3.refs_4_
  80.1 1.9 %collective-permute-start.8 = (bf16[32,40,128]{2,1,0:T(8,128)(2,1)}, bf16[32,40,128]{2,1,0:T(8,128)(2,1)}, u32[]{:S(2)}, u32[]{:S(2)}) collective-permute-start(bf16[32,40,128]{2,1,0:T(8,128)(2,1)} %collective-permute-done.3.refs_4_), channel_id=1, source_target_pairs={{0,16},{16,0},{1,17},{17,1},{2,18},{18,2},{3,19},{19,3},{4,20},{20... | collective-permute-start | bytes 983048 | tf_op jit(solution)/shard_map/ppermute | solution.py:158
  82.1 2.1 %collective-permute-done.2.refs_3_ = bf16[32,40,128]{2,1,0:T(8,128)(2,1)} collective-permute-done((bf16[32,40,128]{2,1,0:T(8,128)(2,1)S(1)}, bf16[32,40,128]{2,1,0:T(8,128)(2,1)}, u32[]{:S(2)}, u32[]{:S(2)}) %collective-permute-start.2) | collective-permute-done | bytes 327712 | tf_op jit(solution)/shard_map/ppermute | solution.py:154
  84.1 1.9 %collective-permute-start.7 = (bf16[32,40,128]{2,1,0:T(8,128)(2,1)}, bf16[32,40,128]{2,1,0:T(8,128)(2,1)}, u32[]{:S(2)}, u32[]{:S(2)}) collective-permute-start(bf16[32,40,128]{2,1,0:T(8,128)(2,1)} %collective-permute-done.2.refs_3_), channel_id=1, source_target_pairs={{0,16},{16,0},{1,17},{17,1},{2,18},{18,2},{3,19},{19,3},{4,20},{20... | collective-permute-start | bytes 983048 | tf_op jit(solution)/shard_map/ppermute | solution.py:158
  86.1 0.7 pad_add_fusion.pos_ref
  86.7 0.0 collective-permute-done.4.refs_5_
  86.7 0.0 collective-permute-done.8.refs_9_
  86.7 0.0 collective-permute-done.6.refs_7_
  86.7 1.2 collective-permute-done.7.refs_8_
  88.0 0.0 collective-permute-done.5.refs_6_
  88.0 7.0 %shard_map.86 = (bf16[256,640]{1,0:T(8,128)(2,1)}, bf16[320,128]{1,0:T(8,128)(2,1)}) custom-call(s32[2]{0:T(128)} %pad_add_fusion.pos_ref, bf16[4096,128]{1,0:T(8,128)(2,1)} %bitcast.37, bf16[128,4096]{1,0:T(8,128)(2,1)} %bitcast.39, bf16[64,40,128]{2,1,0:T(8,128)(2,1)} %copy-done, bf16[64,40,128]{2,1,0:T(8,128)(2,1)} %copy-done.2, ...), custom_call_target="tpu_custom_call" | custom-call | tf_op jit(solution)/shard_map/pallas_call | solution.py:150
  95.0 3.4 %shard_map.87 = (bf16[2,4,320,128]{3,2,1,0:T(8,128)(2,1)}, bf16[2,3,4,320,128]{4,3,2,1,0:T(8,128)(2,1)}) custom-call(s32[2]{0:T(128)} %pad_add_fusion.pos_ref, bf16[4096,128]{1,0:T(8,128)(2,1)} %bitcast.38, bf16[320,128]{1,0:T(8,128)(2,1)} %get-tuple-element.9.pg_ref), custom_call_target="tpu_custom_call" | custom-call | tf_op jit(solution)/shard_map/pallas_call | solution.py:150
  98.4 1.4 slice_bitcast_fusion
  99.8 2.2 %collective-permute-start.9 = (bf16[3,4,320,128]{3,2,1,0:T(8,128)(2,1)S(1)}, bf16[3,4,320,128]{3,2,1,0:T(8,128)(2,1)S(1)}, u32[]{:S(2)}, u32[]{:S(2)}) collective-permute-start(bf16[3,4,320,128]{3,2,1,0:T(8,128)(2,1)S(1)} %slice_bitcast_fusion), channel_id=1, source_target_pairs={{0,16},{16,0},{1,17},{17,1},{2,18},{18,2},{3,19},{19,3},{4,20},{20... | collective-permute-start | bytes 2949128 | tf_op jit(solution)/shard_map/ppermute | solution.py:158
  102.0 2.2 %collective-permute-start.10 = (bf16[4,320,128]{2,1,0:T(8,128)(2,1)S(1)}, bf16[4,320,128]{2,1,0:T(8,128)(2,1)S(1)}, u32[]{:S(2)}, u32[]{:S(2)}) collective-permute-start(bf16[4,320,128]{2,1,0:T(8,128)(2,1)S(1)} %slice_bitcast_fusion.2), channel_id=1, source_target_pairs={{0,16},{16,0},{1,17},{17,1},{2,18},{18,2},{3,19},{19,3},{4,20},{20... | collective-permute-start | bytes 983048 | tf_op jit(solution)/shard_map/ppermute | solution.py:158
  104.2 1.3 collective-permute-done.10
  105.5 0.1 fusion.1
  105.6 1.9 %collective-permute-start.11 = (bf16[2,320,128]{2,1,0:T(8,128)(2,1)S(1)}, bf16[2,320,128]{2,1,0:T(8,128)(2,1)S(1)}, u32[]{:S(2)}, u32[]{:S(2)}) collective-permute-start(bf16[2,320,128]{2,1,0:T(8,128)(2,1)S(1)} %get-tuple-element.19), channel_id=1, source_target_pairs={{0,128},{128,256},{256,384},{384,0},{1,129},{129,257},{257,385},{3... | collective-permute-start | bytes 491528 | tf_op jit(solution)/shard_map/ppermute | solution.py:154
  107.6 5.1 %collective-permute-start.13 = (bf16[2,320,128]{2,1,0:T(8,128)(2,1)S(1)}, bf16[2,320,128]{2,1,0:T(8,128)(2,1)S(1)}, u32[]{:S(2)}, u32[]{:S(2)}) collective-permute-start(bf16[2,320,128]{2,1,0:T(8,128)(2,1)S(1)} %get-tuple-element.20), channel_id=1, source_target_pairs={{0,384},{128,0},{256,128},{384,256},{1,385},{129,1},{257,129},{385... | collective-permute-start | bytes 491528 | tf_op jit(solution)/shard_map/ppermute | solution.py:154
  112.7 0.0 collective-permute-done.9
  112.7 0.3 fusion
  113.0 2.1 %collective-permute-done.11 = bf16[2,320,128]{2,1,0:T(8,128)(2,1)S(1)} collective-permute-done((bf16[2,320,128]{2,1,0:T(8,128)(2,1)S(1)}, bf16[2,320,128]{2,1,0:T(8,128)(2,1)S(1)}, u32[]{:S(2)}, u32[]{:S(2)}) %collective-permute-start.11) | collective-permute-done | bytes 163872 | tf_op jit(solution)/shard_map/ppermute | solution.py:154
  115.1 1.2 collective-permute-done.13
  116.3 0.1 fusion.5
  116.4 5.6 %collective-permute-start.14 = (bf16[4,320,128]{2,1,0:T(8,128)(2,1)S(1)}, bf16[4,320,128]{2,1,0:T(8,128)(2,1)S(1)}, u32[]{:S(2)}, u32[]{:S(2)}) collective-permute-start(bf16[4,320,128]{2,1,0:T(8,128)(2,1)S(1)} %pad_maximum_fusion.1), channel_id=1, source_target_pairs={{0,384},{128,0},{256,128},{384,256},{1,385},{129,1},{257,129},{385... | collective-permute-start | bytes 983048 | tf_op jit(solution)/shard_map/ppermute | solution.py:154
  122.1 1.9 %collective-permute-start.12 = (bf16[4,320,128]{2,1,0:T(8,128)(2,1)S(1)}, bf16[4,320,128]{2,1,0:T(8,128)(2,1)S(1)}, u32[]{:S(2)}, u32[]{:S(2)}) collective-permute-start(bf16[4,320,128]{2,1,0:T(8,128)(2,1)S(1)} %pad_maximum_fusion), channel_id=1, source_target_pairs={{0,128},{128,256},{256,384},{384,0},{1,129},{129,257},{257,385},{3... | collective-permute-start | bytes 983048 | tf_op jit(solution)/shard_map/ppermute | solution.py:154
  124.0 4.3 %collective-permute-done.14 = bf16[4,320,128]{2,1,0:T(8,128)(2,1)S(1)} collective-permute-done((bf16[4,320,128]{2,1,0:T(8,128)(2,1)S(1)}, bf16[4,320,128]{2,1,0:T(8,128)(2,1)S(1)}, u32[]{:S(2)}, u32[]{:S(2)}) %collective-permute-start.14) | collective-permute-done | bytes 327712 | tf_op jit(solution)/shard_map/ppermute | solution.py:154
  128.3 5.4 %collective-permute-done.12 = bf16[4,320,128]{2,1,0:T(8,128)(2,1)S(1)} collective-permute-done((bf16[4,320,128]{2,1,0:T(8,128)(2,1)S(1)}, bf16[4,320,128]{2,1,0:T(8,128)(2,1)S(1)}, u32[]{:S(2)}, u32[]{:S(2)}) %collective-permute-start.12) | collective-permute-done | bytes 327712 | tf_op jit(solution)/shard_map/ppermute | solution.py:154
  133.7 0.1 fusion.3
  133.8 0.8 reshape.19
  134.6 8.1 %all-to-all-start.1 = ((bf16[64,20,128]{2,1,0:T(8,128)(2,1)}), bf16[64,20,128]{2,1,0:T(8,128)(2,1)S(1)}, u32[]{:S(2)}, u32[]{:S(2)}) async-start(bf16[64,20,128]{2,1,0:T(8,128)(2,1)} %reshape.19), calls=%async_computation.1 | async-start | bytes 786432 | tf_op jit(solution)/shard_map/all_to_all | solution.py:195
  142.7 5.8 %shard_map.89 = (bf16[4096,128]{1,0:T(8,128)(2,1)}, bf16[128,4096]{1,0:T(8,128)(2,1)}) custom-call(s32[2]{0:T(128)} %pad_add_fusion.pos_ref, bf16[256,640]{1,0:T(8,128)(2,1)} %get-tuple-element.12.pgact_t_ref, bf16[64,40,128]{2,1,0:T(8,128)(2,1)} %copy-done, bf16[64,40,128]{2,1,0:T(8,128)(2,1)} %copy-done.2, bf16[64,40,128]{2,1,0:T(8,128)(2,1)} %copy-done.1, ...), custom_call_target="tpu_custom_call" | custom-call | tf_op jit(solution)/shard_map/pallas_call | solution.py:150
  148.5 20.5 %all-to-all-done.1.back_ref = bf16[64,20,128]{2,1,0:T(8,128)(2,1)S(1)} async-done(((bf16[64,20,128]{2,1,0:T(8,128)(2,1)}), bf16[64,20,128]{2,1,0:T(8,128)(2,1)S(1)}, u32[]{:S(2)}, u32[]{:S(2)}) %all-to-all-start.1) | async-done | bytes 327712 | tf_op jit(solution)/shard_map/all_to_all | solution.py:195
  169.0 0.8 copy-done.6
  169.8 2.1 %shard_map.88 = bf16[128,128]{1,0:T(8,128)(2,1)} custom-call(s32[2,128]{1,0:T(2,128)} %bitcast.41, bf16[64,20,128]{2,1,0:T(8,128)(2,1)} %copy-done.6), custom_call_target="tpu_custom_call" | custom-call | tf_op jit(solution)/shard_map/pallas_call | solution.py:150
  (21 shorter events, 0.2 us)
Async XLA Ops:
  53.6 34.4 %copy-start = (bf16[64,40,128]{2,1,0:T(8,128)(2,1)}, bf16[64,40,128]{2,1,0:T(8,128)(2,1)S(1)}, u32[]{:S(2)}) copy-start(bf16[64,40,128]{2,1,0:T(8,128)(2,1)S(1)} %all_gather.3.refs_0_) | copy-start | bytes 1966084
  53.6 14.5 %collective-permute-start.1 = (bf16[64,40,128]{2,1,0:T(8,128)(2,1)S(1)}, bf16[64,40,128]{2,1,0:T(8,128)(2,1)S(1)}, u32[]{:S(2)}, u32[]{:S(2)}) collective-permute-start(bf16[64,40,128]{2,1,0:T(8,128)(2,1)S(1)} %all_gather.3.refs_0_), channel_id=1, source_target_pairs={{0,384},{128,0},{256,128},{384,256},{1,385},{129,1},{257,129},{385... | collective-permute-start | bytes 1966088 | tf_op jit(solution)/shard_map/ppermute | solution.py:154
  58.6 15.2 %collective-permute-start = (bf16[64,40,128]{2,1,0:T(8,128)(2,1)S(1)}, bf16[64,40,128]{2,1,0:T(8,128)(2,1)S(1)}, u32[]{:S(2)}, u32[]{:S(2)}) collective-permute-start(bf16[64,40,128]{2,1,0:T(8,128)(2,1)S(1)} %all_gather.3.refs_0_), channel_id=1, source_target_pairs={{0,128},{128,256},{256,384},{384,0},{1,129},{129,257},{257,385},{3... | collective-permute-start | bytes 1966088 | tf_op jit(solution)/shard_map/ppermute | solution.py:154
  60.5 26.2 %collective-permute-start.4 = (bf16[64,40,128]{2,1,0:T(8,128)(2,1)S(1)}, bf16[64,40,128]{2,1,0:T(8,128)(2,1)S(1)}, u32[]{:S(2)}, u32[]{:S(2)}) collective-permute-start(bf16[64,40,128]{2,1,0:T(8,128)(2,1)S(1)} %all_gather.3.refs_0_), channel_id=1, source_target_pairs={{0,16},{16,0},{1,17},{17,1},{2,18},{18,2},{3,19},{19,3},{4,20},{20... | collective-permute-start | bytes 1966088 | tf_op jit(solution)/shard_map/ppermute | solution.py:158
  68.1 19.9 %copy-start.1 = (bf16[64,40,128]{2,1,0:T(8,128)(2,1)}, bf16[64,40,128]{2,1,0:T(8,128)(2,1)S(1)}, u32[]{:S(2)}) copy-start(bf16[64,40,128]{2,1,0:T(8,128)(2,1)S(1)} %collective-permute-done.1.refs_2_) | copy-start | bytes 1966084
  68.2 11.9 %collective-permute-start.3 = (bf16[32,40,128]{2,1,0:T(8,128)(2,1)S(1)}, bf16[32,40,128]{2,1,0:T(8,128)(2,1)}, u32[]{:S(2)}, u32[]{:S(2)}) collective-permute-start(bf16[32,40,128]{2,1,0:T(8,128)(2,1)S(1)} %slice.53), channel_id=1, source_target_pairs={{0,384},{128,0},{256,128},{384,256},{1,385},{129,1},{257,129},{385... | collective-permute-start | bytes 983048 | tf_op jit(solution)/shard_map/ppermute | solution.py:154
  73.8 14.2 %copy-start.2 = (bf16[64,40,128]{2,1,0:T(8,128)(2,1)}, bf16[64,40,128]{2,1,0:T(8,128)(2,1)S(1)}, u32[]{:S(2)}) copy-start(bf16[64,40,128]{2,1,0:T(8,128)(2,1)S(1)} %collective-permute-done.refs_1_) | copy-start | bytes 1966084
  73.9 10.3 %collective-permute-start.2 = (bf16[32,40,128]{2,1,0:T(8,128)(2,1)S(1)}, bf16[32,40,128]{2,1,0:T(8,128)(2,1)}, u32[]{:S(2)}, u32[]{:S(2)}) collective-permute-start(bf16[32,40,128]{2,1,0:T(8,128)(2,1)S(1)} %slice.52), channel_id=1, source_target_pairs={{0,128},{128,256},{256,384},{384,0},{1,129},{129,257},{257,385},{3... | collective-permute-start | bytes 983048 | tf_op jit(solution)/shard_map/ppermute | solution.py:154
  75.8 10.9 %collective-permute-start.6 = (bf16[64,40,128]{2,1,0:T(8,128)(2,1)S(1)}, bf16[64,40,128]{2,1,0:T(8,128)(2,1)S(1)}, u32[]{:S(2)}, u32[]{:S(2)}) collective-permute-start(bf16[64,40,128]{2,1,0:T(8,128)(2,1)S(1)} %collective-permute-done.1.refs_2_), channel_id=1, source_target_pairs={{0,16},{16,0},{1,17},{17,1},{2,18},{18,2},{3,19},{19,3},{4,20},{20... | collective-permute-start | bytes 1966088 | tf_op jit(solution)/shard_map/ppermute | solution.py:158
  77.7 10.3 %collective-permute-start.5 = (bf16[64,40,128]{2,1,0:T(8,128)(2,1)S(1)}, bf16[64,40,128]{2,1,0:T(8,128)(2,1)}, u32[]{:S(2)}, u32[]{:S(2)}) collective-permute-start(bf16[64,40,128]{2,1,0:T(8,128)(2,1)S(1)} %collective-permute-done.refs_1_), channel_id=1, source_target_pairs={{0,16},{16,0},{1,17},{17,1},{2,18},{18,2},{3,19},{19,3},{4,20},{20... | collective-permute-start | bytes 1966088 | tf_op jit(solution)/shard_map/ppermute | solution.py:158
  80.1 6.6 %collective-permute-start.8 = (bf16[32,40,128]{2,1,0:T(8,128)(2,1)}, bf16[32,40,128]{2,1,0:T(8,128)(2,1)}, u32[]{:S(2)}, u32[]{:S(2)}) collective-permute-start(bf16[32,40,128]{2,1,0:T(8,128)(2,1)} %collective-permute-done.3.refs_4_), channel_id=1, source_target_pairs={{0,16},{16,0},{1,17},{17,1},{2,18},{18,2},{3,19},{19,3},{4,20},{20... | collective-permute-start | bytes 983048 | tf_op jit(solution)/shard_map/ppermute | solution.py:158
  84.1 3.9 %collective-permute-start.7 = (bf16[32,40,128]{2,1,0:T(8,128)(2,1)}, bf16[32,40,128]{2,1,0:T(8,128)(2,1)}, u32[]{:S(2)}, u32[]{:S(2)}) collective-permute-start(bf16[32,40,128]{2,1,0:T(8,128)(2,1)} %collective-permute-done.2.refs_3_), channel_id=1, source_target_pairs={{0,16},{16,0},{1,17},{17,1},{2,18},{18,2},{3,19},{19,3},{4,20},{20... | collective-permute-start | bytes 983048 | tf_op jit(solution)/shard_map/ppermute | solution.py:158
  86.7 1.3 copy-start.3
  86.7 1.3 copy-start.4
  98.4 3.6 %copy-start.7 = (bf16[2,4,320,128]{3,2,1,0:T(8,128)(2,1)S(1)}, bf16[2,4,320,128]{3,2,1,0:T(8,128)(2,1)}, u32[]{:S(2)}) copy-start(bf16[2,4,320,128]{3,2,1,0:T(8,128)(2,1)} %get-tuple-element.11) | copy-start | bytes 1966084
  98.4 14.3 %copy-start.5 = (bf16[2,3,4,320,128]{4,3,2,1,0:T(8,128)(2,1)S(1)}, bf16[2,3,4,320,128]{4,3,2,1,0:T(8,128)(2,1)}, u32[]{:S(2)}) copy-start(bf16[2,3,4,320,128]{4,3,2,1,0:T(8,128)(2,1)} %get-tuple-element.10) | copy-start | bytes 5898244
  99.8 12.9 %collective-permute-start.9 = (bf16[3,4,320,128]{3,2,1,0:T(8,128)(2,1)S(1)}, bf16[3,4,320,128]{3,2,1,0:T(8,128)(2,1)S(1)}, u32[]{:S(2)}, u32[]{:S(2)}) collective-permute-start(bf16[3,4,320,128]{3,2,1,0:T(8,128)(2,1)S(1)} %slice_bitcast_fusion), channel_id=1, source_target_pairs={{0,16},{16,0},{1,17},{17,1},{2,18},{18,2},{3,19},{19,3},{4,20},{20... | collective-permute-start | bytes 2949128 | tf_op jit(solution)/shard_map/ppermute | solution.py:158
  102.0 3.5 %collective-permute-start.10 = (bf16[4,320,128]{2,1,0:T(8,128)(2,1)S(1)}, bf16[4,320,128]{2,1,0:T(8,128)(2,1)S(1)}, u32[]{:S(2)}, u32[]{:S(2)}) collective-permute-start(bf16[4,320,128]{2,1,0:T(8,128)(2,1)S(1)} %slice_bitcast_fusion.2), channel_id=1, source_target_pairs={{0,16},{16,0},{1,17},{17,1},{2,18},{18,2},{3,19},{19,3},{4,20},{20... | collective-permute-start | bytes 983048 | tf_op jit(solution)/shard_map/ppermute | solution.py:158
  105.6 9.5 %collective-permute-start.11 = (bf16[2,320,128]{2,1,0:T(8,128)(2,1)S(1)}, bf16[2,320,128]{2,1,0:T(8,128)(2,1)S(1)}, u32[]{:S(2)}, u32[]{:S(2)}) collective-permute-start(bf16[2,320,128]{2,1,0:T(8,128)(2,1)S(1)} %get-tuple-element.19), channel_id=1, source_target_pairs={{0,128},{128,256},{256,384},{384,0},{1,129},{129,257},{257,385},{3... | collective-permute-start | bytes 491528 | tf_op jit(solution)/shard_map/ppermute | solution.py:154
  107.6 8.7 %collective-permute-start.13 = (bf16[2,320,128]{2,1,0:T(8,128)(2,1)S(1)}, bf16[2,320,128]{2,1,0:T(8,128)(2,1)S(1)}, u32[]{:S(2)}, u32[]{:S(2)}) collective-permute-start(bf16[2,320,128]{2,1,0:T(8,128)(2,1)S(1)} %get-tuple-element.20), channel_id=1, source_target_pairs={{0,384},{128,0},{256,128},{384,256},{1,385},{129,1},{257,129},{385... | collective-permute-start | bytes 491528 | tf_op jit(solution)/shard_map/ppermute | solution.py:154
  116.4 11.9 %collective-permute-start.14 = (bf16[4,320,128]{2,1,0:T(8,128)(2,1)S(1)}, bf16[4,320,128]{2,1,0:T(8,128)(2,1)S(1)}, u32[]{:S(2)}, u32[]{:S(2)}) collective-permute-start(bf16[4,320,128]{2,1,0:T(8,128)(2,1)S(1)} %pad_maximum_fusion.1), channel_id=1, source_target_pairs={{0,384},{128,0},{256,128},{384,256},{1,385},{129,1},{257,129},{385... | collective-permute-start | bytes 983048 | tf_op jit(solution)/shard_map/ppermute | solution.py:154
  122.1 11.6 %collective-permute-start.12 = (bf16[4,320,128]{2,1,0:T(8,128)(2,1)S(1)}, bf16[4,320,128]{2,1,0:T(8,128)(2,1)S(1)}, u32[]{:S(2)}, u32[]{:S(2)}) collective-permute-start(bf16[4,320,128]{2,1,0:T(8,128)(2,1)S(1)} %pad_maximum_fusion), channel_id=1, source_target_pairs={{0,128},{128,256},{256,384},{384,0},{1,129},{129,257},{257,385},{3... | collective-permute-start | bytes 983048 | tf_op jit(solution)/shard_map/ppermute | solution.py:154
  134.6 34.4 %all-to-all-start.1 = ((bf16[64,20,128]{2,1,0:T(8,128)(2,1)}), bf16[64,20,128]{2,1,0:T(8,128)(2,1)S(1)}, u32[]{:S(2)}, u32[]{:S(2)}) async-start(bf16[64,20,128]{2,1,0:T(8,128)(2,1)} %reshape.19), calls=%async_computation.1 | async-start | bytes 786432 | tf_op jit(solution)/shard_map/all_to_all | solution.py:195
  169.0 0.8 copy-start.6

commit v2 on v1

v2 whole, which is shorter than its diff:
```python
import jax
import jax.numpy as jnp
from jax import lax
from jax.experimental import pallas as pl
from jax.experimental.pallas import tpu as pltpu
from jax.sharding import Mesh, PartitionSpec as P

NY, NZ, NC, NH, NX = 4, 4, 2, 4, 4
EXPERTS = NH * NX
TOK = 128
CAP = 20
MSG = 2 * CAP
COLS = 128
HID = 128
ROWS = EXPERTS * MSG
KEPT = EXPERTS * CAP
BF16 = jnp.bfloat16
F32 = jnp.float32
VMEM = pltpu.CompilerParams(vmem_limit_bytes=56 * 1024 * 1024)
CONTRACT_LAST = (((1,), (1,)), ((), ()))
CONTRACT_FIRST = (((0,), (0,)), ((), ()))


def slot_table(ids, rows_each, slot_of):
    experts = lax.broadcasted_iota(jnp.int32, (EXPERTS, TOK), 0)
    named = (experts == ids[0:1, :]) | (experts == ids[1:2, :])
    earlier = lax.broadcasted_iota(jnp.int32, (TOK, TOK), 0) < lax.broadcasted_iota(jnp.int32, (TOK, TOK), 1)
    prior = jnp.dot(named.astype(BF16), earlier.astype(BF16), preferred_element_type=F32)
    place = jnp.where(named, prior, -1.0).astype(BF16)
    shape = (EXPERTS, rows_each, TOK)
    expert = lax.broadcasted_iota(jnp.int32, shape, 0).reshape(EXPERTS * rows_each, TOK)
    row = lax.broadcasted_iota(jnp.int32, shape, 1).reshape(EXPERTS * rows_each, TOK)
    spread = (expert[:, :EXPERTS] == lax.broadcasted_iota(jnp.int32, (EXPERTS * rows_each, EXPERTS), 1)).astype(BF16)
    place_of_row = jnp.dot(spread, place, preferred_element_type=F32)
    return place_of_row == slot_of(row).astype(F32), expert, row


def dispatch_kernel(ids_ref, gate_ref, tok_ref, dy_ref, out_ref):
    ids = ids_ref[...]
    table, expert, row = slot_table(ids, MSG, lambda q: jnp.where(q >= CAP, q - CAP, q))
    gate = jnp.where(expert == ids[0:1, :], gate_ref[0:1, :], gate_ref[1:2, :])
    scale = jnp.sum(jnp.where(table, gate, 0.0), axis=1, keepdims=True)
    pick = table.astype(BF16)
    rows_in = jnp.dot(pick, tok_ref[...], preferred_element_type=F32)
    rows_dy = jnp.dot(pick, dy_ref[...], preferred_element_type=F32)
    out = jnp.where(row < CAP, rows_in, scale * rows_dy)
    out_ref[...] = out.astype(BF16).reshape(EXPERTS, MSG, COLS)


def split_kernel(pos_ref, w_in_ref, w_out_ref, after_ref, in_other, out_other):
    del after_ref
    c = pos_ref[1]
    for k in range(NY * NZ):
        first = pl.multiple_of((k * NC + 1 - c) * COLS, COLS)
        in_other[k] = w_in_ref[pl.ds(first, COLS), :]
        out_other[:, k * COLS:(k + 1) * COLS] = w_out_ref[:, pl.ds(first, COLS)]


def places(y, c, step):
    return lax.rem(y + jnp.where(c == 0, NY - step, step), NY)


def chunk(ref, zl):
    return ref[zl * EXPERTS:(zl + 1) * EXPERTS].reshape(ROWS, COLS)


def joined(first, second):
    return jnp.concatenate([first, second], axis=1)


def weights_in(w_in_ref, sib_ref, c, k):
    mine = w_in_ref[pl.ds(pl.multiple_of((k * NC + c) * COLS, COLS), COLS), :]
    return joined(mine, sib_ref[k])


def weights_out(w_out_ref, sib_ref, c, k):
    mine = w_out_ref[:, pl.ds(pl.multiple_of((k * NC + c) * COLS, COLS), COLS)]
    return jnp.concatenate([mine, sib_ref[:, pl.ds(pl.multiple_of(k * COLS, COLS), COLS)]], axis=0)


def forward(pos_ref, w_in_ref, w_in_sib_ref, w_out_ref, w_out_sib_ref, xs):
    y, c = pos_ref[0], pos_ref[1]
    pre = jnp.zeros((ROWS, NC * HID), F32)
    act_grad = jnp.zeros((ROWS, NC * HID), F32)
    for step, blocks in xs:
        at = places(y, c, step) * NZ
        for zl in range(0, NZ, 2):
            x = joined(*[chunk(*block) for block in blocks[zl:zl + 2]])
            w = jnp.concatenate([weights_in(w_in_ref, w_in_sib_ref, c, at + z) for z in (zl, zl + 1)], axis=0)
            v = joined(*[weights_out(w_out_ref, w_out_sib_ref, c, at + z) for z in (zl, zl + 1)])
            pre = pre + jnp.dot(x, w, preferred_element_type=F32)
            act_grad = act_grad + lax.dot_general(x, v, CONTRACT_LAST, preferred_element_type=F32)
    row = lax.broadcasted_iota(jnp.int32, (EXPERTS, MSG, NC * HID), 1).reshape(ROWS, NC * HID)
    return jnp.where(row < CAP, pre, act_grad)


def whole(ref):
    return [(ref, z) for z in range(NZ)]


def halves(low, high):
    return [(low, 0), (low, 1), (high, 0), (high, 1)]


def forward_first_kernel(pos_ref, wi, wis, wo, wos, x0, a1, b1, out_ref):
    out_ref[...] = forward(pos_ref, wi, wis, wo, wos, [(0, whole(x0)), (1, halves(a1, b1))])


def forward_last_kernel(pos_ref, wi, wis, wo, wos, a2, b2, a3, b3, before_ref, out_ref):
    xs = [(2, halves(a2, b2)), (3, halves(a3, b3))]
    out_ref[...] = before_ref[...] + forward(pos_ref, wi, wis, wo, wos, xs)


def middle_kernel(pos_ref, w_in_ref, w_in_sib_ref, part_ref, part_sib_ref, pgact_t_ref, out_ref):
    c = pos_ref[1]
    sib = part_sib_ref[...]
    both = part_ref[...] + joined(sib[:, HID:], sib[:, :HID])
    act_grad = jnp.concatenate([both[CAP:], both[:CAP]], axis=0)
    act, pullback = jax.vjp(lambda v: jax.nn.gelu(v, approximate=True), both)
    pre_grad = pullback(act_grad)[0]
    act = jnp.concatenate([act[ROWS - CAP:], act[:ROWS - CAP]], axis=0)
    row = lax.broadcasted_iota(jnp.int32, (EXPERTS, MSG, NC * HID), 1).reshape(ROWS, NC * HID)
    pre_grad = jnp.where(row < CAP, pre_grad, 0.0).astype(BF16)
    act = jnp.where(row < CAP, 0.0, act).astype(BF16)
    pgact_t_ref[...] = joined(pre_grad, act).T
    block = lax.broadcasted_iota(jnp.int32, (EXPERTS, CAP, ROWS), 0).reshape(KEPT, ROWS)
    within = lax.broadcasted_iota(jnp.int32, (EXPERTS, CAP, ROWS), 1).reshape(KEPT, ROWS)
    keep = (lax.broadcasted_iota(jnp.int32, (KEPT, ROWS), 1) == block * MSG + within).astype(BF16)
    pg = jnp.dot(keep, pre_grad, preferred_element_type=F32).astype(BF16)
    for k in range(0, NY * NZ, 2):
        w = jnp.concatenate([weights_in(w_in_ref, w_in_sib_ref, c, j) for j in (k, k + 1)], axis=0)
        out = lax.dot_general(pg, w, CONTRACT_LAST, preferred_element_type=F32).astype(BF16)
        for j in range(2):
            out_ref[(k + j) // NZ, (k + j) % NZ] = out[:, j * COLS:(j + 1) * COLS]


def grads_kernel(pos_ref, pgact_t_ref, x0, a1, b1, a2, b2, a3, b3, in_mine, in_other, out_mine, out_other):
    y, c = pos_ref[0], pos_ref[1]
    left = pgact_t_ref[...]
    for step, blocks in enumerate((whole(x0), halves(a1, b1), halves(a2, b2), halves(a3, b3))):
        at = places(y, c, step) * NZ
        for zl in range(0, NZ, 2):
            x = joined(*[chunk(*block) for block in blocks[zl:zl + 2]])
            both = jnp.dot(left, x, preferred_element_type=F32).astype(BF16)
            lanes = pl.ds(pl.multiple_of((at + zl) * COLS, 2 * COLS), 2 * COLS)
            for ref, first in ((in_mine, 0), (in_other, HID)):
                turned = both[first:first + HID].T
                ref[at + zl] = turned[:COLS]
                ref[at + zl + 1] = turned[COLS:]
            for ref, first in ((out_mine, 2 * HID), (out_other, 3 * HID)):
                ref[:, lanes] = both[first:first + HID]


def merge_kernel(pos_ref, in_mine, in_sib, out_mine, out_sib, w_in_grad_ref, w_out_grad_ref):
    c = pos_ref[1]
    for k in range(NY * NZ):
        for ins, outs, core in ((in_mine, out_mine, c), (in_sib, out_sib, 1 - c)):
            first = pl.multiple_of((k * NC + core) * COLS, COLS)
            w_in_grad_ref[pl.ds(first, COLS), :] = ins[k]
            w_out_grad_ref[:, pl.ds(first, COLS)] = outs[:, k * COLS:(k + 1) * COLS]


def combine_kernel(ids_ref, back_ref, out_ref):
    table, _, _ = slot_table(ids_ref[...], CAP, lambda q: q)
    total = back_ref[0:EXPERTS].astype(F32)
    for z in range(1, NZ):
        total = total + back_ref[z * EXPERTS:(z + 1) * EXPERTS].astype(F32)
    rows = total.reshape(KEPT, COLS).astype(BF16)
    out_ref[...] = lax.dot_general(
        table.astype(BF16), rows, CONTRACT_FIRST, preferred_element_type=F32
    ).astype(BF16)


SMEM = pl.BlockSpec(memory_space=pltpu.SMEM)
WHOLE = pl.BlockSpec(memory_space=pltpu.VMEM)
UNREAD = pl.BlockSpec(memory_space=pl.ANY)


def shape(*dims, kind=BF16):
    return jax.ShapeDtypeStruct(dims, kind)


def held(*dims, kind=BF16):
    return pltpu.VMEM(dims, kind)


def keep(value):
    return pltpu.with_memory_space_constraint(value, pltpu.VMEM)


def run(kernel, outs, scalars, *args, unread=0):
    specs = [SMEM] * scalars + [WHOLE] * (len(args) - scalars - unread) + [UNREAD] * unread
    out_specs = jax.tree.map(lambda _: WHOLE, outs)
    return pl.pallas_call(kernel, out_shape=outs, in_specs=specs, out_specs=out_specs, compiler_params=VMEM)(*args)


def ring(value):
    steps = [(i * NC + c, (i + (1 if c == 0 else NY - 1)) % NY * NC + c) for i in range(NY) for c in range(NC)]
    return lax.ppermute(value, ("y", "c"), steps)


def across(value):
    return lax.ppermute(value, "c", [(0, 1), (1, 0)])


def on_device(tokens, out_grad, expert_ids, gate_weights, w_in, w_out):
    pos = jnp.stack([lax.axis_index("y"), lax.axis_index("c")]).astype(jnp.int32)
    ids, gate = expert_ids.T, gate_weights.T
    w_in, w_out = w_in[0], w_out[0]
    blocks = NY * NZ
    half_in, half_out = held(blocks, COLS, HID), held(HID, blocks * COLS)
    send = run(dispatch_kernel, shape(EXPERTS, MSG, COLS), 0, ids, gate, tokens, out_grad)
    w_in_other, w_out_other = run(split_kernel, (half_in, half_out), 1, pos, w_in, w_out, send, unread=1)
    w_in_sib, w_out_sib = across(w_in_other), across(w_out_other)
    received = lax.all_to_all(send, ("zh", "x"), 0, 0, tiled=True)
    received, w_in_sib, w_out_sib = lax.optimization_barrier((received, w_in_sib, w_out_sib))
    x0 = lax.all_gather(received, "zl", axis=0, tiled=True)
    w_in_sib, w_out_sib = keep(w_in_sib), keep(w_out_sib)
    weights = (pos, w_in, w_in_sib, w_out, w_out_sib)
    cut = NZ // 2 * EXPERTS
    xs, a, b = [keep(x0)], x0[:cut], x0[cut:]
    for _ in range(NY - 1):
        a, b = ring(a), ring(b)
        xs += [keep(a), keep(b)]
    part = held(ROWS, NC * HID, kind=F32)
    first = run(forward_first_kernel, part, 1, *weights, *xs[:3])
    part = run(forward_last_kernel, part, 1, *weights, *xs[3:], keep(first))
    pgact_t, partial_rows = run(
        middle_kernel,
        (held(2 * NC * HID, ROWS), held(NY, NZ, KEPT, COLS)),
        1, pos, w_in, w_in_sib, keep(part), keep(across(part)),
    )
    parts = lax.all_to_all(partial_rows, "y", 0, 0, tiled=True)
    summed = jnp.sum(parts.astype(F32), axis=0).astype(BF16)
    back = lax.all_to_all(summed.reshape(NZ * EXPERTS, CAP, COLS), ("zl", "zh", "x"), 0, 0, tiled=True)
    tokens_grad = run(combine_kernel, shape(TOK, COLS), 0, ids, keep(back))
    in_mine, in_other, out_mine, out_other = run(
        grads_kernel, (half_in, half_in, half_out, half_out), 1, pos, keep(pgact_t), *xs
    )
    w_in_grad, w_out_grad = run(
        merge_kernel, (shape(*w_in.shape), shape(*w_out.shape)),
        1, pos, keep(in_mine), keep(across(in_other)), keep(out_mine), keep(across(out_other)),
    )
    return tokens_grad, w_in_grad[None], w_out_grad[None]


def solution(mesh):
    fine = Mesh(mesh.devices.reshape(NY, NZ, NC, NH, NX), ("y", "zl", "c", "zh", "x"))
    dp, expert = ("y", "zl", "c"), ("zh", "x")
    placed = (
        P(expert, dp),
        P(expert, dp),
        P(expert, None),
        P(expert, None),
        P(expert, None, dp),
        P(expert, dp, None),
    )
    return jax.shard_map(
        on_device,
        mesh=fine,
        in_specs=placed,
        out_specs=(P(expert, dp), P(expert, None, dp), P(expert, dp, None)),
        check_vma=False,
    )
```

time: 173 us -> 159 us (0.919)
  blocking collectives: 51 us -> 36.7 us
  waiting for transfers between devices: 43.8 us -> 47.1 us
  Pallas kernels: 20.2 us -> 17.4 us
    all_to_all x0 -> x1, starting transfers between devices: none -> 16.8 us  [on_device(): received = lax.all_to_all(send, ('zh', 'x'), 0, 0, tiled=True)]
    all_to_all x1, blocking collectives: 36 us -> 21.6 us  [on_device(): parts = lax.all_to_all(partial_rows, 'y', 0, 0, tiled=True)]
    ppermute x8 -> x6, starting transfers between devices: 28.9 us -> 15.3 us  [ring(): return lax.ppermute(value, ('y', 'c'), steps)]
    all_to_all x0 -> x1, waiting for transfers between devices: none -> 11 us  [on_device(): received = lax.all_to_all(send, ('zh', 'x'), 0, 0, tiled=True)]
    all_to_all x1, waiting for transfers between devices: 20.5 us -> 14.8 us  [on_device(): lax.all_to_all(summed.reshape(NZ * EXPERTS, CAP, COLS), ('zl', 'zh', 'x')...]
    ppermute x8 -> x6, waiting for transfers between devices: 20.7 us -> 16.2 us  [ring(): return lax.ppermute(value, ('y', 'c'), steps)]
    ppermute x7 -> x5, starting transfers between devices: 14.4 us -> 10.6 us  [across(): return lax.ppermute(value, 'c', [(0, 1), (1, 0)])]
    pallas_call x5 -> x8, Pallas kernels: 20.2 us -> 17.4 us  [run(): pl.pallas_call(kernel, out_shape=outs, in_specs=specs, out_specs=out_spec...]
  transfers between devices with their start and end apart: 16 -> 13, of which waited for: 9 -> 11; matrix products, arithmetic and copies ran while one was open for 1% -> 0% of each run, Pallas kernels for 3% -> 6%
where the time goes in v2:
time: 159 us; the launch traced here: 158 us
  starting transfers between devices  49.9 us (31%)
  waiting for transfers between devices  47.1 us (30%)
  blocking collectives  36.7 us (23%)
  Pallas kernels  17.4 us (11%)
  local copies, waits for them, and re-layouts  3.76 us (2%)
  other arithmetic  2.16 us (1%)
    all_to_all x1, blocking collectives, on_device(): parts = lax.all_to_all(partial_rows, 'y', 0, 0, tiled=True)  21.6 us
    pallas_call x8, Pallas kernels, run(): pl.pallas_call(kernel, out_shape=outs, in_specs=specs, out_specs=out_spec...  17.4 us
    all_to_all x1, starting transfers between devices, on_device(): received = lax.all_to_all(send, ('zh', 'x'), 0, 0, tiled=True)  16.8 us
    ppermute x6, waiting for transfers between devices, ring(): return lax.ppermute(value, ('y', 'c'), steps)  16.2 us
    ppermute x6, starting transfers between devices, ring(): return lax.ppermute(value, ('y', 'c'), steps)  15.3 us
    all_gather x1, blocking collectives, on_device(): x0 = lax.all_gather(received, 'zl', axis=0, tiled=True)  15.1 us
    all_to_all x1, waiting for transfers between devices, on_device(): lax.all_to_all(summed.reshape(NZ * EXPERTS, CAP, COLS), ('zl', 'zh', 'x')...  14.8 us
    all_to_all x1, waiting for transfers between devices, on_device(): received = lax.all_to_all(send, ('zh', 'x'), 0, 0, tiled=True)  11 us
  transfers between devices with their start and end apart: 13, of which 11 were waited for; matrix products, arithmetic and copies ran while one was open for 0% of the time, Pallas kernels for 6%

profile of v2, /device:TPU:32, one launch (start us, length us, event | category | flops | bytes accessed | tf_op | source)
XLA Modules:
  0.0 157.9 jit_solution(5913086878174230388)
XLA Ops:
  0.6 2.0 %shard_map.85.after_ref = bf16[16,40,128]{2,1,0:T(8,128)(2,1)} custom-call(s32[2,128]{1,0:T(2,128)} %bitcast.15, f32[2,128]{1,0:T(2,128)} %bitcast.17, bf16[128,128]{1,0:T(8,128)(2,1)} %tok_ref.1, bf16[128,128]{1,0:T(8,128)(2,1)} %dy_ref.1), custom_call_target="tpu_custom_call" | custom-call | tf_op jit(solution)/shard_map/pallas_call | solution.py:194
  2.6 16.8 %all-to-all-start = ((bf16[16,40,128]{2,1,0:T(8,128)(2,1)}), bf16[16,40,128]{2,1,0:T(8,128)(2,1)S(1)}, u32[]{:S(2)}, u32[]{:S(2)}) async-start(bf16[16,40,128]{2,1,0:T(8,128)(2,1)} %shard_map.85.after_ref), calls=%async_computation | async-start | bytes 327680 | tf_op jit(solution)/shard_map/all_to_all | solution.py:215
  19.4 0.6 pad_add_fusion.pos_ref
  20.0 1.7 %shard_map.86 = (bf16[16,128,128]{2,1,0:T(8,128)(2,1)S(1)}, bf16[128,2048]{1,0:T(8,128)(2,1)S(1)}) custom-call(s32[2]{0:T(128)} %pad_add_fusion.pos_ref, bf16[4096,128]{1,0:T(8,128)(2,1)} %bitcast.8, bf16[128,4096]{1,0:T(8,128)(2,1)} %bitcast.12, bf16[16,40,128]{2,1,0:T(8,128)(2,1)} %shard_map.85.after_ref), custom_call_target="tpu_custom_call" | custom-call | tf_op jit(solution)/shard_map/pallas_call | solution.py:194
  21.7 1.9 %collective-permute-start = (bf16[16,128,128]{2,1,0:T(8,128)(2,1)S(1)}, bf16[16,128,128]{2,1,0:T(8,128)(2,1)S(1)}, u32[]{:S(2)}, u32[]{:S(2)}) collective-permute-start(bf16[16,128,128]{2,1,0:T(8,128)(2,1)S(1)} %get-tuple-element.16), channel_id=1, source_target_pairs={{0,16},{16,0},{1,17},{17,1},{2,18},{18,2},{3,19},{19,3},{4,20},{20... | collective-permute-start | bytes 1572872 | tf_op jit(solution)/shard_map/ppermute | solution.py:203
  23.6 2.4 %collective-permute-start.1 = (bf16[128,2048]{1,0:T(8,128)(2,1)S(1)}, bf16[128,2048]{1,0:T(8,128)(2,1)S(1)}, u32[]{:S(2)}, u32[]{:S(2)}) collective-permute-start(bf16[128,2048]{1,0:T(8,128)(2,1)S(1)} %get-tuple-element.17), channel_id=1, source_target_pairs={{0,16},{16,0},{1,17},{17,1},{2,18},{18,2},{3,19},{19,3},{4,20},{20... | collective-permute-start | bytes 1572872 | tf_op jit(solution)/shard_map/ppermute | solution.py:203
  26.0 0.0 collective-permute-done.wis.w_in_sib_ref
  26.0 1.5 collective-permute-done.1.wos
  27.6 11.0 %all-to-all-done = bf16[16,40,128]{2,1,0:T(8,128)(2,1)S(1)} async-done(((bf16[16,40,128]{2,1,0:T(8,128)(2,1)}), bf16[16,40,128]{2,1,0:T(8,128)(2,1)S(1)}, u32[]{:S(2)}, u32[]{:S(2)}) %all-to-all-start) | async-done | bytes 163872 | tf_op jit(solution)/shard_map/all_to_all | solution.py:215
  38.6 15.1 %all_gather.3.x0 = bf16[64,40,128]{2,1,0:T(8,128)(2,1)S(1)} all-gather(bf16[16,40,128]{2,1,0:T(8,128)(2,1)S(1)} %all-to-all-done), channel_id=1, replica_groups=mesh['y'=4,'zl'=4,'c'=2,'zh'=4,'x'=4] {'zl'}, dimensions={0}, use_global_device_ids=true | all-gather | bytes 819200 | tf_op jit(solution)/shard_map/all_gather | solution.py:217
  53.7 0.1 fusion
  53.7 3.5 %collective-permute-start.2 = (bf16[32,40,128]{2,1,0:T(8,128)(2,1)S(1)}, bf16[32,40,128]{2,1,0:T(8,128)(2,1)S(1)}, u32[]{:S(2)}, u32[]{:S(2)}) collective-permute-start(bf16[32,40,128]{2,1,0:T(8,128)(2,1)S(1)} %get-tuple-element.30), channel_id=1, source_target_pairs={{0,128},{16,400},{128,256},{144,16},{256,384},{272,144},{384,0},{4... | collective-permute-start | bytes 983048 | tf_op jit(solution)/shard_map/ppermute | solution.py:199
  57.2 3.5 %collective-permute-start.4 = (bf16[32,40,128]{2,1,0:T(8,128)(2,1)S(1)}, bf16[32,40,128]{2,1,0:T(8,128)(2,1)S(1)}, u32[]{:S(2)}, u32[]{:S(2)}) collective-permute-start(bf16[32,40,128]{2,1,0:T(8,128)(2,1)S(1)} %get-tuple-element.29), channel_id=1, source_target_pairs={{0,128},{16,400},{128,256},{144,16},{256,384},{272,144},{384,0},{4... | collective-permute-start | bytes 983048 | tf_op jit(solution)/shard_map/ppermute | solution.py:199
  60.7 3.2 %collective-permute-done.2.a1 = bf16[32,40,128]{2,1,0:T(8,128)(2,1)S(1)} collective-permute-done((bf16[32,40,128]{2,1,0:T(8,128)(2,1)S(1)}, bf16[32,40,128]{2,1,0:T(8,128)(2,1)S(1)}, u32[]{:S(2)}, u32[]{:S(2)}) %collective-permute-start.2) | collective-permute-done | bytes 327712 | tf_op jit(solution)/shard_map/ppermute | solution.py:199
  63.9 2.3 %collective-permute-start.3 = (bf16[32,40,128]{2,1,0:T(8,128)(2,1)S(1)}, bf16[32,40,128]{2,1,0:T(8,128)(2,1)S(1)}, u32[]{:S(2)}, u32[]{:S(2)}) collective-permute-start(bf16[32,40,128]{2,1,0:T(8,128)(2,1)S(1)} %collective-permute-done.2.a1), channel_id=1, source_target_pairs={{0,128},{16,400},{128,256},{144,16},{256,384},{272,144},{384,0},{4... | collective-permute-start | bytes 983048 | tf_op jit(solution)/shard_map/ppermute | solution.py:199
  66.2 1.2 collective-permute-done.4.b1
  67.4 0.0 copy-start
  67.4 2.3 %collective-permute-start.5 = (bf16[32,40,128]{2,1,0:T(8,128)(2,1)S(1)}, bf16[32,40,128]{2,1,0:T(8,128)(2,1)S(1)}, u32[]{:S(2)}, u32[]{:S(2)}) collective-permute-start(bf16[32,40,128]{2,1,0:T(8,128)(2,1)S(1)} %collective-permute-done.4.b1), channel_id=1, source_target_pairs={{0,128},{16,400},{128,256},{144,16},{256,384},{272,144},{384,0},{4... | collective-permute-start | bytes 983048 | tf_op jit(solution)/shard_map/ppermute | solution.py:199
  69.7 4.4 %collective-permute-done.3.a2 = bf16[32,40,128]{2,1,0:T(8,128)(2,1)S(1)} collective-permute-done((bf16[32,40,128]{2,1,0:T(8,128)(2,1)S(1)}, bf16[32,40,128]{2,1,0:T(8,128)(2,1)S(1)}, u32[]{:S(2)}, u32[]{:S(2)}) %collective-permute-start.3) | collective-permute-done | bytes 327712 | tf_op jit(solution)/shard_map/ppermute | solution.py:199
  74.1 1.9 %collective-permute-start.6 = (bf16[32,40,128]{2,1,0:T(8,128)(2,1)S(1)}, bf16[32,40,128]{2,1,0:T(8,128)(2,1)S(1)}, u32[]{:S(2)}, u32[]{:S(2)}) collective-permute-start(bf16[32,40,128]{2,1,0:T(8,128)(2,1)S(1)} %collective-permute-done.3.a2), channel_id=1, source_target_pairs={{0,128},{16,400},{128,256},{144,16},{256,384},{272,144},{384,0},{4... | collective-permute-start | bytes 983048 | tf_op jit(solution)/shard_map/ppermute | solution.py:199
  76.0 1.6 %collective-permute-done.5.b2 = bf16[32,40,128]{2,1,0:T(8,128)(2,1)S(1)} collective-permute-done((bf16[32,40,128]{2,1,0:T(8,128)(2,1)S(1)}, bf16[32,40,128]{2,1,0:T(8,128)(2,1)S(1)}, u32[]{:S(2)}, u32[]{:S(2)}) %collective-permute-start.5) | collective-permute-done | bytes 327712 | tf_op jit(solution)/shard_map/ppermute | solution.py:199
  77.6 1.9 %collective-permute-start.7 = (bf16[32,40,128]{2,1,0:T(8,128)(2,1)S(1)}, bf16[32,40,128]{2,1,0:T(8,128)(2,1)S(1)}, u32[]{:S(2)}, u32[]{:S(2)}) collective-permute-start(bf16[32,40,128]{2,1,0:T(8,128)(2,1)S(1)} %collective-permute-done.5.b2), channel_id=1, source_target_pairs={{0,128},{16,400},{128,256},{144,16},{256,384},{272,144},{384,0},{4... | collective-permute-start | bytes 983048 | tf_op jit(solution)/shard_map/ppermute | solution.py:199
  79.5 2.4 %shard_map.87.before_ref = f32[640,256]{1,0:T(8,128)S(1)} custom-call(s32[2]{0:T(128)} %pad_add_fusion.pos_ref, bf16[4096,128]{1,0:T(8,128)(2,1)} %bitcast.9, bf16[16,128,128]{2,1,0:T(8,128)(2,1)S(1)} %collective-permute-done.wis.w_in_sib_ref, bf16[128,4096]{1,0:T(8,128)(2,1)} %bitcast.13, bf16[128,2048]{1,0:T(8,128)(2,1)S(1)} %collective-permute-done.1.wos, ...), custom_call_target="tpu_custom_call" | custom-call | tf_op jit(solution)/shard_map/pallas_call | solution.py:194
  81.9 0.0 copy-done
  81.9 2.3 %collective-permute-done.6.a3 = bf16[32,40,128]{2,1,0:T(8,128)(2,1)S(1)} collective-permute-done((bf16[32,40,128]{2,1,0:T(8,128)(2,1)S(1)}, bf16[32,40,128]{2,1,0:T(8,128)(2,1)S(1)}, u32[]{:S(2)}, u32[]{:S(2)}) %collective-permute-start.6) | collective-permute-done | bytes 327712 | tf_op jit(solution)/shard_map/ppermute | solution.py:199
  84.2 3.5 %collective-permute-done.7.b3 = bf16[32,40,128]{2,1,0:T(8,128)(2,1)S(1)} collective-permute-done((bf16[32,40,128]{2,1,0:T(8,128)(2,1)S(1)}, bf16[32,40,128]{2,1,0:T(8,128)(2,1)S(1)}, u32[]{:S(2)}, u32[]{:S(2)}) %collective-permute-start.7) | collective-permute-done | bytes 327712 | tf_op jit(solution)/shard_map/ppermute | solution.py:199
  87.7 2.4 %shard_map.88.part_ref = f32[640,256]{1,0:T(8,128)S(1)} custom-call(s32[2]{0:T(128)} %pad_add_fusion.pos_ref, bf16[4096,128]{1,0:T(8,128)(2,1)} %bitcast.10, bf16[16,128,128]{2,1,0:T(8,128)(2,1)S(1)} %collective-permute-done.wis.w_in_sib_ref, bf16[128,4096]{1,0:T(8,128)(2,1)} %bitcast.14, bf16[128,2048]{1,0:T(8,128)(2,1)S(1)} %collective-permute-done.1.wos, ...), custom_call_target="tpu_custom_call" | custom-call | tf_op jit(solution)/shard_map/pallas_call | solution.py:194
  90.2 1.9 %collective-permute-start.8 = (f32[640,256]{1,0:T(8,128)S(1)}, f32[640,256]{1,0:T(8,128)S(1)}, u32[]{:S(2)}, u32[]{:S(2)}) collective-permute-start(f32[640,256]{1,0:T(8,128)S(1)} %shard_map.88.part_ref), channel_id=1, source_target_pairs={{0,16},{16,0},{1,17},{17,1},{2,18},{18,2},{3,19},{19,3},{4,20},{20... | collective-permute-start | bytes 1966088 | tf_op jit(solution)/shard_map/ppermute | solution.py:203
  92.1 2.1 %collective-permute-done.8.part_sib_ref = f32[640,256]{1,0:T(8,128)S(1)} collective-permute-done((f32[640,256]{1,0:T(8,128)S(1)}, f32[640,256]{1,0:T(8,128)S(1)}, u32[]{:S(2)}, u32[]{:S(2)}) %collective-permute-start.8) | collective-permute-done | bytes 655392 | tf_op jit(solution)/shard_map/ppermute | solution.py:203
  94.2 2.3 %shard_map.89 = (bf16[512,640]{1,0:T(8,128)(2,1)S(1)}, bf16[4,4,320,128]{3,2,1,0:T(8,128)(2,1)S(1)}) custom-call(s32[2]{0:T(128)} %pad_add_fusion.pos_ref, bf16[4096,128]{1,0:T(8,128)(2,1)} %bitcast.11, bf16[16,128,128]{2,1,0:T(8,128)(2,1)S(1)} %collective-permute-done.wis.w_in_sib_ref, f32[640,256]{1,0:T(8,128)S(1)} %shard_map.88.part_ref, ...), custom_call_target="tpu_custom_call" | custom-call | tf_op jit(solution)/shard_map/pallas_call | solution.py:194
  96.5 0.0 copy-start.2
  96.5 0.8 copy-done.2
  97.3 21.6 %all_to_all.15 = bf16[4,4,320,128]{3,2,1,0:T(8,128)(2,1)} all-to-all(bf16[4,4,320,128]{3,2,1,0:T(8,128)(2,1)S(1)} %get-tuple-element.21), channel_id=1, replica_groups=mesh['y'=4,'zl'=4,'c'=2,'zh'=4,'x'=4] {'y'}, dimensions={0} | all-to-all | bytes 2621440 | tf_op jit(solution)/shard_map/all_to_all | solution.py:233
  119.0 1.6 reduce_sum.12
  120.6 0.8 reshape.9
  121.4 7.3 %all-to-all-start.2 = ((bf16[64,20,128]{2,1,0:T(8,128)(2,1)}), bf16[64,20,128]{2,1,0:T(8,128)(2,1)S(1)}, u32[]{:S(2)}, u32[]{:S(2)}) async-start(bf16[64,20,128]{2,1,0:T(8,128)(2,1)} %reshape.9), calls=%async_computation.2 | async-start | bytes 786432 | tf_op jit(solution)/shard_map/all_to_all | solution.py:235
  128.7 0.0 copy-start.1
  128.7 1.0 copy-done.1
  129.6 0.0 copy-start.3
  129.6 1.1 copy-done.3
  130.7 2.5 %shard_map.91 = (bf16[16,128,128]{2,1,0:T(8,128)(2,1)S(1)}, bf16[16,128,128]{2,1,0:T(8,128)(2,1)S(1)}, bf16[128,2048]{1,0:T(8,128)(2,1)S(1)}, bf16[128,2048]{1,0:T(8,128)(2,1)S(1)}) custom-call(s32[2]{0:T(128)} %pad_add_fusion.pos_ref, bf16[512,640]{1,0:T(8,128)(2,1)S(1)} %copy-done.3, bf16[64,40,128]{2,1,0:T(8,128)(2,1)S(1)} %all_gather.3.x0, ...), custom_call_target="tpu_custom_call" | custom-call | tf_op jit(solution)/shard_map/pallas_call | solution.py:194
  133.2 1.9 %collective-permute-start.9 = (bf16[16,128,128]{2,1,0:T(8,128)(2,1)S(1)}, bf16[16,128,128]{2,1,0:T(8,128)(2,1)S(1)}, u32[]{:S(2)}, u32[]{:S(2)}) collective-permute-start(bf16[16,128,128]{2,1,0:T(8,128)(2,1)S(1)} %get-tuple-element.24), channel_id=1, source_target_pairs={{0,16},{16,0},{1,17},{17,1},{2,18},{18,2},{3,19},{19,3},{4,20},{20... | collective-permute-start | bytes 1572872 | tf_op jit(solution)/shard_map/ppermute | solution.py:203
  135.1 2.4 %collective-permute-start.10 = (bf16[128,2048]{1,0:T(8,128)(2,1)S(1)}, bf16[128,2048]{1,0:T(8,128)(2,1)S(1)}, u32[]{:S(2)}, u32[]{:S(2)}) collective-permute-start(bf16[128,2048]{1,0:T(8,128)(2,1)S(1)} %get-tuple-element.26), channel_id=1, source_target_pairs={{0,16},{16,0},{1,17},{17,1},{2,18},{18,2},{3,19},{19,3},{4,20},{20... | collective-permute-start | bytes 1572872 | tf_op jit(solution)/shard_map/ppermute | solution.py:203
  137.5 0.0 collective-permute-done.9.in_sib
  137.5 1.5 collective-permute-done.10.out_sib
  139.1 2.3 %shard_map.92 = (bf16[4096,128]{1,0:T(8,128)(2,1)}, bf16[128,4096]{1,0:T(8,128)(2,1)}) custom-call(s32[2]{0:T(128)} %pad_add_fusion.pos_ref, bf16[16,128,128]{2,1,0:T(8,128)(2,1)S(1)} %get-tuple-element.23.in_mine, bf16[16,128,128]{2,1,0:T(8,128)(2,1)S(1)} %collective-permute-done.9.in_sib, bf16[128,2048]{1,0:T(8,128)(2,1)S(1)} %get-tuple-element.25.out_mine, ...), custom_call_target="tpu_custom_call" | custom-call | tf_op jit(solution)/shard_map/pallas_call | solution.py:194
  141.4 14.8 %all-to-all-done.2.back_ref = bf16[64,20,128]{2,1,0:T(8,128)(2,1)S(1)} async-done(((bf16[64,20,128]{2,1,0:T(8,128)(2,1)}), bf16[64,20,128]{2,1,0:T(8,128)(2,1)S(1)}, u32[]{:S(2)}, u32[]{:S(2)}) %all-to-all-start.2) | async-done | bytes 327712 | tf_op jit(solution)/shard_map/all_to_all | solution.py:235
  156.2 1.8 %shard_map.90 = bf16[128,128]{1,0:T(8,128)(2,1)} custom-call(s32[2,128]{1,0:T(2,128)} %bitcast.16, bf16[64,20,128]{2,1,0:T(8,128)(2,1)S(1)} %all-to-all-done.2.back_ref), custom_call_target="tpu_custom_call" | custom-call | tf_op jit(solution)/shard_map/pallas_call | solution.py:194
Async XLA Ops:
  2.6 36.0 %all-to-all-start = ((bf16[16,40,128]{2,1,0:T(8,128)(2,1)}), bf16[16,40,128]{2,1,0:T(8,128)(2,1)S(1)}, u32[]{:S(2)}, u32[]{:S(2)}) async-start(bf16[16,40,128]{2,1,0:T(8,128)(2,1)} %shard_map.85.after_ref), calls=%async_computation | async-start | bytes 327680 | tf_op jit(solution)/shard_map/all_to_all | solution.py:215
  21.7 4.3 %collective-permute-start = (bf16[16,128,128]{2,1,0:T(8,128)(2,1)S(1)}, bf16[16,128,128]{2,1,0:T(8,128)(2,1)S(1)}, u32[]{:S(2)}, u32[]{:S(2)}) collective-permute-start(bf16[16,128,128]{2,1,0:T(8,128)(2,1)S(1)} %get-tuple-element.16), channel_id=1, source_target_pairs={{0,16},{16,0},{1,17},{17,1},{2,18},{18,2},{3,19},{19,3},{4,20},{20... | collective-permute-start | bytes 1572872 | tf_op jit(solution)/shard_map/ppermute | solution.py:203
  23.6 3.9 %collective-permute-start.1 = (bf16[128,2048]{1,0:T(8,128)(2,1)S(1)}, bf16[128,2048]{1,0:T(8,128)(2,1)S(1)}, u32[]{:S(2)}, u32[]{:S(2)}) collective-permute-start(bf16[128,2048]{1,0:T(8,128)(2,1)S(1)} %get-tuple-element.17), channel_id=1, source_target_pairs={{0,16},{16,0},{1,17},{17,1},{2,18},{18,2},{3,19},{19,3},{4,20},{20... | collective-permute-start | bytes 1572872 | tf_op jit(solution)/shard_map/ppermute | solution.py:203
  53.7 10.2 %collective-permute-start.2 = (bf16[32,40,128]{2,1,0:T(8,128)(2,1)S(1)}, bf16[32,40,128]{2,1,0:T(8,128)(2,1)S(1)}, u32[]{:S(2)}, u32[]{:S(2)}) collective-permute-start(bf16[32,40,128]{2,1,0:T(8,128)(2,1)S(1)} %get-tuple-element.30), channel_id=1, source_target_pairs={{0,128},{16,400},{128,256},{144,16},{256,384},{272,144},{384,0},{4... | collective-permute-start | bytes 983048 | tf_op jit(solution)/shard_map/ppermute | solution.py:199
  57.2 10.2 %collective-permute-start.4 = (bf16[32,40,128]{2,1,0:T(8,128)(2,1)S(1)}, bf16[32,40,128]{2,1,0:T(8,128)(2,1)S(1)}, u32[]{:S(2)}, u32[]{:S(2)}) collective-permute-start(bf16[32,40,128]{2,1,0:T(8,128)(2,1)S(1)} %get-tuple-element.29), channel_id=1, source_target_pairs={{0,128},{16,400},{128,256},{144,16},{256,384},{272,144},{384,0},{4... | collective-permute-start | bytes 983048 | tf_op jit(solution)/shard_map/ppermute | solution.py:199
  63.9 10.2 %collective-permute-start.3 = (bf16[32,40,128]{2,1,0:T(8,128)(2,1)S(1)}, bf16[32,40,128]{2,1,0:T(8,128)(2,1)S(1)}, u32[]{:S(2)}, u32[]{:S(2)}) collective-permute-start(bf16[32,40,128]{2,1,0:T(8,128)(2,1)S(1)} %collective-permute-done.2.a1), channel_id=1, source_target_pairs={{0,128},{16,400},{128,256},{144,16},{256,384},{272,144},{384,0},{4... | collective-permute-start | bytes 983048 | tf_op jit(solution)/shard_map/ppermute | solution.py:199
  67.4 14.5 %copy-start = (bf16[32,40,128]{2,1,0:T(8,128)(2,1)}, bf16[32,40,128]{2,1,0:T(8,128)(2,1)S(1)}, u32[]{:S(2)}) copy-start(bf16[32,40,128]{2,1,0:T(8,128)(2,1)S(1)} %collective-permute-done.4.b1) | copy-start | bytes 983044
  67.4 10.2 %collective-permute-start.5 = (bf16[32,40,128]{2,1,0:T(8,128)(2,1)S(1)}, bf16[32,40,128]{2,1,0:T(8,128)(2,1)S(1)}, u32[]{:S(2)}, u32[]{:S(2)}) collective-permute-start(bf16[32,40,128]{2,1,0:T(8,128)(2,1)S(1)} %collective-permute-done.4.b1), channel_id=1, source_target_pairs={{0,128},{16,400},{128,256},{144,16},{256,384},{272,144},{384,0},{4... | collective-permute-start | bytes 983048 | tf_op jit(solution)/shard_map/ppermute | solution.py:199
  74.1 10.2 %collective-permute-start.6 = (bf16[32,40,128]{2,1,0:T(8,128)(2,1)S(1)}, bf16[32,40,128]{2,1,0:T(8,128)(2,1)S(1)}, u32[]{:S(2)}, u32[]{:S(2)}) collective-permute-start(bf16[32,40,128]{2,1,0:T(8,128)(2,1)S(1)} %collective-permute-done.3.a2), channel_id=1, source_target_pairs={{0,128},{16,400},{128,256},{144,16},{256,384},{272,144},{384,0},{4... | collective-permute-start | bytes 983048 | tf_op jit(solution)/shard_map/ppermute | solution.py:199
  77.6 10.2 %collective-permute-start.7 = (bf16[32,40,128]{2,1,0:T(8,128)(2,1)S(1)}, bf16[32,40,128]{2,1,0:T(8,128)(2,1)S(1)}, u32[]{:S(2)}, u32[]{:S(2)}) collective-permute-start(bf16[32,40,128]{2,1,0:T(8,128)(2,1)S(1)} %collective-permute-done.5.b2), channel_id=1, source_target_pairs={{0,128},{16,400},{128,256},{144,16},{256,384},{272,144},{384,0},{4... | collective-permute-start | bytes 983048 | tf_op jit(solution)/shard_map/ppermute | solution.py:199
  90.2 4.0 %collective-permute-start.8 = (f32[640,256]{1,0:T(8,128)S(1)}, f32[640,256]{1,0:T(8,128)S(1)}, u32[]{:S(2)}, u32[]{:S(2)}) collective-permute-start(f32[640,256]{1,0:T(8,128)S(1)} %shard_map.88.part_ref), channel_id=1, source_target_pairs={{0,16},{16,0},{1,17},{17,1},{2,18},{18,2},{3,19},{19,3},{4,20},{20... | collective-permute-start | bytes 1966088 | tf_op jit(solution)/shard_map/ppermute | solution.py:203
  96.5 0.8 copy-start.2
  121.4 34.8 %all-to-all-start.2 = ((bf16[64,20,128]{2,1,0:T(8,128)(2,1)}), bf16[64,20,128]{2,1,0:T(8,128)(2,1)S(1)}, u32[]{:S(2)}, u32[]{:S(2)}) async-start(bf16[64,20,128]{2,1,0:T(8,128)(2,1)} %reshape.9), calls=%async_computation.2 | async-start | bytes 786432 | tf_op jit(solution)/shard_map/all_to_all | solution.py:235
  128.7 1.0 copy-start.1
  129.6 1.1 copy-start.3
  133.2 4.3 %collective-permute-start.9 = (bf16[16,128,128]{2,1,0:T(8,128)(2,1)S(1)}, bf16[16,128,128]{2,1,0:T(8,128)(2,1)S(1)}, u32[]{:S(2)}, u32[]{:S(2)}) collective-permute-start(bf16[16,128,128]{2,1,0:T(8,128)(2,1)S(1)} %get-tuple-element.24), channel_id=1, source_target_pairs={{0,16},{16,0},{1,17},{17,1},{2,18},{18,2},{3,19},{19,3},{4,20},{20... | collective-permute-start | bytes 1572872 | tf_op jit(solution)/shard_map/ppermute | solution.py:203
  135.1 3.9 %collective-permute-start.10 = (bf16[128,2048]{1,0:T(8,128)(2,1)S(1)}, bf16[128,2048]{1,0:T(8,128)(2,1)S(1)}, u32[]{:S(2)}, u32[]{:S(2)}) collective-permute-start(bf16[128,2048]{1,0:T(8,128)(2,1)S(1)} %get-tuple-element.26), channel_id=1, source_target_pairs={{0,16},{16,0},{1,17},{17,1},{2,18},{18,2},{3,19},{19,3},{4,20},{20... | collective-permute-start | bytes 1572872 | tf_op jit(solution)/shard_map/ppermute | solution.py:203

commit v3 on v2

v3 whole, which is shorter than its diff:
```python
import jax
import jax.numpy as jnp
from jax import lax
from jax.experimental import pallas as pl
from jax.experimental.pallas import tpu as pltpu
from jax.sharding import Mesh, PartitionSpec as P

NY, NZ, NC, NH, NX = 4, 4, 2, 4, 4
EXPERTS = NH * NX
TOK = 128
CAP = 20
MSG = 2 * CAP
COLS = 128
HID = 128
ROWS = EXPERTS * MSG
KEPT = EXPERTS * CAP
BF16 = jnp.bfloat16
F32 = jnp.float32
VMEM = pltpu.CompilerParams(vmem_limit_bytes=24 * 1024 * 1024)
CONTRACT_LAST = (((1,), (1,)), ((), ()))
CONTRACT_FIRST = (((0,), (0,)), ((), ()))


def slot_table(ids, rows_each, slot_of):
    experts = lax.broadcasted_iota(jnp.int32, (EXPERTS, TOK), 0)
    named = (experts == ids[0:1, :]) | (experts == ids[1:2, :])
    earlier = lax.broadcasted_iota(jnp.int32, (TOK, TOK), 0) < lax.broadcasted_iota(jnp.int32, (TOK, TOK), 1)
    prior = jnp.dot(named.astype(BF16), earlier.astype(BF16), preferred_element_type=F32)
    place = jnp.where(named, prior, -1.0).astype(BF16)
    shape = (EXPERTS, rows_each, TOK)
    expert = lax.broadcasted_iota(jnp.int32, shape, 0).reshape(EXPERTS * rows_each, TOK)
    row = lax.broadcasted_iota(jnp.int32, shape, 1).reshape(EXPERTS * rows_each, TOK)
    spread = (expert[:, :EXPERTS] == lax.broadcasted_iota(jnp.int32, (EXPERTS * rows_each, EXPERTS), 1)).astype(BF16)
    place_of_row = jnp.dot(spread, place, preferred_element_type=F32)
    return place_of_row == slot_of(row).astype(F32), expert, row


def dispatch_kernel(ids_ref, gate_ref, tok_ref, dy_ref, out_ref):
    ids = ids_ref[...]
    table, expert, row = slot_table(ids, MSG, lambda q: jnp.where(q >= CAP, q - CAP, q))
    gate = jnp.where(expert == ids[0:1, :], gate_ref[0:1, :], gate_ref[1:2, :])
    scale = jnp.sum(jnp.where(table, gate, 0.0), axis=1, keepdims=True)
    pick = table.astype(BF16)
    rows_in = jnp.dot(pick, tok_ref[...], preferred_element_type=F32)
    rows_dy = jnp.dot(pick, dy_ref[...], preferred_element_type=F32)
    out = jnp.where(row < CAP, rows_in, scale * rows_dy)
    out_ref[...] = out.astype(BF16).reshape(EXPERTS, MSG, COLS)


def split_kernel(pos_ref, w_in_ref, w_out_ref, after_ref, in_ref, out_ref, sems):
    del after_ref
    other = 1 - pos_ref[1]
    blocks = NY * NZ
    copies = [pltpu.make_async_copy(w_in_ref.at[:, other], in_ref, sems.at[blocks])]
    for k in range(blocks):
        columns = pl.ds(pl.multiple_of((k * NC + other) * COLS, COLS), COLS)
        copies.append(pltpu.make_async_copy(w_out_ref.at[:, columns], out_ref.at[k], sems.at[k]))
    for copy in copies:
        copy.start()
    for copy in copies:
        copy.wait()


def table_kernel(ids_ref, after_ref, table_ref):
    del after_ref
    table, _, _ = slot_table(ids_ref[...], CAP, lambda q: q)
    table_ref[...] = table.astype(BF16)


def places(y, c):
    near, far = y + 1 - 2 * lax.rem(y, 2), NY - 1 - y
    return y, jnp.where(c == 0, near, far), jnp.where(c == 0, far, near), lax.rem(y + 2, NY)


def chunk(ref, zl):
    return ref[zl * EXPERTS:(zl + 1) * EXPERTS].reshape(ROWS, COLS)


def joined(first, second):
    return jnp.concatenate([first, second], axis=1)


def weights_in(w_in_ref, sib_ref, c, k):
    mine = w_in_ref[pl.ds(pl.multiple_of((k * NC + c) * COLS, COLS), COLS), :]
    return joined(mine, sib_ref[k])


def weights_out(w_out_ref, sib_ref, c, k):
    mine = w_out_ref[:, pl.ds(pl.multiple_of((k * NC + c) * COLS, COLS), COLS)]
    return jnp.concatenate([mine, sib_ref[k]], axis=0)


def forward(pos_ref, w_in_ref, w_out_ref, in_sib_ref, out_sib_ref, xs):
    c = pos_ref[1]
    at_of = places(pos_ref[0], c)
    pre = jnp.zeros((ROWS, NC * HID), F32)
    act_grad = jnp.zeros((ROWS, NC * HID), F32)
    for place, blocks in xs:
        at = at_of[place] * NZ
        for zl in range(0, NZ, 2):
            x = joined(chunk(*blocks[zl]), chunk(*blocks[zl + 1]))
            w = jnp.concatenate([weights_in(w_in_ref, in_sib_ref, c, at + z) for z in (zl, zl + 1)], axis=0)
            v = joined(*[weights_out(w_out_ref, out_sib_ref, c, at + z) for z in (zl, zl + 1)])
            pre = pre + jnp.dot(x, w, preferred_element_type=F32)
            act_grad = act_grad + lax.dot_general(x, v, CONTRACT_LAST, preferred_element_type=F32)
    row = lax.broadcasted_iota(jnp.int32, (EXPERTS, MSG, NC * HID), 1).reshape(ROWS, NC * HID)
    return jnp.where(row < CAP, pre, act_grad)


def whole(ref):
    return [(ref, z) for z in range(NZ)]


def halves(low, high):
    return [(low, 0), (low, 1), (high, 0), (high, 1)]


def forward_first_kernel(pos_ref, wi, wo, wis, wos, own, first_a, first_b, out_ref):
    out_ref[...] = forward(pos_ref, wi, wo, wis, wos, [(0, whole(own)), (1, halves(first_a, first_b))])


def forward_second_kernel(pos_ref, wi, wo, wis, wos, second_a, second_b, before_ref, out_ref):
    out_ref[...] = before_ref[...] + forward(pos_ref, wi, wo, wis, wos, [(2, halves(second_a, second_b))])


def forward_last_kernel(pos_ref, wi, wo, wis, wos, last_a, last_b, before_ref, out_ref, sent_ref):
    total = before_ref[...] + forward(pos_ref, wi, wo, wis, wos, [(3, halves(last_a, last_b))])
    out_ref[...] = total
    sent_ref[...] = total.astype(BF16)


def middle_kernel(pos_ref, w_in_ref, sib_ref, part_ref, part_sib_ref, pgact_ref, *outs):
    c = pos_ref[1]
    passed = part_sib_ref[...]
    both = part_ref[...] + joined(passed[:, HID:], passed[:, :HID]).astype(F32)
    act_grad = jnp.concatenate([both[CAP:], both[:CAP]], axis=0)
    act, pullback = jax.vjp(lambda v: jax.nn.gelu(v, approximate=True), both)
    pre_grad = pullback(act_grad)[0]
    act = jnp.concatenate([act[ROWS - CAP:], act[:ROWS - CAP]], axis=0)
    row = lax.broadcasted_iota(jnp.int32, (EXPERTS, MSG, NC * HID), 1).reshape(ROWS, NC * HID)
    pre_grad = jnp.where(row < CAP, pre_grad, 0.0).astype(BF16)
    act = jnp.where(row < CAP, 0.0, act).astype(BF16)
    pgact_ref[...] = joined(pre_grad, act)
    block = lax.broadcasted_iota(jnp.int32, (EXPERTS, CAP, ROWS), 0).reshape(KEPT, ROWS)
    within = lax.broadcasted_iota(jnp.int32, (EXPERTS, CAP, ROWS), 1).reshape(KEPT, ROWS)
    keep = (lax.broadcasted_iota(jnp.int32, (KEPT, ROWS), 1) == block * MSG + within).astype(BF16)
    pg = jnp.dot(keep, pre_grad, preferred_element_type=F32).astype(BF16)
    for at, out_ref in zip(places(pos_ref[0], c), outs):
        for zl in range(0, NZ, 2):
            w = jnp.concatenate([weights_in(w_in_ref, sib_ref, c, at * NZ + z) for z in (zl, zl + 1)], axis=0)
            out = lax.dot_general(pg, w, CONTRACT_LAST, preferred_element_type=F32).astype(BF16)
            for j in range(2):
                out_ref[zl + j] = out[:, j * COLS:(j + 1) * COLS]


def relay_kernel(mine_ref, passed_ref, out_ref):
    out_ref[...] = (mine_ref[...].astype(F32) + passed_ref[...].astype(F32)).astype(BF16)


def total_kernel(mine_ref, first_ref, second_ref, out_ref):
    for zl in range(NZ):
        total = mine_ref[zl].astype(F32) + first_ref[zl].astype(F32) + second_ref[zl].astype(F32)
        out_ref[zl * EXPERTS:(zl + 1) * EXPERTS] = total.reshape(EXPERTS, CAP, COLS).astype(BF16)


def grads_kernel(pos_ref, pgact_ref, *refs):
    xs, (in_mine, out_mine, in_other, out_other) = refs[:7], refs[8:]
    left = pgact_ref[...].T
    xs = [whole(xs[0])] + [halves(*xs[i:i + 2]) for i in (1, 3, 5)]
    for y, blocks in zip(places(pos_ref[0], pos_ref[1]), xs):
        at = y * NZ
        for zl in range(0, NZ, 2):
            x = joined(chunk(*blocks[zl]), chunk(*blocks[zl + 1]))
            both = jnp.dot(left, x, preferred_element_type=F32).astype(BF16)
            for ref, first in ((in_mine, 0), (in_other, HID)):
                turned = both[first:first + HID].T
                ref[at + zl] = turned[:COLS]
                ref[at + zl + 1] = turned[COLS:]
            lanes = pl.ds(pl.multiple_of((at + zl) * COLS, 2 * COLS), 2 * COLS)
            out_mine[:, lanes] = both[2 * HID:3 * HID]
            for j in range(2):
                out_other[at + zl + j] = both[3 * HID:, j * COLS:(j + 1) * COLS]


def merge_kernel(pos_ref, in_mine, out_mine, in_sib, out_sib, w_in_grad_ref, w_out_grad_ref):
    c = pos_ref[1]
    blocks = NY * NZ
    for k in range(blocks):
        mine = pl.ds(pl.multiple_of((k * NC + c) * COLS, COLS), COLS)
        other = pl.ds(pl.multiple_of((k * NC + 1 - c) * COLS, COLS), COLS)
        w_in_grad_ref[mine, :] = in_mine[k]
        w_in_grad_ref[other, :] = in_sib[k]
        w_out_grad_ref[:, mine] = out_mine[:, k * COLS:(k + 1) * COLS]
        w_out_grad_ref[:, other] = out_sib[k]


def combine_kernel(table_ref, back_ref, out_ref):
    total = back_ref[0:EXPERTS].astype(F32)
    for z in range(1, NZ):
        total = total + back_ref[z * EXPERTS:(z + 1) * EXPERTS].astype(F32)
    rows = total.reshape(KEPT, COLS).astype(BF16)
    out_ref[...] = lax.dot_general(table_ref[...], rows, CONTRACT_FIRST, preferred_element_type=F32).astype(BF16)


SMEM = pl.BlockSpec(memory_space=pltpu.SMEM)
WHOLE = pl.BlockSpec(memory_space=pltpu.VMEM)
UNREAD = pl.BlockSpec(memory_space=pl.ANY)


def shape(*dims, kind=BF16):
    return jax.ShapeDtypeStruct(dims, kind)


def held(*dims, kind=BF16):
    return pltpu.VMEM(dims, kind)


def keep(value):
    return pltpu.with_memory_space_constraint(value, pltpu.VMEM)


def far(value):
    return pltpu.with_memory_space_constraint(value, pltpu.HBM)


def run(kernel, outs, scalars, *args, unread=0, scratch=()):
    specs = [SMEM] * scalars + [WHOLE] * (len(args) - scalars - unread) + [UNREAD] * unread
    out_specs = jax.tree.map(lambda _: WHOLE, outs)
    return pl.pallas_call(
        kernel, out_shape=outs, in_specs=specs, out_specs=out_specs, scratch_shapes=scratch, compiler_params=VMEM
    )(*args)


def partner(value, which):
    near, far = [i ^ 1 for i in range(NY)], [NY - 1 - i for i in range(NY)]
    to = [(near, far), (far, near)]
    return lax.ppermute(value, ("y", "c"), [(i * NC + c, to[c][which][i] * NC + c) for i in range(NY) for c in range(NC)])


def across(value):
    return lax.ppermute(value, "c", [(0, 1), (1, 0)])


def on_device(tokens, out_grad, expert_ids, gate_weights, w_in, w_out):
    pos = jnp.stack([lax.axis_index("y"), lax.axis_index("c")]).astype(jnp.int32)
    ids, gate = far(expert_ids.T), far(gate_weights.T)
    w_in, w_out = w_in[0], w_out[0]
    blocks = NY * NZ
    half_in, half_out = held(blocks, COLS, HID), held(HID, blocks * COLS)
    send = run(dispatch_kernel, shape(EXPERTS, MSG, COLS), 0, ids, gate, far(tokens), far(out_grad))
    in_other, out_other = run(
        split_kernel, (half_in, half_in), 1, pos, far(w_in.reshape(blocks, NC, COLS, HID)), far(w_out), send,
        unread=3, scratch=[pltpu.SemaphoreType.DMA((blocks + 1,))],
    )
    in_sib, out_sib = across(in_other), across(out_other)
    received = lax.all_to_all(send, ("zh", "x"), 0, 0, tiled=True)
    received, in_sib, out_sib = lax.optimization_barrier((received, in_sib, out_sib))
    own = lax.all_gather(received, "zl", axis=0, tiled=True)
    weights = (pos, w_in, w_out, keep(in_sib), keep(out_sib))
    cut = NZ // 2 * EXPERTS
    low, high = own[:cut], own[cut:]
    first_a, second_b = partner(low, 0), partner(high, 1)
    first_b, second_a = partner(high, 0), partner(low, 1)
    last_a, last_b = partner(first_a, 1), partner(second_b, 0)
    xs = [keep(x) for x in (own, first_a, first_b, second_a, second_b, last_a, last_b)]
    part = held(ROWS, NC * HID, kind=F32)
    some = run(forward_first_kernel, part, 1, *weights, *xs[:3])
    more = run(forward_second_kernel, part, 1, *weights, *xs[3:5], keep(some))
    mine, sent = run(
        forward_last_kernel, (part, held(ROWS, NC * HID)), 1, *weights, *xs[5:], keep(more)
    )
    rows = held(NZ, KEPT, COLS)
    pgact, to_own, to_first, to_second, to_last = run(
        middle_kernel,
        (pltpu.HBM((ROWS, 2 * NC * HID), BF16), rows, rows, rows, rows),
        1, pos, w_in, keep(in_sib), keep(mine), keep(across(sent)),
    )
    passed, from_second = partner(to_last, 1), partner(to_second, 1)
    from_first = partner(run(relay_kernel, rows, 0, keep(to_first), keep(passed)), 0)
    summed = run(total_kernel, held(NZ * EXPERTS, CAP, COLS), 0, keep(to_own), keep(from_first), keep(from_second))
    table = run(table_kernel, held(KEPT, TOK), 0, ids, summed, unread=1)
    back = lax.all_to_all(summed, ("zl", "zh", "x"), 0, 0, tiled=True)
    tokens_grad = run(combine_kernel, shape(TOK, COLS), 0, keep(table), keep(back))
    in_mine, out_mine, in_other, out_other = run(
        grads_kernel, (half_in, half_out, half_in, half_in), 1, pos, pgact, *xs, summed, unread=1
    )
    w_in_grad, w_out_grad = run(
        merge_kernel, (shape(*w_in.shape), shape(*w_out.shape)),
        1, pos, keep(in_mine), keep(out_mine), keep(across(in_other)), keep(across(out_other)),
    )
    return tokens_grad, w_in_grad[None], w_out_grad[None]


def solution(mesh):
    fine = Mesh(mesh.devices.reshape(NY, NZ, NC, NH, NX), ("y", "zl", "c", "zh", "x"))
    dp, expert = ("y", "zl", "c"), ("zh", "x")
    placed = (
        P(expert, dp),
        P(expert, dp),
        P(expert, None),
        P(expert, None),
        P(expert, None, dp),
        P(expert, dp, None),
    )
    return jax.shard_map(
        on_device,
        mesh=fine,
        in_specs=placed,
        out_specs=(P(expert, dp), P(expert, None, dp), P(expert, dp, None)),
        check_vma=False,
    )
```

time: 159 us -> 145 us (0.912)
  blocking collectives: 36.7 us -> 15.1 us
  starting transfers between devices: 49.9 us -> 62.9 us
  waiting for transfers between devices: 47.1 us -> 44.5 us
  other arithmetic: 2.16 us -> 0.08 us
    all_to_all x1 -> x0, blocking collectives: 21.6 us -> none  [on_device(): parts = lax.all_to_all(partial_rows, 'y', 0, 0, tiled=True)]
    ppermute x6 -> x9, starting transfers between devices: 15.3 us -> 27.4 us  [partner(): lax.ppermute(value, ('y', 'c'), [(i * NC + c, to[c][which][i] * NC + c) f...]
    ppermute x6 -> x9, waiting for transfers between devices: 16.2 us -> 15.5 us  [partner(): lax.ppermute(value, ('y', 'c'), [(i * NC + c, to[c][which][i] * NC + c) f...]
    pallas_call x8 -> x12, Pallas kernels: 17.4 us -> 17.2 us  [run(): pl.pallas_call(kernel, out_shape=outs, in_specs=specs, out_specs=out_spec...]
  transfers between devices with their start and end apart: 13 -> 16, of which waited for: 11 -> 12; matrix products, arithmetic and copies ran while one was open for 0% -> 0% of each run, Pallas kernels for 6% -> 7%
where the time goes in v3:
time: 145 us; the launch traced here: 144 us
  starting transfers between devices  62.9 us (43%)
  waiting for transfers between devices  44.5 us (31%)
  Pallas kernels  17.2 us (12%)
  blocking collectives  15.1 us (10%)
  local copies, waits for them, and re-layouts  3.15 us (2%)
    ppermute x9, starting transfers between devices, partner(): lax.ppermute(value, ('y', 'c'), [(i * NC + c, to[c][which][i] * NC + c) f...  27.4 us
    pallas_call x12, Pallas kernels, run(): pl.pallas_call(kernel, out_shape=outs, in_specs=specs, out_specs=out_spec...  17.2 us
    all_to_all x1, starting transfers between devices, on_device(): received = lax.all_to_all(send, ('zh', 'x'), 0, 0, tiled=True)  16.8 us
    ppermute x9, waiting for transfers between devices, partner(): lax.ppermute(value, ('y', 'c'), [(i * NC + c, to[c][which][i] * NC + c) f...  15.5 us
    all_gather x1, blocking collectives, on_device(): own = lax.all_gather(received, 'zl', axis=0, tiled=True)  15.1 us
    all_to_all x1, waiting for transfers between devices, on_device(): back = lax.all_to_all(summed, ('zl', 'zh', 'x'), 0, 0, tiled=True)  14.9 us
    ppermute x5, starting transfers between devices, across(): return lax.ppermute(value, 'c', [(0, 1), (1, 0)])  10.7 us
    all_to_all x1, waiting for transfers between devices, on_device(): received = lax.all_to_all(send, ('zh', 'x'), 0, 0, tiled=True)  10.5 us
  transfers between devices with their start and end apart: 16, of which 12 were waited for; matrix products, arithmetic and copies ran while one was open for 0% of the time, Pallas kernels for 7%

profile of v3, /device:TPU:32, one launch (start us, length us, event | category | flops | bytes accessed | tf_op | source)
XLA Modules:
  0.0 143.9 jit_solution(8231846173715269122)
XLA Ops:
  0.6 2.0 %shard_map.85.after_ref = bf16[16,40,128]{2,1,0:T(8,128)(2,1)} custom-call(s32[2,128]{1,0:T(2,128)} %bitcast.18, f32[2,128]{1,0:T(2,128)} %bitcast.20, bf16[128,128]{1,0:T(8,128)(2,1)} %tok_ref.1, bf16[128,128]{1,0:T(8,128)(2,1)} %dy_ref.1), custom_call_target="tpu_custom_call" | custom-call | tf_op jit(solution)/shard_map/pallas_call | solution.py:229
  2.6 16.8 %all-to-all-start = ((bf16[16,40,128]{2,1,0:T(8,128)(2,1)}), bf16[16,40,128]{2,1,0:T(8,128)(2,1)S(1)}, u32[]{:S(2)}, u32[]{:S(2)}) async-start(bf16[16,40,128]{2,1,0:T(8,128)(2,1)} %shard_map.85.after_ref), calls=%async_computation | async-start | bytes 327680 | tf_op jit(solution)/shard_map/all_to_all | solution.py:256
  19.4 0.1 pad_add_fusion.pos_ref
  19.4 1.8 %shard_map.86 = (bf16[16,128,128]{2,1,0:T(8,128)(2,1)S(1)}, bf16[16,128,128]{2,1,0:T(8,128)(2,1)S(1)}) custom-call(s32[2]{0:T(128)S(1)} %pad_add_fusion.pos_ref, bf16[16,2,128,128]{3,2,1,0:T(8,128)(2,1)} %bitcast.9, bf16[128,4096]{1,0:T(8,128)(2,1)} %bitcast.14, bf16[16,40,128]{2,1,0:T(8,128)(2,1)} %shard_map.85.after_ref), custom_call_target="tpu_custom_call" | custom-call | tf_op jit(solution)/shard_map/pallas_call | solution.py:229
  21.3 1.9 %collective-permute-start = (bf16[16,128,128]{2,1,0:T(8,128)(2,1)S(1)}, bf16[16,128,128]{2,1,0:T(8,128)(2,1)S(1)}, u32[]{:S(2)}, u32[]{:S(2)}) collective-permute-start(bf16[16,128,128]{2,1,0:T(8,128)(2,1)S(1)} %get-tuple-element.21), channel_id=1, source_target_pairs={{0,16},{16,0},{1,17},{17,1},{2,18},{18,2},{3,19},{19,3},{4,20},{20... | collective-permute-start | bytes 1572872 | tf_op jit(solution)/shard_map/ppermute | solution.py:241
  23.2 0.0 copy-start
  23.2 0.0 copy-start.1
  23.2 2.5 %collective-permute-start.1 = (bf16[16,128,128]{2,1,0:T(8,128)(2,1)S(1)}, bf16[16,128,128]{2,1,0:T(8,128)(2,1)S(1)}, u32[]{:S(2)}, u32[]{:S(2)}) collective-permute-start(bf16[16,128,128]{2,1,0:T(8,128)(2,1)S(1)} %get-tuple-element.22), channel_id=1, source_target_pairs={{0,16},{16,0},{1,17},{17,1},{2,18},{18,2},{3,19},{19,3},{4,20},{20... | collective-permute-start | bytes 1572872 | tf_op jit(solution)/shard_map/ppermute | solution.py:241
  25.8 1.5 %collective-permute-done.1.wos = bf16[16,128,128]{2,1,0:T(8,128)(2,1)S(1)} collective-permute-done((bf16[16,128,128]{2,1,0:T(8,128)(2,1)S(1)}, bf16[16,128,128]{2,1,0:T(8,128)(2,1)S(1)}, u32[]{:S(2)}, u32[]{:S(2)}) %collective-permute-start.1) | collective-permute-done | bytes 524320 | tf_op jit(solution)/shard_map/ppermute | solution.py:241
  27.3 0.8 copy-done.2
  28.1 10.5 %all-to-all-done = bf16[16,40,128]{2,1,0:T(8,128)(2,1)S(1)} async-done(((bf16[16,40,128]{2,1,0:T(8,128)(2,1)}), bf16[16,40,128]{2,1,0:T(8,128)(2,1)S(1)}, u32[]{:S(2)}, u32[]{:S(2)}) %all-to-all-start) | async-done | bytes 163872 | tf_op jit(solution)/shard_map/all_to_all | solution.py:256
  38.6 15.1 %all_gather.3.own.refs_0_ = bf16[64,40,128]{2,1,0:T(8,128)(2,1)S(1)} all-gather(bf16[16,40,128]{2,1,0:T(8,128)(2,1)S(1)} %all-to-all-done), channel_id=1, replica_groups=mesh['y'=4,'zl'=4,'c'=2,'zh'=4,'x'=4] {'zl'}, dimensions={0}, use_global_device_ids=true | all-gather | bytes 819200 | tf_op jit(solution)/shard_map/all_gather | solution.py:258
  53.7 0.1 fusion
  53.7 4.9 %collective-permute-start.4 = (bf16[32,40,128]{2,1,0:T(8,128)(2,1)S(1)}, bf16[32,40,128]{2,1,0:T(8,128)(2,1)S(1)}, u32[]{:S(2)}, u32[]{:S(2)}) collective-permute-start(bf16[32,40,128]{2,1,0:T(8,128)(2,1)S(1)} %get-tuple-element.39), channel_id=1, source_target_pairs={{0,384},{16,144},{128,256},{144,16},{256,128},{272,400},{384,0},{4... | collective-permute-start | bytes 983048 | tf_op jit(solution)/shard_map/ppermute | solution.py:237
  58.6 2.0 %collective-permute-start.2 = (bf16[32,40,128]{2,1,0:T(8,128)(2,1)S(1)}, bf16[32,40,128]{2,1,0:T(8,128)(2,1)S(1)}, u32[]{:S(2)}, u32[]{:S(2)}) collective-permute-start(bf16[32,40,128]{2,1,0:T(8,128)(2,1)S(1)} %get-tuple-element.40), channel_id=1, source_target_pairs={{0,128},{16,400},{128,0},{144,272},{256,384},{272,144},{384,256},{... | collective-permute-start | bytes 983048 | tf_op jit(solution)/shard_map/ppermute | solution.py:237
  60.7 3.8 %collective-permute-start.7 = (bf16[32,40,128]{2,1,0:T(8,128)(2,1)S(1)}, bf16[32,40,128]{2,1,0:T(8,128)(2,1)S(1)}, u32[]{:S(2)}, u32[]{:S(2)}) collective-permute-start(bf16[32,40,128]{2,1,0:T(8,128)(2,1)S(1)} %get-tuple-element.39), channel_id=1, source_target_pairs={{0,128},{16,400},{128,0},{144,272},{256,384},{272,144},{384,256},{... | collective-permute-start | bytes 983048 | tf_op jit(solution)/shard_map/ppermute | solution.py:237
  64.5 2.1 %collective-permute-start.6 = (bf16[32,40,128]{2,1,0:T(8,128)(2,1)S(1)}, bf16[32,40,128]{2,1,0:T(8,128)(2,1)S(1)}, u32[]{:S(2)}, u32[]{:S(2)}) collective-permute-start(bf16[32,40,128]{2,1,0:T(8,128)(2,1)S(1)} %get-tuple-element.40), channel_id=1, source_target_pairs={{0,384},{16,144},{128,256},{144,16},{256,128},{272,400},{384,0},{4... | collective-permute-start | bytes 983048 | tf_op jit(solution)/shard_map/ppermute | solution.py:237
  66.6 0.8 collective-permute-done.4.second_b.refs_4_
  67.5 2.3 %collective-permute-start.5 = (bf16[32,40,128]{2,1,0:T(8,128)(2,1)S(1)}, bf16[32,40,128]{2,1,0:T(8,128)(2,1)S(1)}, u32[]{:S(2)}, u32[]{:S(2)}) collective-permute-start(bf16[32,40,128]{2,1,0:T(8,128)(2,1)S(1)} %collective-permute-done.4.second_b.refs_4_), channel_id=1, source_target_pairs={{0,128},{16,400},{128,0},{144,272},{256,384},{272,144},{384,256},{... | collective-permute-start | bytes 983048 | tf_op jit(solution)/shard_map/ppermute | solution.py:237
  69.7 1.3 collective-permute-done.2.first_a.refs_1_
  71.1 3.3 %collective-permute-start.3 = (bf16[32,40,128]{2,1,0:T(8,128)(2,1)S(1)}, bf16[32,40,128]{2,1,0:T(8,128)(2,1)S(1)}, u32[]{:S(2)}, u32[]{:S(2)}) collective-permute-start(bf16[32,40,128]{2,1,0:T(8,128)(2,1)S(1)} %collective-permute-done.2.first_a.refs_1_), channel_id=1, source_target_pairs={{0,384},{16,144},{128,256},{144,16},{256,128},{272,400},{384,0},{4... | collective-permute-start | bytes 983048 | tf_op jit(solution)/shard_map/ppermute | solution.py:237
  74.3 3.1 %collective-permute-done.7.first_b.refs_2_ = bf16[32,40,128]{2,1,0:T(8,128)(2,1)S(1)} collective-permute-done((bf16[32,40,128]{2,1,0:T(8,128)(2,1)S(1)}, bf16[32,40,128]{2,1,0:T(8,128)(2,1)S(1)}, u32[]{:S(2)}, u32[]{:S(2)}) %collective-permute-start.7) | collective-permute-done | bytes 327712 | tf_op jit(solution)/shard_map/ppermute | solution.py:237
  77.4 1.2 copy-done.3
  78.6 1.4 shard_map.87.before_ref
  80.1 1.1 shard_map.88.before_ref
  81.2 0.1 collective-permute-done.3.last_a.refs_5_
  81.2 1.1 shard_map.89
  82.3 1.9 %collective-permute-start.8 = (bf16[640,256]{1,0:T(8,128)(2,1)S(1)}, bf16[640,256]{1,0:T(8,128)(2,1)S(1)}, u32[]{:S(2)}, u32[]{:S(2)}) collective-permute-start(bf16[640,256]{1,0:T(8,128)(2,1)S(1)} %get-tuple-element.27), channel_id=1, source_target_pairs={{0,16},{16,0},{1,17},{17,1},{2,18},{18,2},{3,19},{19,3},{4,20},{20... | collective-permute-start | bytes 983048 | tf_op jit(solution)/shard_map/ppermute | solution.py:241
  84.3 1.6 %collective-permute-done.8.part_sib_ref = bf16[640,256]{1,0:T(8,128)(2,1)S(1)} collective-permute-done((bf16[640,256]{1,0:T(8,128)(2,1)S(1)}, bf16[640,256]{1,0:T(8,128)(2,1)S(1)}, u32[]{:S(2)}, u32[]{:S(2)}) %collective-permute-start.8) | collective-permute-done | bytes 327712 | tf_op jit(solution)/shard_map/ppermute | solution.py:241
  85.9 2.5 %shard_map.90 = (bf16[640,512]{1,0:T(8,128)(2,1)}, bf16[4,320,128]{2,1,0:T(8,128)(2,1)S(1)}, bf16[4,320,128]{2,1,0:T(8,128)(2,1)S(1)}, bf16[4,320,128]{2,1,0:T(8,128)(2,1)S(1)}, bf16[4,320,128]{2,1,0:T(8,128)(2,1)S(1)}) custom-call(s32[2]{0:T(128)S(1)} %pad_add_fusion.pos_ref, bf16[4096,128]{1,0:T(8,128)(2,1)S(1)} %bitcast.13, ...), custom_call_target="tpu_custom_call" | custom-call | tf_op jit(solution)/shard_map/pallas_call | solution.py:229
  88.4 3.3 %collective-permute-start.9 = (bf16[4,320,128]{2,1,0:T(8,128)(2,1)S(1)}, bf16[4,320,128]{2,1,0:T(8,128)(2,1)S(1)}, u32[]{:S(2)}, u32[]{:S(2)}) collective-permute-start(bf16[4,320,128]{2,1,0:T(8,128)(2,1)S(1)} %get-tuple-element.30), channel_id=1, source_target_pairs={{0,384},{16,144},{128,256},{144,16},{256,128},{272,400},{384,0},{4... | collective-permute-start | bytes 983048 | tf_op jit(solution)/shard_map/ppermute | solution.py:237
  91.6 3.8 %collective-permute-start.11 = (bf16[4,320,128]{2,1,0:T(8,128)(2,1)S(1)}, bf16[4,320,128]{2,1,0:T(8,128)(2,1)S(1)}, u32[]{:S(2)}, u32[]{:S(2)}) collective-permute-start(bf16[4,320,128]{2,1,0:T(8,128)(2,1)S(1)} %get-tuple-element.31), channel_id=1, source_target_pairs={{0,384},{16,144},{128,256},{144,16},{256,128},{272,400},{384,0},{4... | collective-permute-start | bytes 983048 | tf_op jit(solution)/shard_map/ppermute | solution.py:237
  95.4 3.1 %collective-permute-done.9.passed_ref = bf16[4,320,128]{2,1,0:T(8,128)(2,1)S(1)} collective-permute-done((bf16[4,320,128]{2,1,0:T(8,128)(2,1)S(1)}, bf16[4,320,128]{2,1,0:T(8,128)(2,1)S(1)}, u32[]{:S(2)}, u32[]{:S(2)}) %collective-permute-start.9) | collective-permute-done | bytes 327712 | tf_op jit(solution)/shard_map/ppermute | solution.py:237
  98.5 0.1 shard_map.91
  98.6 1.9 %collective-permute-start.10 = (bf16[4,320,128]{2,1,0:T(8,128)(2,1)S(1)}, bf16[4,320,128]{2,1,0:T(8,128)(2,1)S(1)}, u32[]{:S(2)}, u32[]{:S(2)}) collective-permute-start(bf16[4,320,128]{2,1,0:T(8,128)(2,1)S(1)} %shard_map.91), channel_id=1, source_target_pairs={{0,128},{16,400},{128,0},{144,272},{256,384},{272,144},{384,256},{... | collective-permute-start | bytes 983048 | tf_op jit(solution)/shard_map/ppermute | solution.py:237
  100.5 1.5 %collective-permute-done.11.second_ref = bf16[4,320,128]{2,1,0:T(8,128)(2,1)S(1)} collective-permute-done((bf16[4,320,128]{2,1,0:T(8,128)(2,1)S(1)}, bf16[4,320,128]{2,1,0:T(8,128)(2,1)S(1)}, u32[]{:S(2)}, u32[]{:S(2)}) %collective-permute-start.11) | collective-permute-done | bytes 327712 | tf_op jit(solution)/shard_map/ppermute | solution.py:237
  102.0 5.5 %collective-permute-done.10.first_ref = bf16[4,320,128]{2,1,0:T(8,128)(2,1)S(1)} collective-permute-done((bf16[4,320,128]{2,1,0:T(8,128)(2,1)S(1)}, bf16[4,320,128]{2,1,0:T(8,128)(2,1)S(1)}, u32[]{:S(2)}, u32[]{:S(2)}) %collective-permute-start.10) | collective-permute-done | bytes 327712 | tf_op jit(solution)/shard_map/ppermute | solution.py:237
  107.6 0.9 shard_map.92.after_ref.refs_7_
  108.5 8.0 %all-to-all-start.1 = ((bf16[64,20,128]{2,1,0:T(8,128)(2,1)}), bf16[64,20,128]{2,1,0:T(8,128)(2,1)S(1)}, u32[]{:S(2)}, u32[]{:S(2)}) async-start(bf16[64,20,128]{2,1,0:T(8,128)(2,1)} %shard_map.92.after_ref.refs_7_), calls=%async_computation.1 | async-start | bytes 786432 | tf_op jit(solution)/shard_map/all_to_all | solution.py:282
  116.6 1.1 copy-done.16
  117.7 2.4 %shard_map.95 = (bf16[16,128,128]{2,1,0:T(8,128)(2,1)S(1)}, bf16[128,2048]{1,0:T(8,128)(2,1)S(1)}, bf16[16,128,128]{2,1,0:T(8,128)(2,1)S(1)}, bf16[16,128,128]{2,1,0:T(8,128)(2,1)S(1)}) custom-call(s32[2]{0:T(128)S(1)} %pad_add_fusion.pos_ref, bf16[640,512]{1,0:T(8,128)(2,1)S(1)} %copy-done.16, bf16[64,40,128]{2,1,0:T(8,128)(2,1)S(1)} %all_gather.3.own.refs_0_, ...), custom_call_target="tpu_custom_call" | custom-call | tf_op jit(solution)/shard_map/pallas_call | solution.py:229
  120.1 1.9 %collective-permute-start.12 = (bf16[16,128,128]{2,1,0:T(8,128)(2,1)S(1)}, bf16[16,128,128]{2,1,0:T(8,128)(2,1)S(1)}, u32[]{:S(2)}, u32[]{:S(2)}) collective-permute-start(bf16[16,128,128]{2,1,0:T(8,128)(2,1)S(1)} %get-tuple-element.35), channel_id=1, source_target_pairs={{0,16},{16,0},{1,17},{17,1},{2,18},{18,2},{3,19},{19,3},{4,20},{20... | collective-permute-start | bytes 1572872 | tf_op jit(solution)/shard_map/ppermute | solution.py:241
  122.0 2.4 %collective-permute-start.13 = (bf16[16,128,128]{2,1,0:T(8,128)(2,1)S(1)}, bf16[16,128,128]{2,1,0:T(8,128)(2,1)S(1)}, u32[]{:S(2)}, u32[]{:S(2)}) collective-permute-start(bf16[16,128,128]{2,1,0:T(8,128)(2,1)S(1)} %get-tuple-element.36), channel_id=1, source_target_pairs={{0,16},{16,0},{1,17},{17,1},{2,18},{18,2},{3,19},{19,3},{4,20},{20... | collective-permute-start | bytes 1572872 | tf_op jit(solution)/shard_map/ppermute | solution.py:241
  124.4 1.0 shard_map.93.table_ref
  125.4 0.5 collective-permute-done.13.out_sib
  126.0 2.2 %shard_map.96 = (bf16[4096,128]{1,0:T(8,128)(2,1)}, bf16[128,4096]{1,0:T(8,128)(2,1)}) custom-call(s32[2]{0:T(128)S(1)} %pad_add_fusion.pos_ref, bf16[16,128,128]{2,1,0:T(8,128)(2,1)S(1)} %get-tuple-element.33.in_mine, bf16[128,2048]{1,0:T(8,128)(2,1)S(1)} %get-tuple-element.34.out_mine, bf16[16,128,128]{2,1,0:T(8,128)(2,1)S(1)} %collective-permute-done.12.in_sib, ...), custom_call_target="tpu_custom_call" | custom-call | tf_op jit(solution)/shard_map/pallas_call | solution.py:229
  128.2 14.9 %all-to-all-done.1.back_ref = bf16[64,20,128]{2,1,0:T(8,128)(2,1)S(1)} async-done(((bf16[64,20,128]{2,1,0:T(8,128)(2,1)}), bf16[64,20,128]{2,1,0:T(8,128)(2,1)S(1)}, u32[]{:S(2)}, u32[]{:S(2)}) %all-to-all-start.1) | async-done | bytes 327712 | tf_op jit(solution)/shard_map/all_to_all | solution.py:282
  143.1 0.8 shard_map.94
  (33 shorter events, 0.1 us)
Async XLA Ops:
  2.6 36.0 %all-to-all-start = ((bf16[16,40,128]{2,1,0:T(8,128)(2,1)}), bf16[16,40,128]{2,1,0:T(8,128)(2,1)S(1)}, u32[]{:S(2)}, u32[]{:S(2)}) async-start(bf16[16,40,128]{2,1,0:T(8,128)(2,1)} %shard_map.85.after_ref), calls=%async_computation | async-start | bytes 327680 | tf_op jit(solution)/shard_map/all_to_all | solution.py:256
  21.3 4.5 %collective-permute-start = (bf16[16,128,128]{2,1,0:T(8,128)(2,1)S(1)}, bf16[16,128,128]{2,1,0:T(8,128)(2,1)S(1)}, u32[]{:S(2)}, u32[]{:S(2)}) collective-permute-start(bf16[16,128,128]{2,1,0:T(8,128)(2,1)S(1)} %get-tuple-element.21), channel_id=1, source_target_pairs={{0,16},{16,0},{1,17},{17,1},{2,18},{18,2},{3,19},{19,3},{4,20},{20... | collective-permute-start | bytes 1572872 | tf_op jit(solution)/shard_map/ppermute | solution.py:241
  23.2 54.2 %copy-start = (bf16[1,4096,128]{2,1,0:T(8,128)(2,1)S(1)}, bf16[1,4096,128]{2,1,0:T(8,128)(2,1)}, u32[]{:S(2)}) copy-start(bf16[1,4096,128]{2,1,0:T(8,128)(2,1)} %param.10) | copy-start | bytes 3145732
  23.2 54.2 %copy-start.1 = (bf16[1,128,4096]{2,1,0:T(8,128)(2,1)S(1)}, bf16[1,128,4096]{2,1,0:T(8,128)(2,1)}, u32[]{:S(2)}) copy-start(bf16[1,128,4096]{2,1,0:T(8,128)(2,1)} %param.11) | copy-start | bytes 3145732
  23.2 4.1 %collective-permute-start.1 = (bf16[16,128,128]{2,1,0:T(8,128)(2,1)S(1)}, bf16[16,128,128]{2,1,0:T(8,128)(2,1)S(1)}, u32[]{:S(2)}, u32[]{:S(2)}) collective-permute-start(bf16[16,128,128]{2,1,0:T(8,128)(2,1)S(1)} %get-tuple-element.22), channel_id=1, source_target_pairs={{0,16},{16,0},{1,17},{17,1},{2,18},{18,2},{3,19},{19,3},{4,20},{20... | collective-permute-start | bytes 1572872 | tf_op jit(solution)/shard_map/ppermute | solution.py:241
  27.3 0.8 copy-start.2
  53.7 13.8 %collective-permute-start.4 = (bf16[32,40,128]{2,1,0:T(8,128)(2,1)S(1)}, bf16[32,40,128]{2,1,0:T(8,128)(2,1)S(1)}, u32[]{:S(2)}, u32[]{:S(2)}) collective-permute-start(bf16[32,40,128]{2,1,0:T(8,128)(2,1)S(1)} %get-tuple-element.39), channel_id=1, source_target_pairs={{0,384},{16,144},{128,256},{144,16},{256,128},{272,400},{384,0},{4... | collective-permute-start | bytes 983048 | tf_op jit(solution)/shard_map/ppermute | solution.py:237
  58.6 12.4 %collective-permute-start.2 = (bf16[32,40,128]{2,1,0:T(8,128)(2,1)S(1)}, bf16[32,40,128]{2,1,0:T(8,128)(2,1)S(1)}, u32[]{:S(2)}, u32[]{:S(2)}) collective-permute-start(bf16[32,40,128]{2,1,0:T(8,128)(2,1)S(1)} %get-tuple-element.40), channel_id=1, source_target_pairs={{0,128},{16,400},{128,0},{144,272},{256,384},{272,144},{384,256},{... | collective-permute-start | bytes 983048 | tf_op jit(solution)/shard_map/ppermute | solution.py:237
  60.7 16.7 %collective-permute-start.7 = (bf16[32,40,128]{2,1,0:T(8,128)(2,1)S(1)}, bf16[32,40,128]{2,1,0:T(8,128)(2,1)S(1)}, u32[]{:S(2)}, u32[]{:S(2)}) collective-permute-start(bf16[32,40,128]{2,1,0:T(8,128)(2,1)S(1)} %get-tuple-element.39), channel_id=1, source_target_pairs={{0,128},{16,400},{128,0},{144,272},{256,384},{272,144},{384,256},{... | collective-permute-start | bytes 983048 | tf_op jit(solution)/shard_map/ppermute | solution.py:237
  64.5 15.5 %collective-permute-start.6 = (bf16[32,40,128]{2,1,0:T(8,128)(2,1)S(1)}, bf16[32,40,128]{2,1,0:T(8,128)(2,1)S(1)}, u32[]{:S(2)}, u32[]{:S(2)}) collective-permute-start(bf16[32,40,128]{2,1,0:T(8,128)(2,1)S(1)} %get-tuple-element.40), channel_id=1, source_target_pairs={{0,384},{16,144},{128,256},{144,16},{256,128},{272,400},{384,0},{4... | collective-permute-start | bytes 983048 | tf_op jit(solution)/shard_map/ppermute | solution.py:237
  67.5 12.6 %copy-start.8 = (bf16[32,40,128]{2,1,0:T(8,128)(2,1)}, bf16[32,40,128]{2,1,0:T(8,128)(2,1)S(1)}, u32[]{:S(2)}) copy-start(bf16[32,40,128]{2,1,0:T(8,128)(2,1)S(1)} %collective-permute-done.4.second_b.refs_4_) | copy-start | bytes 983044
  67.5 13.7 %collective-permute-start.5 = (bf16[32,40,128]{2,1,0:T(8,128)(2,1)S(1)}, bf16[32,40,128]{2,1,0:T(8,128)(2,1)S(1)}, u32[]{:S(2)}, u32[]{:S(2)}) collective-permute-start(bf16[32,40,128]{2,1,0:T(8,128)(2,1)S(1)} %collective-permute-done.4.second_b.refs_4_), channel_id=1, source_target_pairs={{0,128},{16,400},{128,0},{144,272},{256,384},{272,144},{384,256},{... | collective-permute-start | bytes 983048 | tf_op jit(solution)/shard_map/ppermute | solution.py:237
  71.1 8.9 %copy-start.10 = (bf16[32,40,128]{2,1,0:T(8,128)(2,1)}, bf16[32,40,128]{2,1,0:T(8,128)(2,1)S(1)}, u32[]{:S(2)}) copy-start(bf16[32,40,128]{2,1,0:T(8,128)(2,1)S(1)} %collective-permute-done.2.first_a.refs_1_) | copy-start | bytes 983044
  71.1 10.2 %collective-permute-start.3 = (bf16[32,40,128]{2,1,0:T(8,128)(2,1)S(1)}, bf16[32,40,128]{2,1,0:T(8,128)(2,1)S(1)}, u32[]{:S(2)}, u32[]{:S(2)}) collective-permute-start(bf16[32,40,128]{2,1,0:T(8,128)(2,1)S(1)} %collective-permute-done.2.first_a.refs_1_), channel_id=1, source_target_pairs={{0,384},{16,144},{128,256},{144,16},{256,128},{272,400},{384,0},{4... | collective-permute-start | bytes 983048 | tf_op jit(solution)/shard_map/ppermute | solution.py:237
  77.4 2.6 %copy-start.12 = (bf16[32,40,128]{2,1,0:T(8,128)(2,1)}, bf16[32,40,128]{2,1,0:T(8,128)(2,1)S(1)}, u32[]{:S(2)}) copy-start(bf16[32,40,128]{2,1,0:T(8,128)(2,1)S(1)} %collective-permute-done.7.first_b.refs_2_) | copy-start | bytes 983044
  77.4 1.2 copy-start.3
  80.0 1.1 copy-start.14
  81.2 1.2 copy-start.4
  81.2 1.1 copy-start.6
  82.3 3.5 %collective-permute-start.8 = (bf16[640,256]{1,0:T(8,128)(2,1)S(1)}, bf16[640,256]{1,0:T(8,128)(2,1)S(1)}, u32[]{:S(2)}, u32[]{:S(2)}) collective-permute-start(bf16[640,256]{1,0:T(8,128)(2,1)S(1)} %get-tuple-element.27), channel_id=1, source_target_pairs={{0,16},{16,0},{1,17},{17,1},{2,18},{18,2},{3,19},{19,3},{4,20},{20... | collective-permute-start | bytes 983048 | tf_op jit(solution)/shard_map/ppermute | solution.py:241
  88.4 10.2 %collective-permute-start.9 = (bf16[4,320,128]{2,1,0:T(8,128)(2,1)S(1)}, bf16[4,320,128]{2,1,0:T(8,128)(2,1)S(1)}, u32[]{:S(2)}, u32[]{:S(2)}) collective-permute-start(bf16[4,320,128]{2,1,0:T(8,128)(2,1)S(1)} %get-tuple-element.30), channel_id=1, source_target_pairs={{0,384},{16,144},{128,256},{144,16},{256,128},{272,400},{384,0},{4... | collective-permute-start | bytes 983048 | tf_op jit(solution)/shard_map/ppermute | solution.py:237
  91.6 10.4 %collective-permute-start.11 = (bf16[4,320,128]{2,1,0:T(8,128)(2,1)S(1)}, bf16[4,320,128]{2,1,0:T(8,128)(2,1)S(1)}, u32[]{:S(2)}, u32[]{:S(2)}) collective-permute-start(bf16[4,320,128]{2,1,0:T(8,128)(2,1)S(1)} %get-tuple-element.31), channel_id=1, source_target_pairs={{0,384},{16,144},{128,256},{144,16},{256,128},{272,400},{384,0},{4... | collective-permute-start | bytes 983048 | tf_op jit(solution)/shard_map/ppermute | solution.py:237
  98.6 9.0 %collective-permute-start.10 = (bf16[4,320,128]{2,1,0:T(8,128)(2,1)S(1)}, bf16[4,320,128]{2,1,0:T(8,128)(2,1)S(1)}, u32[]{:S(2)}, u32[]{:S(2)}) collective-permute-start(bf16[4,320,128]{2,1,0:T(8,128)(2,1)S(1)} %shard_map.91), channel_id=1, source_target_pairs={{0,128},{16,400},{128,0},{144,272},{256,384},{272,144},{384,256},{... | collective-permute-start | bytes 983048 | tf_op jit(solution)/shard_map/ppermute | solution.py:237
  107.6 9.0 %copy-start.9 = (bf16[32,40,128]{2,1,0:T(8,128)(2,1)S(1)}, bf16[32,40,128]{2,1,0:T(8,128)(2,1)}, u32[]{:S(2)}) copy-start(bf16[32,40,128]{2,1,0:T(8,128)(2,1)} %copy-done.8) | copy-start | bytes 983044
  107.6 9.0 %copy-start.11 = (bf16[32,40,128]{2,1,0:T(8,128)(2,1)S(1)}, bf16[32,40,128]{2,1,0:T(8,128)(2,1)}, u32[]{:S(2)}) copy-start(bf16[32,40,128]{2,1,0:T(8,128)(2,1)} %copy-done.10) | copy-start | bytes 983044
  107.6 9.0 %copy-start.13 = (bf16[32,40,128]{2,1,0:T(8,128)(2,1)S(1)}, bf16[32,40,128]{2,1,0:T(8,128)(2,1)}, u32[]{:S(2)}) copy-start(bf16[32,40,128]{2,1,0:T(8,128)(2,1)} %copy-done.12) | copy-start | bytes 983044
  107.6 9.0 %copy-start.15 = (bf16[32,40,128]{2,1,0:T(8,128)(2,1)S(1)}, bf16[32,40,128]{2,1,0:T(8,128)(2,1)}, u32[]{:S(2)}) copy-start(bf16[32,40,128]{2,1,0:T(8,128)(2,1)} %copy-done.14) | copy-start | bytes 983044
  108.5 8.1 %copy-start.5 = (bf16[32,40,128]{2,1,0:T(8,128)(2,1)S(1)}, bf16[32,40,128]{2,1,0:T(8,128)(2,1)}, u32[]{:S(2)}) copy-start(bf16[32,40,128]{2,1,0:T(8,128)(2,1)} %copy-done.4) | copy-start | bytes 983044
  108.5 8.1 %copy-start.7 = (bf16[32,40,128]{2,1,0:T(8,128)(2,1)S(1)}, bf16[32,40,128]{2,1,0:T(8,128)(2,1)}, u32[]{:S(2)}) copy-start(bf16[32,40,128]{2,1,0:T(8,128)(2,1)} %copy-done.6) | copy-start | bytes 983044
  108.5 34.6 %all-to-all-start.1 = ((bf16[64,20,128]{2,1,0:T(8,128)(2,1)}), bf16[64,20,128]{2,1,0:T(8,128)(2,1)S(1)}, u32[]{:S(2)}, u32[]{:S(2)}) async-start(bf16[64,20,128]{2,1,0:T(8,128)(2,1)} %shard_map.92.after_ref.refs_7_), calls=%async_computation.1 | async-start | bytes 786432 | tf_op jit(solution)/shard_map/all_to_all | solution.py:282
  116.6 1.1 copy-start.16
  120.1 5.3 %collective-permute-start.12 = (bf16[16,128,128]{2,1,0:T(8,128)(2,1)S(1)}, bf16[16,128,128]{2,1,0:T(8,128)(2,1)S(1)}, u32[]{:S(2)}, u32[]{:S(2)}) collective-permute-start(bf16[16,128,128]{2,1,0:T(8,128)(2,1)S(1)} %get-tuple-element.35), channel_id=1, source_target_pairs={{0,16},{16,0},{1,17},{17,1},{2,18},{18,2},{3,19},{19,3},{4,20},{20... | collective-permute-start | bytes 1572872 | tf_op jit(solution)/shard_map/ppermute | solution.py:241
  122.0 3.9 %collective-permute-start.13 = (bf16[16,128,128]{2,1,0:T(8,128)(2,1)S(1)}, bf16[16,128,128]{2,1,0:T(8,128)(2,1)S(1)}, u32[]{:S(2)}, u32[]{:S(2)}) collective-permute-start(bf16[16,128,128]{2,1,0:T(8,128)(2,1)S(1)} %get-tuple-element.36), channel_id=1, source_target_pairs={{0,16},{16,0},{1,17},{17,1},{2,18},{18,2},{3,19},{19,3},{4,20},{20... | collective-permute-start | bytes 1572872 | tf_op jit(solution)/shard_map/ppermute | solution.py:241

commit v4 on v3

--- a/solution.py
+++ b/solution.py
@@ -16,7 +16,7 @@
 KEPT = EXPERTS * CAP
 BF16 = jnp.bfloat16
 F32 = jnp.float32
-VMEM = pltpu.CompilerParams(vmem_limit_bytes=24 * 1024 * 1024)
+VMEM = pltpu.CompilerParams(vmem_limit_bytes=14 * 1024 * 1024)
 CONTRACT_LAST = (((1,), (1,)), ((), ()))
 CONTRACT_FIRST = (((0,), (0,)), ((), ()))
 
@@ -47,9 +47,9 @@
     out_ref[...] = out.astype(BF16).reshape(EXPERTS, MSG, COLS)
 
 
-def split_kernel(pos_ref, w_in_ref, w_out_ref, after_ref, in_ref, out_ref, sems):
+def split_kernel(w_in_ref, w_out_ref, after_ref, in_ref, out_ref, sems):
     del after_ref
-    other = 1 - pos_ref[1]
+    other = 1 - position()[1]
     blocks = NY * NZ
     copies = [pltpu.make_async_copy(w_in_ref.at[:, other], in_ref, sems.at[blocks])]
     for k in range(blocks):
@@ -67,6 +67,10 @@
     table_ref[...] = table.astype(BF16)
 
 
+def position():
+    return lax.axis_index("y"), lax.axis_index("c")
+
+
 def places(y, c):
     near, far = y + 1 - 2 * lax.rem(y, 2), NY - 1 - y
     return y, jnp.where(c == 0, near, far), jnp.where(c == 0, far, near), lax.rem(y + 2, NY)
@@ -90,9 +94,9 @@
     return jnp.concatenate([mine, sib_ref[k]], axis=0)
 
 
-def forward(pos_ref, w_in_ref, w_out_ref, in_sib_ref, out_sib_ref, xs):
-    c = pos_ref[1]
-    at_of = places(pos_ref[0], c)
+def forward(w_in_ref, w_out_ref, in_sib_ref, out_sib_ref, xs):
+    _, c = position()
+    at_of = places(position()[0], c)
     pre = jnp.zeros((ROWS, NC * HID), F32)
     act_grad = jnp.zeros((ROWS, NC * HID), F32)
     for place, blocks in xs:
@@ -115,22 +119,21 @@
     return [(low, 0), (low, 1), (high, 0), (high, 1)]
 
 
-def forward_first_kernel(pos_ref, wi, wo, wis, wos, own, first_a, first_b, out_ref):
-    out_ref[...] = forward(pos_ref, wi, wo, wis, wos, [(0, whole(own)), (1, halves(first_a, first_b))])
-
-
-def forward_second_kernel(pos_ref, wi, wo, wis, wos, second_a, second_b, before_ref, out_ref):
-    out_ref[...] = before_ref[...] + forward(pos_ref, wi, wo, wis, wos, [(2, halves(second_a, second_b))])
-
-
-def forward_last_kernel(pos_ref, wi, wo, wis, wos, last_a, last_b, before_ref, out_ref, sent_ref):
-    total = before_ref[...] + forward(pos_ref, wi, wo, wis, wos, [(3, halves(last_a, last_b))])
+def forward_first_kernel(wi, wo, wis, wos, own, first_a, first_b, out_ref):
+    out_ref[...] = forward(wi, wo, wis, wos, [(0, whole(own)), (1, halves(first_a, first_b))])
+
+
+def forward_second_kernel(wi, wo, wis, wos, second_a, second_b, before_ref, out_ref):
+    out_ref[...] = before_ref[...] + forward(wi, wo, wis, wos, [(2, halves(second_a, second_b))])
+
+
+def forward_last_kernel(wi, wo, wis, wos, last_a, last_b, before_ref, out_ref, sent_ref):
+    total = before_ref[...] + forward(wi, wo, wis, wos, [(3, halves(last_a, last_b))])
     out_ref[...] = total
     sent_ref[...] = total.astype(BF16)
 
 
-def middle_kernel(pos_ref, w_in_ref, sib_ref, part_ref, part_sib_ref, pgact_ref, *outs):
-    c = pos_ref[1]
+def activations(part_ref, part_sib_ref):
     passed = part_sib_ref[...]
     both = part_ref[...] + joined(passed[:, HID:], passed[:, :HID]).astype(F32)
     act_grad = jnp.concatenate([both[CAP:], both[:CAP]], axis=0)
@@ -138,14 +141,17 @@
     pre_grad = pullback(act_grad)[0]
     act = jnp.concatenate([act[ROWS - CAP:], act[:ROWS - CAP]], axis=0)
     row = lax.broadcasted_iota(jnp.int32, (EXPERTS, MSG, NC * HID), 1).reshape(ROWS, NC * HID)
-    pre_grad = jnp.where(row < CAP, pre_grad, 0.0).astype(BF16)
-    act = jnp.where(row < CAP, 0.0, act).astype(BF16)
-    pgact_ref[...] = joined(pre_grad, act)
+    return jnp.where(row < CAP, pre_grad, 0.0).astype(BF16), jnp.where(row < CAP, 0.0, act).astype(BF16)
+
+
+def middle_kernel(w_in_ref, sib_ref, part_ref, part_sib_ref, *outs):
+    y, c = position()
+    pre_grad, _ = activations(part_ref, part_sib_ref)
     block = lax.broadcasted_iota(jnp.int32, (EXPERTS, CAP, ROWS), 0).reshape(KEPT, ROWS)
     within = lax.broadcasted_iota(jnp.int32, (EXPERTS, CAP, ROWS), 1).reshape(KEPT, ROWS)
     keep = (lax.broadcasted_iota(jnp.int32, (KEPT, ROWS), 1) == block * MSG + within).astype(BF16)
     pg = jnp.dot(keep, pre_grad, preferred_element_type=F32).astype(BF16)
-    for at, out_ref in zip(places(pos_ref[0], c), outs):
+    for at, out_ref in zip(places(y, c), outs):
         for zl in range(0, NZ, 2):
             w = jnp.concatenate([weights_in(w_in_ref, sib_ref, c, at * NZ + z) for z in (zl, zl + 1)], axis=0)
             out = lax.dot_general(pg, w, CONTRACT_LAST, preferred_element_type=F32).astype(BF16)
@@ -157,17 +163,23 @@
     out_ref[...] = (mine_ref[...].astype(F32) + passed_ref[...].astype(F32)).astype(BF16)
 
 
-def total_kernel(mine_ref, first_ref, second_ref, out_ref):
-    for zl in range(NZ):
-        total = mine_ref[zl].astype(F32) + first_ref[zl].astype(F32) + second_ref[zl].astype(F32)
-        out_ref[zl * EXPERTS:(zl + 1) * EXPERTS] = total.reshape(EXPERTS, CAP, COLS).astype(BF16)
-
-
-def grads_kernel(pos_ref, pgact_ref, *refs):
+def total_kernel(mine_ref, first_ref, second_ref, after_ref, out_ref):
+    del after_ref
+    out_ref[...] = (mine_ref[...].astype(F32) + first_ref[...].astype(F32) + second_ref[...].astype(F32)).astype(BF16)
+
+
+def gathered_kernel(parts_ref, out_ref):
+    total = parts_ref[0].astype(F32)
+    for zl in range(1, NZ):
+        total = total + parts_ref[zl].astype(F32)
+    out_ref[...] = total.reshape(EXPERTS, CAP, COLS).astype(BF16)
+
+
+def grads_kernel(part_ref, part_sib_ref, *refs):
     xs, (in_mine, out_mine, in_other, out_other) = refs[:7], refs[8:]
-    left = pgact_ref[...].T
+    left = joined(*activations(part_ref, part_sib_ref)).T
     xs = [whole(xs[0])] + [halves(*xs[i:i + 2]) for i in (1, 3, 5)]
-    for y, blocks in zip(places(pos_ref[0], pos_ref[1]), xs):
+    for y, blocks in zip(places(*position()), xs):
         at = y * NZ
         for zl in range(0, NZ, 2):
             x = joined(chunk(*blocks[zl]), chunk(*blocks[zl + 1]))
@@ -182,8 +194,8 @@
                 out_other[at + zl + j] = both[3 * HID:, j * COLS:(j + 1) * COLS]
 
 
-def merge_kernel(pos_ref, in_mine, out_mine, in_sib, out_sib, w_in_grad_ref, w_out_grad_ref):
-    c = pos_ref[1]
+def merge_kernel(in_mine, out_mine, in_sib, out_sib, w_in_grad_ref, w_out_grad_ref):
+    _, c = position()
     blocks = NY * NZ
     for k in range(blocks):
         mine = pl.ds(pl.multiple_of((k * NC + c) * COLS, COLS), COLS)
@@ -195,10 +207,7 @@
 
 
 def combine_kernel(table_ref, back_ref, out_ref):
-    total = back_ref[0:EXPERTS].astype(F32)
-    for z in range(1, NZ):
-        total = total + back_ref[z * EXPERTS:(z + 1) * EXPERTS].astype(F32)
-    rows = total.reshape(KEPT, COLS).astype(BF16)
+    rows = back_ref[...].astype(F32).reshape(KEPT, COLS).astype(BF16)
     out_ref[...] = lax.dot_general(table_ref[...], rows, CONTRACT_FIRST, preferred_element_type=F32).astype(BF16)
 
 
@@ -242,21 +251,20 @@
 
 
 def on_device(tokens, out_grad, expert_ids, gate_weights, w_in, w_out):
-    pos = jnp.stack([lax.axis_index("y"), lax.axis_index("c")]).astype(jnp.int32)
     ids, gate = far(expert_ids.T), far(gate_weights.T)
     w_in, w_out = w_in[0], w_out[0]
     blocks = NY * NZ
     half_in, half_out = held(blocks, COLS, HID), held(HID, blocks * COLS)
     send = run(dispatch_kernel, shape(EXPERTS, MSG, COLS), 0, ids, gate, far(tokens), far(out_grad))
     in_other, out_other = run(
-        split_kernel, (half_in, half_in), 1, pos, far(w_in.reshape(blocks, NC, COLS, HID)), far(w_out), send,
+        split_kernel, (half_in, half_in), 0, far(w_in.reshape(blocks, NC, COLS, HID)), far(w_out), send,
         unread=3, scratch=[pltpu.SemaphoreType.DMA((blocks + 1,))],
     )
     in_sib, out_sib = across(in_other), across(out_other)
     received = lax.all_to_all(send, ("zh", "x"), 0, 0, tiled=True)
     received, in_sib, out_sib = lax.optimization_barrier((received, in_sib, out_sib))
     own = lax.all_gather(received, "zl", axis=0, tiled=True)
-    weights = (pos, w_in, w_out, keep(in_sib), keep(out_sib))
+    weights = (w_in, w_out, keep(in_sib), keep(out_sib))
     cut = NZ // 2 * EXPERTS
     low, high = own[:cut], own[cut:]
     first_a, second_b = partner(low, 0), partner(high, 1)
@@ -264,29 +272,31 @@
     last_a, last_b = partner(first_a, 1), partner(second_b, 0)
     xs = [keep(x) for x in (own, first_a, first_b, second_a, second_b, last_a, last_b)]
     part = held(ROWS, NC * HID, kind=F32)
-    some = run(forward_first_kernel, part, 1, *weights, *xs[:3])
-    more = run(forward_second_kernel, part, 1, *weights, *xs[3:5], keep(some))
+    some = run(forward_first_kernel, part, 0, *weights, *xs[:3])
+    more = run(forward_second_kernel, part, 0, *weights, *xs[3:5], keep(some))
     mine, sent = run(
-        forward_last_kernel, (part, held(ROWS, NC * HID)), 1, *weights, *xs[5:], keep(more)
+        forward_last_kernel, (part, held(ROWS, NC * HID)), 0, *weights, *xs[5:], keep(more)
     )
     rows = held(NZ, KEPT, COLS)
-    pgact, to_own, to_first, to_second, to_last = run(
-        middle_kernel,
-        (pltpu.HBM((ROWS, 2 * NC * HID), BF16), rows, rows, rows, rows),
-        1, pos, w_in, keep(in_sib), keep(mine), keep(across(sent)),
+    parts = keep(mine), keep(across(sent))
+    to_own, to_first, to_second, to_last = run(
+        middle_kernel, (rows, rows, rows, rows), 0, w_in, keep(in_sib), *parts
     )
     passed, from_second = partner(to_last, 1), partner(to_second, 1)
-    from_first = partner(run(relay_kernel, rows, 0, keep(to_first), keep(passed)), 0)
-    summed = run(total_kernel, held(NZ * EXPERTS, CAP, COLS), 0, keep(to_own), keep(from_first), keep(from_second))
-    table = run(table_kernel, held(KEPT, TOK), 0, ids, summed, unread=1)
-    back = lax.all_to_all(summed, ("zl", "zh", "x"), 0, 0, tiled=True)
+    relayed = run(relay_kernel, rows, 0, keep(to_first), keep(passed))
+    from_first = partner(relayed, 0)
+    in_mine, out_mine, in_other, out_other = run(
+        grads_kernel, (half_in, half_out, half_in, half_in), 0, *parts, *xs, relayed, unread=1
+    )
+    summed = run(total_kernel, rows, 0, keep(to_own), keep(from_first), keep(from_second), in_other, unread=1)
+    collected = lax.all_to_all(summed, "zl", 0, 0, tiled=True)
+    total = run(gathered_kernel, held(EXPERTS, CAP, COLS), 0, keep(collected))
+    table = run(table_kernel, held(KEPT, TOK), 0, ids, total, unread=1)
+    back = lax.all_to_all(total, ("zh", "x"), 0, 0, tiled=True)
     tokens_grad = run(combine_kernel, shape(TOK, COLS), 0, keep(table), keep(back))
-    in_mine, out_mine, in_other, out_other = run(
-        grads_kernel, (half_in, half_out, half_in, half_in), 1, pos, pgact, *xs, summed, unread=1
-    )
     w_in_grad, w_out_grad = run(
         merge_kernel, (shape(*w_in.shape), shape(*w_out.shape)),
-        1, pos, keep(in_mine), keep(out_mine), keep(across(in_other)), keep(across(out_other)),
+        0, keep(in_mine), keep(out_mine), keep(across(in_other)), keep(across(out_other)),
     )
     return tokens_grad, w_in_grad[None], w_out_grad[None]
 

time: 145 us -> 141 us (0.972)
  the two profiles are of different devices: /device:TPU:32 before, /device:TPU:2 now
where the time goes in v4:
time: 141 us; the launch traced here: 140 us
  starting transfers between devices  65.2 us (46%)
  waiting for transfers between devices  43.2 us (31%)
  blocking collectives  17.3 us (12%)
  Pallas kernels  13.3 us (9%)
    ppermute x9, starting transfers between devices, partner(): lax.ppermute(value, ('y', 'c'), [(i * NC + c, to[c][which][i] * NC + c) f...  27.3 us
    all_to_all x1, starting transfers between devices, on_device(): received = lax.all_to_all(send, ('zh', 'x'), 0, 0, tiled=True)  18.1 us
    all_gather x1, blocking collectives, on_device(): own = lax.all_gather(received, 'zl', axis=0, tiled=True)  17.3 us
    ppermute x9, waiting for transfers between devices, partner(): lax.ppermute(value, ('y', 'c'), [(i * NC + c, to[c][which][i] * NC + c) f...  15.9 us
    pallas_call x13, Pallas kernels, run(): pl.pallas_call(kernel, out_shape=outs, in_specs=specs, out_specs=out_spec...  13.3 us
    all_to_all x1, waiting for transfers between devices, on_device(): back = lax.all_to_all(total, ('zh', 'x'), 0, 0, tiled=True)  10.9 us
    ppermute x5, starting transfers between devices, across(): return lax.ppermute(value, 'c', [(0, 1), (1, 0)])  10.7 us
    all_to_all x1, waiting for transfers between devices, on_device(): received = lax.all_to_all(send, ('zh', 'x'), 0, 0, tiled=True)  8.76 us
  transfers between devices with their start and end apart: 17, of which 11 were waited for; matrix products, arithmetic and copies ran while one was open for 0% of the time, Pallas kernels for 6%

profile of v4, /device:TPU:2, one launch (start us, length us, event | category | flops | bytes accessed | tf_op | source)
XLA Modules:
  0.0 140.1 jit_solution(1330127450300997007)
XLA Ops:
  0.6 2.0 %shard_map.85.after_ref = bf16[16,40,128]{2,1,0:T(8,128)(2,1)} custom-call(s32[2,128]{1,0:T(2,128)} %bitcast.16, f32[2,128]{1,0:T(2,128)} %bitcast.18, bf16[128,128]{1,0:T(8,128)(2,1)} %tok_ref.1, bf16[128,128]{1,0:T(8,128)(2,1)} %dy_ref.1), custom_call_target="tpu_custom_call" | custom-call | tf_op jit(solution)/shard_map/pallas_call | solution.py:238
  2.6 18.1 %all-to-all-start = ((bf16[16,40,128]{2,1,0:T(8,128)(2,1)}), bf16[16,40,128]{2,1,0:T(8,128)(2,1)S(1)}, u32[]{:S(2)}, u32[]{:S(2)}) async-start(bf16[16,40,128]{2,1,0:T(8,128)(2,1)} %shard_map.85.after_ref), calls=%async_computation | async-start | bytes 327680 | tf_op jit(solution)/shard_map/all_to_all | solution.py:264
  20.7 1.3 shard_map.86
  22.0 1.9 %collective-permute-start = (bf16[16,128,128]{2,1,0:T(8,128)(2,1)S(1)}, bf16[16,128,128]{2,1,0:T(8,128)(2,1)S(1)}, u32[]{:S(2)}, u32[]{:S(2)}) collective-permute-start(bf16[16,128,128]{2,1,0:T(8,128)(2,1)S(1)} %get-tuple-element.20), channel_id=1, source_target_pairs={{0,16},{16,0},{1,17},{17,1},{2,18},{18,2},{3,19},{19,3},{4,20},{20... | collective-permute-start | bytes 1572872 | tf_op jit(solution)/shard_map/ppermute | solution.py:250
  23.9 0.0 copy-start
  23.9 0.0 copy-start.1
  23.9 2.5 %collective-permute-start.1 = (bf16[16,128,128]{2,1,0:T(8,128)(2,1)S(1)}, bf16[16,128,128]{2,1,0:T(8,128)(2,1)S(1)}, u32[]{:S(2)}, u32[]{:S(2)}) collective-permute-start(bf16[16,128,128]{2,1,0:T(8,128)(2,1)S(1)} %get-tuple-element.21), channel_id=1, source_target_pairs={{0,16},{16,0},{1,17},{17,1},{2,18},{18,2},{3,19},{19,3},{4,20},{20... | collective-permute-start | bytes 1572872 | tf_op jit(solution)/shard_map/ppermute | solution.py:250
  26.5 0.0 collective-permute-done.wis.sib_ref
  26.5 1.5 %collective-permute-done.1.wos = bf16[16,128,128]{2,1,0:T(8,128)(2,1)S(1)} collective-permute-done((bf16[16,128,128]{2,1,0:T(8,128)(2,1)S(1)}, bf16[16,128,128]{2,1,0:T(8,128)(2,1)S(1)}, u32[]{:S(2)}, u32[]{:S(2)}) %collective-permute-start.1) | collective-permute-done | bytes 524320 | tf_op jit(solution)/shard_map/ppermute | solution.py:250
  28.0 8.8 %all-to-all-done = bf16[16,40,128]{2,1,0:T(8,128)(2,1)S(1)} async-done(((bf16[16,40,128]{2,1,0:T(8,128)(2,1)}), bf16[16,40,128]{2,1,0:T(8,128)(2,1)S(1)}, u32[]{:S(2)}, u32[]{:S(2)}) %all-to-all-start) | async-done | bytes 163872 | tf_op jit(solution)/shard_map/all_to_all | solution.py:264
  36.7 17.3 %all_gather.3.own.refs_0_ = bf16[64,40,128]{2,1,0:T(8,128)(2,1)S(1)} all-gather(bf16[16,40,128]{2,1,0:T(8,128)(2,1)S(1)} %all-to-all-done), channel_id=1, replica_groups=mesh['y'=4,'zl'=4,'c'=2,'zh'=4,'x'=4] {'zl'}, dimensions={0}, use_global_device_ids=true | all-gather | bytes 819200 | tf_op jit(solution)/shard_map/all_gather | solution.py:266
  54.1 0.1 fusion
  54.1 4.9 %collective-permute-start.4 = (bf16[32,40,128]{2,1,0:T(8,128)(2,1)S(1)}, bf16[32,40,128]{2,1,0:T(8,128)(2,1)S(1)}, u32[]{:S(2)}, u32[]{:S(2)}) collective-permute-start(bf16[32,40,128]{2,1,0:T(8,128)(2,1)S(1)} %get-tuple-element.37), channel_id=1, source_target_pairs={{0,384},{16,144},{128,256},{144,16},{256,128},{272,400},{384,0},{4... | collective-permute-start | bytes 983048 | tf_op jit(solution)/shard_map/ppermute | solution.py:246
  59.0 2.0 %collective-permute-start.2 = (bf16[32,40,128]{2,1,0:T(8,128)(2,1)S(1)}, bf16[32,40,128]{2,1,0:T(8,128)(2,1)S(1)}, u32[]{:S(2)}, u32[]{:S(2)}) collective-permute-start(bf16[32,40,128]{2,1,0:T(8,128)(2,1)S(1)} %get-tuple-element.38), channel_id=1, source_target_pairs={{0,128},{16,400},{128,0},{144,272},{256,384},{272,144},{384,256},{... | collective-permute-start | bytes 983048 | tf_op jit(solution)/shard_map/ppermute | solution.py:246
  61.1 3.8 %collective-permute-start.7 = (bf16[32,40,128]{2,1,0:T(8,128)(2,1)S(1)}, bf16[32,40,128]{2,1,0:T(8,128)(2,1)S(1)}, u32[]{:S(2)}, u32[]{:S(2)}) collective-permute-start(bf16[32,40,128]{2,1,0:T(8,128)(2,1)S(1)} %get-tuple-element.37), channel_id=1, source_target_pairs={{0,128},{16,400},{128,0},{144,272},{256,384},{272,144},{384,256},{... | collective-permute-start | bytes 983048 | tf_op jit(solution)/shard_map/ppermute | solution.py:246
  64.9 2.1 %collective-permute-start.6 = (bf16[32,40,128]{2,1,0:T(8,128)(2,1)S(1)}, bf16[32,40,128]{2,1,0:T(8,128)(2,1)S(1)}, u32[]{:S(2)}, u32[]{:S(2)}) collective-permute-start(bf16[32,40,128]{2,1,0:T(8,128)(2,1)S(1)} %get-tuple-element.38), channel_id=1, source_target_pairs={{0,384},{16,144},{128,256},{144,16},{256,128},{272,400},{384,0},{4... | collective-permute-start | bytes 983048 | tf_op jit(solution)/shard_map/ppermute | solution.py:246
  67.1 0.8 collective-permute-done.4.second_b.refs_4_
  67.9 2.3 %collective-permute-start.5 = (bf16[32,40,128]{2,1,0:T(8,128)(2,1)S(1)}, bf16[32,40,128]{2,1,0:T(8,128)(2,1)S(1)}, u32[]{:S(2)}, u32[]{:S(2)}) collective-permute-start(bf16[32,40,128]{2,1,0:T(8,128)(2,1)S(1)} %collective-permute-done.4.second_b.refs_4_), channel_id=1, source_target_pairs={{0,128},{16,400},{128,0},{144,272},{256,384},{272,144},{384,256},{... | collective-permute-start | bytes 983048 | tf_op jit(solution)/shard_map/ppermute | solution.py:246
  70.1 1.4 collective-permute-done.2.first_a.refs_1_
  71.5 3.2 %collective-permute-start.3 = (bf16[32,40,128]{2,1,0:T(8,128)(2,1)S(1)}, bf16[32,40,128]{2,1,0:T(8,128)(2,1)S(1)}, u32[]{:S(2)}, u32[]{:S(2)}) collective-permute-start(bf16[32,40,128]{2,1,0:T(8,128)(2,1)S(1)} %collective-permute-done.2.first_a.refs_1_), channel_id=1, source_target_pairs={{0,384},{16,144},{128,256},{144,16},{256,128},{272,400},{384,0},{4... | collective-permute-start | bytes 983048 | tf_op jit(solution)/shard_map/ppermute | solution.py:246
  74.7 3.5 %collective-permute-done.7.first_b.refs_2_ = bf16[32,40,128]{2,1,0:T(8,128)(2,1)S(1)} collective-permute-done((bf16[32,40,128]{2,1,0:T(8,128)(2,1)S(1)}, bf16[32,40,128]{2,1,0:T(8,128)(2,1)S(1)}, u32[]{:S(2)}, u32[]{:S(2)}) %collective-permute-start.7) | collective-permute-done | bytes 327712 | tf_op jit(solution)/shard_map/ppermute | solution.py:246
  78.3 0.9 shard_map.87.before_ref
  79.1 0.0 collective-permute-done.6.second_a.refs_3_
  79.2 0.5 shard_map.88.before_ref
  79.7 2.1 %collective-permute-done.5.last_b.refs_6_ = bf16[32,40,128]{2,1,0:T(8,128)(2,1)S(1)} collective-permute-done((bf16[32,40,128]{2,1,0:T(8,128)(2,1)S(1)}, bf16[32,40,128]{2,1,0:T(8,128)(2,1)S(1)}, u32[]{:S(2)}, u32[]{:S(2)}) %collective-permute-start.5) | collective-permute-done | bytes 327712 | tf_op jit(solution)/shard_map/ppermute | solution.py:246
  81.8 0.0 collective-permute-done.3.last_a.refs_5_
  81.8 0.5 shard_map.89
  82.3 1.9 %collective-permute-start.8 = (bf16[640,256]{1,0:T(8,128)(2,1)S(1)}, bf16[640,256]{1,0:T(8,128)(2,1)S(1)}, u32[]{:S(2)}, u32[]{:S(2)}) collective-permute-start(bf16[640,256]{1,0:T(8,128)(2,1)S(1)} %get-tuple-element.26), channel_id=1, source_target_pairs={{0,16},{16,0},{1,17},{17,1},{2,18},{18,2},{3,19},{19,3},{4,20},{20... | collective-permute-start | bytes 983048 | tf_op jit(solution)/shard_map/ppermute | solution.py:250
  84.2 1.6 %collective-permute-done.8.part_sib_ref = bf16[640,256]{1,0:T(8,128)(2,1)S(1)} collective-permute-done((bf16[640,256]{1,0:T(8,128)(2,1)S(1)}, bf16[640,256]{1,0:T(8,128)(2,1)S(1)}, u32[]{:S(2)}, u32[]{:S(2)}) %collective-permute-start.8) | collective-permute-done | bytes 327712 | tf_op jit(solution)/shard_map/ppermute | solution.py:250
  85.8 1.1 shard_map.90
  87.0 3.1 %collective-permute-start.9 = (bf16[4,320,128]{2,1,0:T(8,128)(2,1)S(1)}, bf16[4,320,128]{2,1,0:T(8,128)(2,1)S(1)}, u32[]{:S(2)}, u32[]{:S(2)}) collective-permute-start(bf16[4,320,128]{2,1,0:T(8,128)(2,1)S(1)} %get-tuple-element.29), channel_id=1, source_target_pairs={{0,384},{16,144},{128,256},{144,16},{256,128},{272,400},{384,0},{4... | collective-permute-start | bytes 983048 | tf_op jit(solution)/shard_map/ppermute | solution.py:246
  90.1 3.9 %collective-permute-start.11 = (bf16[4,320,128]{2,1,0:T(8,128)(2,1)S(1)}, bf16[4,320,128]{2,1,0:T(8,128)(2,1)S(1)}, u32[]{:S(2)}, u32[]{:S(2)}) collective-permute-start(bf16[4,320,128]{2,1,0:T(8,128)(2,1)S(1)} %get-tuple-element.30), channel_id=1, source_target_pairs={{0,384},{16,144},{128,256},{144,16},{256,128},{272,400},{384,0},{4... | collective-permute-start | bytes 983048 | tf_op jit(solution)/shard_map/ppermute | solution.py:246
  94.0 3.1 %collective-permute-done.9.passed_ref = bf16[4,320,128]{2,1,0:T(8,128)(2,1)S(1)} collective-permute-done((bf16[4,320,128]{2,1,0:T(8,128)(2,1)S(1)}, bf16[4,320,128]{2,1,0:T(8,128)(2,1)S(1)}, u32[]{:S(2)}, u32[]{:S(2)}) %collective-permute-start.9) | collective-permute-done | bytes 327712 | tf_op jit(solution)/shard_map/ppermute | solution.py:246
  97.1 0.1 shard_map.91.refs_7_
  97.2 1.9 %collective-permute-start.10 = (bf16[4,320,128]{2,1,0:T(8,128)(2,1)S(1)}, bf16[4,320,128]{2,1,0:T(8,128)(2,1)S(1)}, u32[]{:S(2)}, u32[]{:S(2)}) collective-permute-start(bf16[4,320,128]{2,1,0:T(8,128)(2,1)S(1)} %shard_map.91.refs_7_), channel_id=1, source_target_pairs={{0,128},{16,400},{128,0},{144,272},{256,384},{272,144},{384,256},{... | collective-permute-start | bytes 983048 | tf_op jit(solution)/shard_map/ppermute | solution.py:246
  99.1 2.0 %shard_map.92 = (bf16[16,128,128]{2,1,0:T(8,128)(2,1)S(1)}, bf16[128,2048]{1,0:T(8,128)(2,1)S(1)}, bf16[16,128,128]{2,1,0:T(8,128)(2,1)S(1)}, bf16[16,128,128]{2,1,0:T(8,128)(2,1)S(1)}) custom-call(f32[640,256]{1,0:T(8,128)S(1)} %get-tuple-element.25.part_ref, bf16[640,256]{1,0:T(8,128)(2,1)S(1)} %collective-permute-done.8.part_sib_ref, ...), custom_call_target="tpu_custom_call" | custom-call | tf_op jit(solution)/shard_map/pallas_call | solution.py:238
  101.2 5.0 %collective-permute-done.10.first_ref = bf16[4,320,128]{2,1,0:T(8,128)(2,1)S(1)} collective-permute-done((bf16[4,320,128]{2,1,0:T(8,128)(2,1)S(1)}, bf16[4,320,128]{2,1,0:T(8,128)(2,1)S(1)}, u32[]{:S(2)}, u32[]{:S(2)}) %collective-permute-start.10) | collective-permute-done | bytes 327712 | tf_op jit(solution)/shard_map/ppermute | solution.py:246
  106.2 0.8 shard_map.93
  107.0 3.5 %all-to-all-start.1 = ((bf16[4,320,128]{2,1,0:T(8,128)(2,1)}), bf16[4,320,128]{2,1,0:T(8,128)(2,1)S(1)}, u32[]{:S(2)}, u32[]{:S(2)}) async-start(bf16[4,320,128]{2,1,0:T(8,128)(2,1)} %shard_map.93), calls=%async_computation.1 | async-start | bytes 655360 | tf_op jit(solution)/shard_map/all_to_all | solution.py:292
  110.5 1.9 %collective-permute-start.13 = (bf16[16,128,128]{2,1,0:T(8,128)(2,1)S(1)}, bf16[16,128,128]{2,1,0:T(8,128)(2,1)S(1)}, u32[]{:S(2)}, u32[]{:S(2)}) collective-permute-start(bf16[16,128,128]{2,1,0:T(8,128)(2,1)S(1)} %get-tuple-element.34), channel_id=1, source_target_pairs={{0,16},{16,0},{1,17},{17,1},{2,18},{18,2},{3,19},{19,3},{4,20},{20... | collective-permute-start | bytes 1572872 | tf_op jit(solution)/shard_map/ppermute | solution.py:250
  112.4 2.4 %collective-permute-start.12 = (bf16[16,128,128]{2,1,0:T(8,128)(2,1)S(1)}, bf16[16,128,128]{2,1,0:T(8,128)(2,1)S(1)}, u32[]{:S(2)}, u32[]{:S(2)}) collective-permute-start(bf16[16,128,128]{2,1,0:T(8,128)(2,1)S(1)} %get-tuple-element.31.after_ref), channel_id=1, source_target_pairs={{0,16},{16,0},{1,17},{17,1},{2,18},{18,2},{3,19},{19,3},{4,20},{20... | collective-permute-start | bytes 1572872 | tf_op jit(solution)/shard_map/ppermute | solution.py:250
  114.8 4.5 %all-to-all-done.1.parts_ref = bf16[4,320,128]{2,1,0:T(8,128)(2,1)S(1)} async-done(((bf16[4,320,128]{2,1,0:T(8,128)(2,1)}), bf16[4,320,128]{2,1,0:T(8,128)(2,1)S(1)}, u32[]{:S(2)}, u32[]{:S(2)}) %all-to-all-start.1) | async-done | bytes 327712 | tf_op jit(solution)/shard_map/all_to_all | solution.py:292
  119.3 0.7 shard_map.94.after_ref
  120.0 5.7 %all-to-all-start.2 = ((bf16[16,20,128]{2,1,0:T(8,128)(2,1)}), bf16[16,20,128]{2,1,0:T(8,128)(2,1)S(1)}, u32[]{:S(2)}, u32[]{:S(2)}) async-start(bf16[16,20,128]{2,1,0:T(8,128)(2,1)} %shard_map.94.after_ref), calls=%async_computation.2 | async-start | bytes 196608 | tf_op jit(solution)/shard_map/all_to_all | solution.py:295
  125.7 1.6 %shard_map.97 = (bf16[4096,128]{1,0:T(8,128)(2,1)}, bf16[128,4096]{1,0:T(8,128)(2,1)}) custom-call(bf16[16,128,128]{2,1,0:T(8,128)(2,1)S(1)} %get-tuple-element.32.in_mine, bf16[128,2048]{1,0:T(8,128)(2,1)S(1)} %get-tuple-element.33.out_mine, bf16[16,128,128]{2,1,0:T(8,128)(2,1)S(1)} %collective-permute-done.12.in_sib, ...), custom_call_target="tpu_custom_call" | custom-call | tf_op jit(solution)/shard_map/pallas_call | solution.py:238
  127.3 1.0 shard_map.95.table_ref
  128.3 10.9 %all-to-all-done.2.back_ref = bf16[16,20,128]{2,1,0:T(8,128)(2,1)S(1)} async-done(((bf16[16,20,128]{2,1,0:T(8,128)(2,1)}), bf16[16,20,128]{2,1,0:T(8,128)(2,1)S(1)}, u32[]{:S(2)}, u32[]{:S(2)}) %all-to-all-start.2) | async-done | bytes 81952 | tf_op jit(solution)/shard_map/all_to_all | solution.py:295
  139.2 0.8 shard_map.96
  (5 shorter events, 0.0 us)
Async XLA Ops:
  2.6 34.1 %all-to-all-start = ((bf16[16,40,128]{2,1,0:T(8,128)(2,1)}), bf16[16,40,128]{2,1,0:T(8,128)(2,1)S(1)}, u32[]{:S(2)}, u32[]{:S(2)}) async-start(bf16[16,40,128]{2,1,0:T(8,128)(2,1)} %shard_map.85.after_ref), calls=%async_computation | async-start | bytes 327680 | tf_op jit(solution)/shard_map/all_to_all | solution.py:264
  22.0 4.5 %collective-permute-start = (bf16[16,128,128]{2,1,0:T(8,128)(2,1)S(1)}, bf16[16,128,128]{2,1,0:T(8,128)(2,1)S(1)}, u32[]{:S(2)}, u32[]{:S(2)}) collective-permute-start(bf16[16,128,128]{2,1,0:T(8,128)(2,1)S(1)} %get-tuple-element.20), channel_id=1, source_target_pairs={{0,16},{16,0},{1,17},{17,1},{2,18},{18,2},{3,19},{19,3},{4,20},{20... | collective-permute-start | bytes 1572872 | tf_op jit(solution)/shard_map/ppermute | solution.py:250
  23.9 54.4 %copy-start = (bf16[1,4096,128]{2,1,0:T(8,128)(2,1)S(1)}, bf16[1,4096,128]{2,1,0:T(8,128)(2,1)}, u32[]{:S(2)}) copy-start(bf16[1,4096,128]{2,1,0:T(8,128)(2,1)} %param.10) | copy-start | bytes 3145732
  23.9 54.4 %copy-start.1 = (bf16[1,128,4096]{2,1,0:T(8,128)(2,1)S(1)}, bf16[1,128,4096]{2,1,0:T(8,128)(2,1)}, u32[]{:S(2)}) copy-start(bf16[1,128,4096]{2,1,0:T(8,128)(2,1)} %param.11) | copy-start | bytes 3145732
  23.9 4.1 %collective-permute-start.1 = (bf16[16,128,128]{2,1,0:T(8,128)(2,1)S(1)}, bf16[16,128,128]{2,1,0:T(8,128)(2,1)S(1)}, u32[]{:S(2)}, u32[]{:S(2)}) collective-permute-start(bf16[16,128,128]{2,1,0:T(8,128)(2,1)S(1)} %get-tuple-element.21), channel_id=1, source_target_pairs={{0,16},{16,0},{1,17},{17,1},{2,18},{18,2},{3,19},{19,3},{4,20},{20... | collective-permute-start | bytes 1572872 | tf_op jit(solution)/shard_map/ppermute | solution.py:250
  54.1 13.8 %collective-permute-start.4 = (bf16[32,40,128]{2,1,0:T(8,128)(2,1)S(1)}, bf16[32,40,128]{2,1,0:T(8,128)(2,1)S(1)}, u32[]{:S(2)}, u32[]{:S(2)}) collective-permute-start(bf16[32,40,128]{2,1,0:T(8,128)(2,1)S(1)} %get-tuple-element.37), channel_id=1, source_target_pairs={{0,384},{16,144},{128,256},{144,16},{256,128},{272,400},{384,0},{4... | collective-permute-start | bytes 983048 | tf_op jit(solution)/shard_map/ppermute | solution.py:246
  59.0 12.5 %collective-permute-start.2 = (bf16[32,40,128]{2,1,0:T(8,128)(2,1)S(1)}, bf16[32,40,128]{2,1,0:T(8,128)(2,1)S(1)}, u32[]{:S(2)}, u32[]{:S(2)}) collective-permute-start(bf16[32,40,128]{2,1,0:T(8,128)(2,1)S(1)} %get-tuple-element.38), channel_id=1, source_target_pairs={{0,128},{16,400},{128,0},{144,272},{256,384},{272,144},{384,256},{... | collective-permute-start | bytes 983048 | tf_op jit(solution)/shard_map/ppermute | solution.py:246
  61.1 17.2 %collective-permute-start.7 = (bf16[32,40,128]{2,1,0:T(8,128)(2,1)S(1)}, bf16[32,40,128]{2,1,0:T(8,128)(2,1)S(1)}, u32[]{:S(2)}, u32[]{:S(2)}) collective-permute-start(bf16[32,40,128]{2,1,0:T(8,128)(2,1)S(1)} %get-tuple-element.37), channel_id=1, source_target_pairs={{0,128},{16,400},{128,0},{144,272},{256,384},{272,144},{384,256},{... | collective-permute-start | bytes 983048 | tf_op jit(solution)/shard_map/ppermute | solution.py:246
  64.9 14.2 %collective-permute-start.6 = (bf16[32,40,128]{2,1,0:T(8,128)(2,1)S(1)}, bf16[32,40,128]{2,1,0:T(8,128)(2,1)S(1)}, u32[]{:S(2)}, u32[]{:S(2)}) collective-permute-start(bf16[32,40,128]{2,1,0:T(8,128)(2,1)S(1)} %get-tuple-element.38), channel_id=1, source_target_pairs={{0,384},{16,144},{128,256},{144,16},{256,128},{272,400},{384,0},{4... | collective-permute-start | bytes 983048 | tf_op jit(solution)/shard_map/ppermute | solution.py:246
  67.9 13.9 %collective-permute-start.5 = (bf16[32,40,128]{2,1,0:T(8,128)(2,1)S(1)}, bf16[32,40,128]{2,1,0:T(8,128)(2,1)S(1)}, u32[]{:S(2)}, u32[]{:S(2)}) collective-permute-start(bf16[32,40,128]{2,1,0:T(8,128)(2,1)S(1)} %collective-permute-done.4.second_b.refs_4_), channel_id=1, source_target_pairs={{0,128},{16,400},{128,0},{144,272},{256,384},{272,144},{384,256},{... | collective-permute-start | bytes 983048 | tf_op jit(solution)/shard_map/ppermute | solution.py:246
  71.5 10.3 %collective-permute-start.3 = (bf16[32,40,128]{2,1,0:T(8,128)(2,1)S(1)}, bf16[32,40,128]{2,1,0:T(8,128)(2,1)S(1)}, u32[]{:S(2)}, u32[]{:S(2)}) collective-permute-start(bf16[32,40,128]{2,1,0:T(8,128)(2,1)S(1)} %collective-permute-done.2.first_a.refs_1_), channel_id=1, source_target_pairs={{0,384},{16,144},{128,256},{144,16},{256,128},{272,400},{384,0},{4... | collective-permute-start | bytes 983048 | tf_op jit(solution)/shard_map/ppermute | solution.py:246
  82.3 3.5 %collective-permute-start.8 = (bf16[640,256]{1,0:T(8,128)(2,1)S(1)}, bf16[640,256]{1,0:T(8,128)(2,1)S(1)}, u32[]{:S(2)}, u32[]{:S(2)}) collective-permute-start(bf16[640,256]{1,0:T(8,128)(2,1)S(1)} %get-tuple-element.26), channel_id=1, source_target_pairs={{0,16},{16,0},{1,17},{17,1},{2,18},{18,2},{3,19},{19,3},{4,20},{20... | collective-permute-start | bytes 983048 | tf_op jit(solution)/shard_map/ppermute | solution.py:250
  87.0 10.2 %collective-permute-start.9 = (bf16[4,320,128]{2,1,0:T(8,128)(2,1)S(1)}, bf16[4,320,128]{2,1,0:T(8,128)(2,1)S(1)}, u32[]{:S(2)}, u32[]{:S(2)}) collective-permute-start(bf16[4,320,128]{2,1,0:T(8,128)(2,1)S(1)} %get-tuple-element.29), channel_id=1, source_target_pairs={{0,384},{16,144},{128,256},{144,16},{256,128},{272,400},{384,0},{4... | collective-permute-start | bytes 983048 | tf_op jit(solution)/shard_map/ppermute | solution.py:246
  90.1 11.1 %collective-permute-start.11 = (bf16[4,320,128]{2,1,0:T(8,128)(2,1)S(1)}, bf16[4,320,128]{2,1,0:T(8,128)(2,1)S(1)}, u32[]{:S(2)}, u32[]{:S(2)}) collective-permute-start(bf16[4,320,128]{2,1,0:T(8,128)(2,1)S(1)} %get-tuple-element.30), channel_id=1, source_target_pairs={{0,384},{16,144},{128,256},{144,16},{256,128},{272,400},{384,0},{4... | collective-permute-start | bytes 983048 | tf_op jit(solution)/shard_map/ppermute | solution.py:246
  97.2 9.0 %collective-permute-start.10 = (bf16[4,320,128]{2,1,0:T(8,128)(2,1)S(1)}, bf16[4,320,128]{2,1,0:T(8,128)(2,1)S(1)}, u32[]{:S(2)}, u32[]{:S(2)}) collective-permute-start(bf16[4,320,128]{2,1,0:T(8,128)(2,1)S(1)} %shard_map.91.refs_7_), channel_id=1, source_target_pairs={{0,128},{16,400},{128,0},{144,272},{256,384},{272,144},{384,256},{... | collective-permute-start | bytes 983048 | tf_op jit(solution)/shard_map/ppermute | solution.py:246
  107.0 12.3 %all-to-all-start.1 = ((bf16[4,320,128]{2,1,0:T(8,128)(2,1)}), bf16[4,320,128]{2,1,0:T(8,128)(2,1)S(1)}, u32[]{:S(2)}, u32[]{:S(2)}) async-start(bf16[4,320,128]{2,1,0:T(8,128)(2,1)} %shard_map.93), calls=%async_computation.1 | async-start | bytes 655360 | tf_op jit(solution)/shard_map/all_to_all | solution.py:292
  110.5 15.2 %collective-permute-start.13 = (bf16[16,128,128]{2,1,0:T(8,128)(2,1)S(1)}, bf16[16,128,128]{2,1,0:T(8,128)(2,1)S(1)}, u32[]{:S(2)}, u32[]{:S(2)}) collective-permute-start(bf16[16,128,128]{2,1,0:T(8,128)(2,1)S(1)} %get-tuple-element.34), channel_id=1, source_target_pairs={{0,16},{16,0},{1,17},{17,1},{2,18},{18,2},{3,19},{19,3},{4,20},{20... | collective-permute-start | bytes 1572872 | tf_op jit(solution)/shard_map/ppermute | solution.py:250
  112.4 13.3 %collective-permute-start.12 = (bf16[16,128,128]{2,1,0:T(8,128)(2,1)S(1)}, bf16[16,128,128]{2,1,0:T(8,128)(2,1)S(1)}, u32[]{:S(2)}, u32[]{:S(2)}) collective-permute-start(bf16[16,128,128]{2,1,0:T(8,128)(2,1)S(1)} %get-tuple-element.31.after_ref), channel_id=1, source_target_pairs={{0,16},{16,0},{1,17},{17,1},{2,18},{18,2},{3,19},{19,3},{4,20},{20... | collective-permute-start | bytes 1572872 | tf_op jit(solution)/shard_map/ppermute | solution.py:250
  120.0 19.2 %all-to-all-start.2 = ((bf16[16,20,128]{2,1,0:T(8,128)(2,1)}), bf16[16,20,128]{2,1,0:T(8,128)(2,1)S(1)}, u32[]{:S(2)}, u32[]{:S(2)}) async-start(bf16[16,20,128]{2,1,0:T(8,128)(2,1)} %shard_map.94.after_ref), calls=%async_computation.2 | async-start | bytes 196608 | tf_op jit(solution)/shard_map/all_to_all | solution.py:295

commit v5 on v4

--- a/solution.py
+++ b/solution.py
@@ -262,8 +262,8 @@
     )
     in_sib, out_sib = across(in_other), across(out_other)
     received = lax.all_to_all(send, ("zh", "x"), 0, 0, tiled=True)
-    received, in_sib, out_sib = lax.optimization_barrier((received, in_sib, out_sib))
     own = lax.all_gather(received, "zl", axis=0, tiled=True)
+    own, in_sib, out_sib = lax.optimization_barrier((own, in_sib, out_sib))
     weights = (w_in, w_out, keep(in_sib), keep(out_sib))
     cut = NZ // 2 * EXPERTS
     low, high = own[:cut], own[cut:]

time: 141 us -> 141 us (level)
    ppermute x5, waiting for transfers between devices: 3.11 us -> 1.61 us  [across(): return lax.ppermute(value, 'c', [(0, 1), (1, 0)])]
  transfers between devices with their start and end apart: 17 -> 17, of which waited for: 11 -> 10; matrix products, arithmetic and copies ran while one was open for 0% -> 0% of each run, Pallas kernels for 6% -> 6%
where the time goes in v5:
time: 141 us; the launch traced here: 140 us
  starting transfers between devices  65.1 us (46%)
  waiting for transfers between devices  42.3 us (30%)
  blocking collectives  17.3 us (12%)
  Pallas kernels  14.3 us (10%)
    ppermute x9, starting transfers between devices, partner(): lax.ppermute(value, ('y', 'c'), [(i * NC + c, to[c][which][i] * NC + c) f...  27.3 us
    all_to_all x1, starting transfers between devices, on_device(): received = lax.all_to_all(send, ('zh', 'x'), 0, 0, tiled=True)  18.1 us
    all_gather x1, blocking collectives, on_device(): own = lax.all_gather(received, 'zl', axis=0, tiled=True)  17.3 us
    ppermute x9, waiting for transfers between devices, partner(): lax.ppermute(value, ('y', 'c'), [(i * NC + c, to[c][which][i] * NC + c) f...  15.9 us
    pallas_call x13, Pallas kernels, run(): pl.pallas_call(kernel, out_shape=outs, in_specs=specs, out_specs=out_spec...  14.3 us
    all_to_all x1, waiting for transfers between devices, on_device(): back = lax.all_to_all(total, ('zh', 'x'), 0, 0, tiled=True)  10.9 us
    ppermute x5, starting transfers between devices, across(): return lax.ppermute(value, 'c', [(0, 1), (1, 0)])  10.7 us
    all_to_all x1, waiting for transfers between devices, on_device(): received = lax.all_to_all(send, ('zh', 'x'), 0, 0, tiled=True)  9.31 us
  transfers between devices with their start and end apart: 17, of which 10 were waited for; matrix products, arithmetic and copies ran while one was open for 0% of the time, Pallas kernels for 6%

profile of v5, /device:TPU:2, one launch (start us, length us, event | category | flops | bytes accessed | tf_op | source)
XLA Modules:
  0.0 140.0 jit_solution(11972908808212452177)
XLA Ops:
  0.6 2.0 %shard_map.85.after_ref = bf16[16,40,128]{2,1,0:T(8,128)(2,1)} custom-call(s32[2,128]{1,0:T(2,128)} %bitcast.16, f32[2,128]{1,0:T(2,128)} %bitcast.18, bf16[128,128]{1,0:T(8,128)(2,1)} %tok_ref.1, bf16[128,128]{1,0:T(8,128)(2,1)} %dy_ref.1), custom_call_target="tpu_custom_call" | custom-call | tf_op jit(solution)/shard_map/pallas_call | solution.py:238
  2.6 18.1 %all-to-all-start = ((bf16[16,40,128]{2,1,0:T(8,128)(2,1)}), bf16[16,40,128]{2,1,0:T(8,128)(2,1)S(1)}, u32[]{:S(2)}, u32[]{:S(2)}) async-start(bf16[16,40,128]{2,1,0:T(8,128)(2,1)} %shard_map.85.after_ref), calls=%async_computation | async-start | bytes 327680 | tf_op jit(solution)/shard_map/all_to_all | solution.py:264
  20.7 2.2 %shard_map.86 = (bf16[16,128,128]{2,1,0:T(8,128)(2,1)}, bf16[16,128,128]{2,1,0:T(8,128)(2,1)}) custom-call(bf16[16,2,128,128]{3,2,1,0:T(8,128)(2,1)} %bitcast.7, bf16[128,4096]{1,0:T(8,128)(2,1)} %bitcast.12, bf16[16,40,128]{2,1,0:T(8,128)(2,1)} %shard_map.85.after_ref), custom_call_target="tpu_custom_call" | custom-call | tf_op jit(solution)/shard_map/pallas_call | solution.py:238
  22.9 1.9 %collective-permute-start = (bf16[16,128,128]{2,1,0:T(8,128)(2,1)}, bf16[16,128,128]{2,1,0:T(8,128)(2,1)S(1)}, u32[]{:S(2)}, u32[]{:S(2)}) collective-permute-start(bf16[16,128,128]{2,1,0:T(8,128)(2,1)} %get-tuple-element.20), channel_id=1, source_target_pairs={{0,16},{16,0},{1,17},{17,1},{2,18},{18,2},{3,19},{19,3},{4,20},{20... | collective-permute-start | bytes 1572872 | tf_op jit(solution)/shard_map/ppermute | solution.py:250
  24.9 0.0 copy-start
  24.9 0.0 copy-start.1
  24.9 2.5 %collective-permute-start.1 = (bf16[16,128,128]{2,1,0:T(8,128)(2,1)}, bf16[16,128,128]{2,1,0:T(8,128)(2,1)S(1)}, u32[]{:S(2)}, u32[]{:S(2)}) collective-permute-start(bf16[16,128,128]{2,1,0:T(8,128)(2,1)} %get-tuple-element.21), channel_id=1, source_target_pairs={{0,16},{16,0},{1,17},{17,1},{2,18},{18,2},{3,19},{19,3},{4,20},{20... | collective-permute-start | bytes 1572872 | tf_op jit(solution)/shard_map/ppermute | solution.py:250
  27.4 9.3 %all-to-all-done = bf16[16,40,128]{2,1,0:T(8,128)(2,1)S(1)} async-done(((bf16[16,40,128]{2,1,0:T(8,128)(2,1)}), bf16[16,40,128]{2,1,0:T(8,128)(2,1)S(1)}, u32[]{:S(2)}, u32[]{:S(2)}) %all-to-all-start) | async-done | bytes 163872 | tf_op jit(solution)/shard_map/all_to_all | solution.py:264
  36.7 17.3 %all_gather.3.own.refs_0_ = bf16[64,40,128]{2,1,0:T(8,128)(2,1)S(1)} all-gather(bf16[16,40,128]{2,1,0:T(8,128)(2,1)S(1)} %all-to-all-done), channel_id=1, replica_groups=mesh['y'=4,'zl'=4,'c'=2,'zh'=4,'x'=4] {'zl'}, dimensions={0}, use_global_device_ids=true | all-gather | bytes 819200 | tf_op jit(solution)/shard_map/all_gather | solution.py:265
  54.1 0.1 fusion
  54.1 4.9 %collective-permute-start.4 = (bf16[32,40,128]{2,1,0:T(8,128)(2,1)S(1)}, bf16[32,40,128]{2,1,0:T(8,128)(2,1)S(1)}, u32[]{:S(2)}, u32[]{:S(2)}) collective-permute-start(bf16[32,40,128]{2,1,0:T(8,128)(2,1)S(1)} %get-tuple-element.37), channel_id=1, source_target_pairs={{0,384},{16,144},{128,256},{144,16},{256,128},{272,400},{384,0},{4... | collective-permute-start | bytes 983048 | tf_op jit(solution)/shard_map/ppermute | solution.py:246
  59.1 2.0 %collective-permute-start.2 = (bf16[32,40,128]{2,1,0:T(8,128)(2,1)S(1)}, bf16[32,40,128]{2,1,0:T(8,128)(2,1)S(1)}, u32[]{:S(2)}, u32[]{:S(2)}) collective-permute-start(bf16[32,40,128]{2,1,0:T(8,128)(2,1)S(1)} %get-tuple-element.38), channel_id=1, source_target_pairs={{0,128},{16,400},{128,0},{144,272},{256,384},{272,144},{384,256},{... | collective-permute-start | bytes 983048 | tf_op jit(solution)/shard_map/ppermute | solution.py:246
  61.1 3.8 %collective-permute-start.7 = (bf16[32,40,128]{2,1,0:T(8,128)(2,1)S(1)}, bf16[32,40,128]{2,1,0:T(8,128)(2,1)S(1)}, u32[]{:S(2)}, u32[]{:S(2)}) collective-permute-start(bf16[32,40,128]{2,1,0:T(8,128)(2,1)S(1)} %get-tuple-element.37), channel_id=1, source_target_pairs={{0,128},{16,400},{128,0},{144,272},{256,384},{272,144},{384,256},{... | collective-permute-start | bytes 983048 | tf_op jit(solution)/shard_map/ppermute | solution.py:246
  64.9 2.1 %collective-permute-start.6 = (bf16[32,40,128]{2,1,0:T(8,128)(2,1)S(1)}, bf16[32,40,128]{2,1,0:T(8,128)(2,1)S(1)}, u32[]{:S(2)}, u32[]{:S(2)}) collective-permute-start(bf16[32,40,128]{2,1,0:T(8,128)(2,1)S(1)} %get-tuple-element.38), channel_id=1, source_target_pairs={{0,384},{16,144},{128,256},{144,16},{256,128},{272,400},{384,0},{4... | collective-permute-start | bytes 983048 | tf_op jit(solution)/shard_map/ppermute | solution.py:246
  67.1 0.8 collective-permute-done.4.second_b.refs_4_
  67.9 2.3 %collective-permute-start.5 = (bf16[32,40,128]{2,1,0:T(8,128)(2,1)S(1)}, bf16[32,40,128]{2,1,0:T(8,128)(2,1)S(1)}, u32[]{:S(2)}, u32[]{:S(2)}) collective-permute-start(bf16[32,40,128]{2,1,0:T(8,128)(2,1)S(1)} %collective-permute-done.4.second_b.refs_4_), channel_id=1, source_target_pairs={{0,128},{16,400},{128,0},{144,272},{256,384},{272,144},{384,256},{... | collective-permute-start | bytes 983048 | tf_op jit(solution)/shard_map/ppermute | solution.py:246
  70.2 1.4 collective-permute-done.2.first_a.refs_1_
  71.5 3.2 %collective-permute-start.3 = (bf16[32,40,128]{2,1,0:T(8,128)(2,1)S(1)}, bf16[32,40,128]{2,1,0:T(8,128)(2,1)S(1)}, u32[]{:S(2)}, u32[]{:S(2)}) collective-permute-start(bf16[32,40,128]{2,1,0:T(8,128)(2,1)S(1)} %collective-permute-done.2.first_a.refs_1_), channel_id=1, source_target_pairs={{0,384},{16,144},{128,256},{144,16},{256,128},{272,400},{384,0},{4... | collective-permute-start | bytes 983048 | tf_op jit(solution)/shard_map/ppermute | solution.py:246
  74.7 3.5 %collective-permute-done.7.first_b.refs_2_ = bf16[32,40,128]{2,1,0:T(8,128)(2,1)S(1)} collective-permute-done((bf16[32,40,128]{2,1,0:T(8,128)(2,1)S(1)}, bf16[32,40,128]{2,1,0:T(8,128)(2,1)S(1)}, u32[]{:S(2)}, u32[]{:S(2)}) %collective-permute-start.7) | collective-permute-done | bytes 327712 | tf_op jit(solution)/shard_map/ppermute | solution.py:246
  78.3 0.9 shard_map.87.before_ref
  79.2 0.0 collective-permute-done.6.second_a.refs_3_
  79.2 0.5 shard_map.88.before_ref
  79.7 2.1 %collective-permute-done.5.last_b.refs_6_ = bf16[32,40,128]{2,1,0:T(8,128)(2,1)S(1)} collective-permute-done((bf16[32,40,128]{2,1,0:T(8,128)(2,1)S(1)}, bf16[32,40,128]{2,1,0:T(8,128)(2,1)S(1)}, u32[]{:S(2)}, u32[]{:S(2)}) %collective-permute-start.5) | collective-permute-done | bytes 327712 | tf_op jit(solution)/shard_map/ppermute | solution.py:246
  81.8 0.0 collective-permute-done.3.last_a.refs_5_
  81.8 0.5 shard_map.89
  82.3 1.9 %collective-permute-start.8 = (bf16[640,256]{1,0:T(8,128)(2,1)S(1)}, bf16[640,256]{1,0:T(8,128)(2,1)S(1)}, u32[]{:S(2)}, u32[]{:S(2)}) collective-permute-start(bf16[640,256]{1,0:T(8,128)(2,1)S(1)} %get-tuple-element.26), channel_id=1, source_target_pairs={{0,16},{16,0},{1,17},{17,1},{2,18},{18,2},{3,19},{19,3},{4,20},{20... | collective-permute-start | bytes 983048 | tf_op jit(solution)/shard_map/ppermute | solution.py:250
  84.3 1.6 %collective-permute-done.8.part_sib_ref = bf16[640,256]{1,0:T(8,128)(2,1)S(1)} collective-permute-done((bf16[640,256]{1,0:T(8,128)(2,1)S(1)}, bf16[640,256]{1,0:T(8,128)(2,1)S(1)}, u32[]{:S(2)}, u32[]{:S(2)}) %collective-permute-start.8) | collective-permute-done | bytes 327712 | tf_op jit(solution)/shard_map/ppermute | solution.py:250
  85.8 1.1 shard_map.90
  87.0 3.1 %collective-permute-start.9 = (bf16[4,320,128]{2,1,0:T(8,128)(2,1)S(1)}, bf16[4,320,128]{2,1,0:T(8,128)(2,1)S(1)}, u32[]{:S(2)}, u32[]{:S(2)}) collective-permute-start(bf16[4,320,128]{2,1,0:T(8,128)(2,1)S(1)} %get-tuple-element.29), channel_id=1, source_target_pairs={{0,384},{16,144},{128,256},{144,16},{256,128},{272,400},{384,0},{4... | collective-permute-start | bytes 983048 | tf_op jit(solution)/shard_map/ppermute | solution.py:246
  90.1 3.9 %collective-permute-start.11 = (bf16[4,320,128]{2,1,0:T(8,128)(2,1)S(1)}, bf16[4,320,128]{2,1,0:T(8,128)(2,1)S(1)}, u32[]{:S(2)}, u32[]{:S(2)}) collective-permute-start(bf16[4,320,128]{2,1,0:T(8,128)(2,1)S(1)} %get-tuple-element.30), channel_id=1, source_target_pairs={{0,384},{16,144},{128,256},{144,16},{256,128},{272,400},{384,0},{4... | collective-permute-start | bytes 983048 | tf_op jit(solution)/shard_map/ppermute | solution.py:246
  94.0 3.1 %collective-permute-done.9.passed_ref = bf16[4,320,128]{2,1,0:T(8,128)(2,1)S(1)} collective-permute-done((bf16[4,320,128]{2,1,0:T(8,128)(2,1)S(1)}, bf16[4,320,128]{2,1,0:T(8,128)(2,1)S(1)}, u32[]{:S(2)}, u32[]{:S(2)}) %collective-permute-start.9) | collective-permute-done | bytes 327712 | tf_op jit(solution)/shard_map/ppermute | solution.py:246
  97.1 0.1 shard_map.91.refs_7_
  97.2 1.9 %collective-permute-start.10 = (bf16[4,320,128]{2,1,0:T(8,128)(2,1)S(1)}, bf16[4,320,128]{2,1,0:T(8,128)(2,1)S(1)}, u32[]{:S(2)}, u32[]{:S(2)}) collective-permute-start(bf16[4,320,128]{2,1,0:T(8,128)(2,1)S(1)} %shard_map.91.refs_7_), channel_id=1, source_target_pairs={{0,128},{16,400},{128,0},{144,272},{256,384},{272,144},{384,256},{... | collective-permute-start | bytes 983048 | tf_op jit(solution)/shard_map/ppermute | solution.py:246
  99.2 2.0 %shard_map.92 = (bf16[16,128,128]{2,1,0:T(8,128)(2,1)S(1)}, bf16[128,2048]{1,0:T(8,128)(2,1)S(1)}, bf16[16,128,128]{2,1,0:T(8,128)(2,1)S(1)}, bf16[16,128,128]{2,1,0:T(8,128)(2,1)S(1)}) custom-call(f32[640,256]{1,0:T(8,128)S(1)} %get-tuple-element.25.part_ref, bf16[640,256]{1,0:T(8,128)(2,1)S(1)} %collective-permute-done.8.part_sib_ref, ...), custom_call_target="tpu_custom_call" | custom-call | tf_op jit(solution)/shard_map/pallas_call | solution.py:238
  101.2 0.0 collective-permute-done.11.second_ref
  101.2 5.0 %collective-permute-done.10.first_ref = bf16[4,320,128]{2,1,0:T(8,128)(2,1)S(1)} collective-permute-done((bf16[4,320,128]{2,1,0:T(8,128)(2,1)S(1)}, bf16[4,320,128]{2,1,0:T(8,128)(2,1)S(1)}, u32[]{:S(2)}, u32[]{:S(2)}) %collective-permute-start.10) | collective-permute-done | bytes 327712 | tf_op jit(solution)/shard_map/ppermute | solution.py:246
  106.2 0.8 shard_map.93
  107.0 3.5 %all-to-all-start.1 = ((bf16[4,320,128]{2,1,0:T(8,128)(2,1)}), bf16[4,320,128]{2,1,0:T(8,128)(2,1)S(1)}, u32[]{:S(2)}, u32[]{:S(2)}) async-start(bf16[4,320,128]{2,1,0:T(8,128)(2,1)} %shard_map.93), calls=%async_computation.1 | async-start | bytes 655360 | tf_op jit(solution)/shard_map/all_to_all | solution.py:292
  110.5 1.9 %collective-permute-start.13 = (bf16[16,128,128]{2,1,0:T(8,128)(2,1)S(1)}, bf16[16,128,128]{2,1,0:T(8,128)(2,1)S(1)}, u32[]{:S(2)}, u32[]{:S(2)}) collective-permute-start(bf16[16,128,128]{2,1,0:T(8,128)(2,1)S(1)} %get-tuple-element.34), channel_id=1, source_target_pairs={{0,16},{16,0},{1,17},{17,1},{2,18},{18,2},{3,19},{19,3},{4,20},{20... | collective-permute-start | bytes 1572872 | tf_op jit(solution)/shard_map/ppermute | solution.py:250
  112.4 2.4 %collective-permute-start.12 = (bf16[16,128,128]{2,1,0:T(8,128)(2,1)S(1)}, bf16[16,128,128]{2,1,0:T(8,128)(2,1)S(1)}, u32[]{:S(2)}, u32[]{:S(2)}) collective-permute-start(bf16[16,128,128]{2,1,0:T(8,128)(2,1)S(1)} %get-tuple-element.31.after_ref), channel_id=1, source_target_pairs={{0,16},{16,0},{1,17},{17,1},{2,18},{18,2},{3,19},{19,3},{4,20},{20... | collective-permute-start | bytes 1572872 | tf_op jit(solution)/shard_map/ppermute | solution.py:250
  114.8 4.5 %all-to-all-done.1.parts_ref = bf16[4,320,128]{2,1,0:T(8,128)(2,1)S(1)} async-done(((bf16[4,320,128]{2,1,0:T(8,128)(2,1)}), bf16[4,320,128]{2,1,0:T(8,128)(2,1)S(1)}, u32[]{:S(2)}, u32[]{:S(2)}) %all-to-all-start.1) | async-done | bytes 327712 | tf_op jit(solution)/shard_map/all_to_all | solution.py:292
  119.3 0.7 shard_map.94.after_ref
  120.0 5.6 %all-to-all-start.2 = ((bf16[16,20,128]{2,1,0:T(8,128)(2,1)}), bf16[16,20,128]{2,1,0:T(8,128)(2,1)S(1)}, u32[]{:S(2)}, u32[]{:S(2)}) async-start(bf16[16,20,128]{2,1,0:T(8,128)(2,1)} %shard_map.94.after_ref), calls=%async_computation.2 | async-start | bytes 196608 | tf_op jit(solution)/shard_map/all_to_all | solution.py:295
  125.6 0.0 collective-permute-done.13.out_sib
  125.6 1.6 %shard_map.97 = (bf16[4096,128]{1,0:T(8,128)(2,1)}, bf16[128,4096]{1,0:T(8,128)(2,1)}) custom-call(bf16[16,128,128]{2,1,0:T(8,128)(2,1)S(1)} %get-tuple-element.32.in_mine, bf16[128,2048]{1,0:T(8,128)(2,1)S(1)} %get-tuple-element.33.out_mine, bf16[16,128,128]{2,1,0:T(8,128)(2,1)S(1)} %collective-permute-done.12.in_sib, ...), custom_call_target="tpu_custom_call" | custom-call | tf_op jit(solution)/shard_map/pallas_call | solution.py:238
  127.2 1.0 shard_map.95.table_ref
  128.2 10.9 %all-to-all-done.2.back_ref = bf16[16,20,128]{2,1,0:T(8,128)(2,1)S(1)} async-done(((bf16[16,20,128]{2,1,0:T(8,128)(2,1)}), bf16[16,20,128]{2,1,0:T(8,128)(2,1)S(1)}, u32[]{:S(2)}, u32[]{:S(2)}) %all-to-all-start.2) | async-done | bytes 81952 | tf_op jit(solution)/shard_map/all_to_all | solution.py:295
  139.1 0.8 shard_map.96
  (5 shorter events, 0.0 us)
Async XLA Ops:
  2.6 34.1 %all-to-all-start = ((bf16[16,40,128]{2,1,0:T(8,128)(2,1)}), bf16[16,40,128]{2,1,0:T(8,128)(2,1)S(1)}, u32[]{:S(2)}, u32[]{:S(2)}) async-start(bf16[16,40,128]{2,1,0:T(8,128)(2,1)} %shard_map.85.after_ref), calls=%async_computation | async-start | bytes 327680 | tf_op jit(solution)/shard_map/all_to_all | solution.py:264
  22.9 31.1 %collective-permute-start = (bf16[16,128,128]{2,1,0:T(8,128)(2,1)}, bf16[16,128,128]{2,1,0:T(8,128)(2,1)S(1)}, u32[]{:S(2)}, u32[]{:S(2)}) collective-permute-start(bf16[16,128,128]{2,1,0:T(8,128)(2,1)} %get-tuple-element.20), channel_id=1, source_target_pairs={{0,16},{16,0},{1,17},{17,1},{2,18},{18,2},{3,19},{19,3},{4,20},{20... | collective-permute-start | bytes 1572872 | tf_op jit(solution)/shard_map/ppermute | solution.py:250
  24.9 53.4 %copy-start = (bf16[1,4096,128]{2,1,0:T(8,128)(2,1)S(1)}, bf16[1,4096,128]{2,1,0:T(8,128)(2,1)}, u32[]{:S(2)}) copy-start(bf16[1,4096,128]{2,1,0:T(8,128)(2,1)} %param.10) | copy-start | bytes 3145732
  24.9 53.4 %copy-start.1 = (bf16[1,128,4096]{2,1,0:T(8,128)(2,1)S(1)}, bf16[1,128,4096]{2,1,0:T(8,128)(2,1)}, u32[]{:S(2)}) copy-start(bf16[1,128,4096]{2,1,0:T(8,128)(2,1)} %param.11) | copy-start | bytes 3145732
  24.9 29.2 %collective-permute-start.1 = (bf16[16,128,128]{2,1,0:T(8,128)(2,1)}, bf16[16,128,128]{2,1,0:T(8,128)(2,1)S(1)}, u32[]{:S(2)}, u32[]{:S(2)}) collective-permute-start(bf16[16,128,128]{2,1,0:T(8,128)(2,1)} %get-tuple-element.21), channel_id=1, source_target_pairs={{0,16},{16,0},{1,17},{17,1},{2,18},{18,2},{3,19},{19,3},{4,20},{20... | collective-permute-start | bytes 1572872 | tf_op jit(solution)/shard_map/ppermute | solution.py:250
  54.1 13.8 %collective-permute-start.4 = (bf16[32,40,128]{2,1,0:T(8,128)(2,1)S(1)}, bf16[32,40,128]{2,1,0:T(8,128)(2,1)S(1)}, u32[]{:S(2)}, u32[]{:S(2)}) collective-permute-start(bf16[32,40,128]{2,1,0:T(8,128)(2,1)S(1)} %get-tuple-element.37), channel_id=1, source_target_pairs={{0,384},{16,144},{128,256},{144,16},{256,128},{272,400},{384,0},{4... | collective-permute-start | bytes 983048 | tf_op jit(solution)/shard_map/ppermute | solution.py:246
  59.1 12.5 %collective-permute-start.2 = (bf16[32,40,128]{2,1,0:T(8,128)(2,1)S(1)}, bf16[32,40,128]{2,1,0:T(8,128)(2,1)S(1)}, u32[]{:S(2)}, u32[]{:S(2)}) collective-permute-start(bf16[32,40,128]{2,1,0:T(8,128)(2,1)S(1)} %get-tuple-element.38), channel_id=1, source_target_pairs={{0,128},{16,400},{128,0},{144,272},{256,384},{272,144},{384,256},{... | collective-permute-start | bytes 983048 | tf_op jit(solution)/shard_map/ppermute | solution.py:246
  61.1 17.2 %collective-permute-start.7 = (bf16[32,40,128]{2,1,0:T(8,128)(2,1)S(1)}, bf16[32,40,128]{2,1,0:T(8,128)(2,1)S(1)}, u32[]{:S(2)}, u32[]{:S(2)}) collective-permute-start(bf16[32,40,128]{2,1,0:T(8,128)(2,1)S(1)} %get-tuple-element.37), channel_id=1, source_target_pairs={{0,128},{16,400},{128,0},{144,272},{256,384},{272,144},{384,256},{... | collective-permute-start | bytes 983048 | tf_op jit(solution)/shard_map/ppermute | solution.py:246
  64.9 14.2 %collective-permute-start.6 = (bf16[32,40,128]{2,1,0:T(8,128)(2,1)S(1)}, bf16[32,40,128]{2,1,0:T(8,128)(2,1)S(1)}, u32[]{:S(2)}, u32[]{:S(2)}) collective-permute-start(bf16[32,40,128]{2,1,0:T(8,128)(2,1)S(1)} %get-tuple-element.38), channel_id=1, source_target_pairs={{0,384},{16,144},{128,256},{144,16},{256,128},{272,400},{384,0},{4... | collective-permute-start | bytes 983048 | tf_op jit(solution)/shard_map/ppermute | solution.py:246
  67.9 13.9 %collective-permute-start.5 = (bf16[32,40,128]{2,1,0:T(8,128)(2,1)S(1)}, bf16[32,40,128]{2,1,0:T(8,128)(2,1)S(1)}, u32[]{:S(2)}, u32[]{:S(2)}) collective-permute-start(bf16[32,40,128]{2,1,0:T(8,128)(2,1)S(1)} %collective-permute-done.4.second_b.refs_4_), channel_id=1, source_target_pairs={{0,128},{16,400},{128,0},{144,272},{256,384},{272,144},{384,256},{... | collective-permute-start | bytes 983048 | tf_op jit(solution)/shard_map/ppermute | solution.py:246
  71.5 10.3 %collective-permute-start.3 = (bf16[32,40,128]{2,1,0:T(8,128)(2,1)S(1)}, bf16[32,40,128]{2,1,0:T(8,128)(2,1)S(1)}, u32[]{:S(2)}, u32[]{:S(2)}) collective-permute-start(bf16[32,40,128]{2,1,0:T(8,128)(2,1)S(1)} %collective-permute-done.2.first_a.refs_1_), channel_id=1, source_target_pairs={{0,384},{16,144},{128,256},{144,16},{256,128},{272,400},{384,0},{4... | collective-permute-start | bytes 983048 | tf_op jit(solution)/shard_map/ppermute | solution.py:246
  82.3 3.5 %collective-permute-start.8 = (bf16[640,256]{1,0:T(8,128)(2,1)S(1)}, bf16[640,256]{1,0:T(8,128)(2,1)S(1)}, u32[]{:S(2)}, u32[]{:S(2)}) collective-permute-start(bf16[640,256]{1,0:T(8,128)(2,1)S(1)} %get-tuple-element.26), channel_id=1, source_target_pairs={{0,16},{16,0},{1,17},{17,1},{2,18},{18,2},{3,19},{19,3},{4,20},{20... | collective-permute-start | bytes 983048 | tf_op jit(solution)/shard_map/ppermute | solution.py:250
  87.0 10.2 %collective-permute-start.9 = (bf16[4,320,128]{2,1,0:T(8,128)(2,1)S(1)}, bf16[4,320,128]{2,1,0:T(8,128)(2,1)S(1)}, u32[]{:S(2)}, u32[]{:S(2)}) collective-permute-start(bf16[4,320,128]{2,1,0:T(8,128)(2,1)S(1)} %get-tuple-element.29), channel_id=1, source_target_pairs={{0,384},{16,144},{128,256},{144,16},{256,128},{272,400},{384,0},{4... | collective-permute-start | bytes 983048 | tf_op jit(solution)/shard_map/ppermute | solution.py:246
  90.1 11.1 %collective-permute-start.11 = (bf16[4,320,128]{2,1,0:T(8,128)(2,1)S(1)}, bf16[4,320,128]{2,1,0:T(8,128)(2,1)S(1)}, u32[]{:S(2)}, u32[]{:S(2)}) collective-permute-start(bf16[4,320,128]{2,1,0:T(8,128)(2,1)S(1)} %get-tuple-element.30), channel_id=1, source_target_pairs={{0,384},{16,144},{128,256},{144,16},{256,128},{272,400},{384,0},{4... | collective-permute-start | bytes 983048 | tf_op jit(solution)/shard_map/ppermute | solution.py:246
  97.2 9.0 %collective-permute-start.10 = (bf16[4,320,128]{2,1,0:T(8,128)(2,1)S(1)}, bf16[4,320,128]{2,1,0:T(8,128)(2,1)S(1)}, u32[]{:S(2)}, u32[]{:S(2)}) collective-permute-start(bf16[4,320,128]{2,1,0:T(8,128)(2,1)S(1)} %shard_map.91.refs_7_), channel_id=1, source_target_pairs={{0,128},{16,400},{128,0},{144,272},{256,384},{272,144},{384,256},{... | collective-permute-start | bytes 983048 | tf_op jit(solution)/shard_map/ppermute | solution.py:246
  107.0 12.3 %all-to-all-start.1 = ((bf16[4,320,128]{2,1,0:T(8,128)(2,1)}), bf16[4,320,128]{2,1,0:T(8,128)(2,1)S(1)}, u32[]{:S(2)}, u32[]{:S(2)}) async-start(bf16[4,320,128]{2,1,0:T(8,128)(2,1)} %shard_map.93), calls=%async_computation.1 | async-start | bytes 655360 | tf_op jit(solution)/shard_map/all_to_all | solution.py:292
  110.5 15.1 %collective-permute-start.13 = (bf16[16,128,128]{2,1,0:T(8,128)(2,1)S(1)}, bf16[16,128,128]{2,1,0:T(8,128)(2,1)S(1)}, u32[]{:S(2)}, u32[]{:S(2)}) collective-permute-start(bf16[16,128,128]{2,1,0:T(8,128)(2,1)S(1)} %get-tuple-element.34), channel_id=1, source_target_pairs={{0,16},{16,0},{1,17},{17,1},{2,18},{18,2},{3,19},{19,3},{4,20},{20... | collective-permute-start | bytes 1572872 | tf_op jit(solution)/shard_map/ppermute | solution.py:250
  112.4 13.2 %collective-permute-start.12 = (bf16[16,128,128]{2,1,0:T(8,128)(2,1)S(1)}, bf16[16,128,128]{2,1,0:T(8,128)(2,1)S(1)}, u32[]{:S(2)}, u32[]{:S(2)}) collective-permute-start(bf16[16,128,128]{2,1,0:T(8,128)(2,1)S(1)} %get-tuple-element.31.after_ref), channel_id=1, source_target_pairs={{0,16},{16,0},{1,17},{17,1},{2,18},{18,2},{3,19},{19,3},{4,20},{20... | collective-permute-start | bytes 1572872 | tf_op jit(solution)/shard_map/ppermute | solution.py:250
  120.0 19.1 %all-to-all-start.2 = ((bf16[16,20,128]{2,1,0:T(8,128)(2,1)}), bf16[16,20,128]{2,1,0:T(8,128)(2,1)S(1)}, u32[]{:S(2)}, u32[]{:S(2)}) async-start(bf16[16,20,128]{2,1,0:T(8,128)(2,1)} %shard_map.94.after_ref), calls=%async_computation.2 | async-start | bytes 196608 | tf_op jit(solution)/shard_map/all_to_all | solution.py:295

commit v6 on v5

--- a/solution.py
+++ b/solution.py
@@ -37,13 +37,22 @@
 
 def dispatch_kernel(ids_ref, gate_ref, tok_ref, dy_ref, out_ref):
     ids = ids_ref[...]
-    table, expert, row = slot_table(ids, MSG, lambda q: jnp.where(q >= CAP, q - CAP, q))
-    gate = jnp.where(expert == ids[0:1, :], gate_ref[0:1, :], gate_ref[1:2, :])
-    scale = jnp.sum(jnp.where(table, gate, 0.0), axis=1, keepdims=True)
-    pick = table.astype(BF16)
+    experts = lax.broadcasted_iota(jnp.int32, (EXPERTS, TOK), 0)
+    first, second = experts == ids[0:1, :], experts == ids[1:2, :]
+    earlier = lax.broadcasted_iota(jnp.int32, (TOK, TOK), 0) < lax.broadcasted_iota(jnp.int32, (TOK, TOK), 1)
+    prior = jnp.dot((first | second).astype(BF16), earlier.astype(BF16), preferred_element_type=F32)
+    place = jnp.where(first | second, prior, -1.0)
+    gate = jnp.where(first, gate_ref[0:1, :], gate_ref[1:2, :])
+    shape = (EXPERTS, MSG, TOK)
+    row = lax.broadcasted_iota(jnp.int32, shape, 1)
+    slot = jnp.where(row >= CAP, row - CAP, row).astype(F32)
+    table = jnp.broadcast_to(place[:, None, :], shape) == slot
+    weight = jnp.where(table, jnp.broadcast_to(gate[:, None, :], shape), 0.0)
+    scale = jnp.sum(weight, axis=2, keepdims=True).reshape(ROWS, 1)
+    pick = jnp.where(table, 1.0, 0.0).reshape(ROWS, TOK).astype(BF16)
     rows_in = jnp.dot(pick, tok_ref[...], preferred_element_type=F32)
     rows_dy = jnp.dot(pick, dy_ref[...], preferred_element_type=F32)
-    out = jnp.where(row < CAP, rows_in, scale * rows_dy)
+    out = jnp.where(row.reshape(ROWS, COLS) < CAP, rows_in, scale * rows_dy)
     out_ref[...] = out.astype(BF16).reshape(EXPERTS, MSG, COLS)
 
 
@@ -144,19 +153,29 @@
     return jnp.where(row < CAP, pre_grad, 0.0).astype(BF16), jnp.where(row < CAP, 0.0, act).astype(BF16)
 
 
-def middle_kernel(w_in_ref, sib_ref, part_ref, part_sib_ref, *outs):
-    y, c = position()
+def partials(w_in_ref, sib_ref, pg, at, out_ref):
+    _, c = position()
+    for zl in range(0, NZ, 2):
+        w = jnp.concatenate([weights_in(w_in_ref, sib_ref, c, at * NZ + z) for z in (zl, zl + 1)], axis=0)
+        out = lax.dot_general(pg, w, CONTRACT_LAST, preferred_element_type=F32).astype(BF16)
+        for j in range(2):
+            out_ref[zl + j] = out[:, j * COLS:(j + 1) * COLS]
+
+
+def far_kernel(w_in_ref, sib_ref, part_ref, part_sib_ref, pg_ref, out_ref):
     pre_grad, _ = activations(part_ref, part_sib_ref)
     block = lax.broadcasted_iota(jnp.int32, (EXPERTS, CAP, ROWS), 0).reshape(KEPT, ROWS)
     within = lax.broadcasted_iota(jnp.int32, (EXPERTS, CAP, ROWS), 1).reshape(KEPT, ROWS)
     keep = (lax.broadcasted_iota(jnp.int32, (KEPT, ROWS), 1) == block * MSG + within).astype(BF16)
     pg = jnp.dot(keep, pre_grad, preferred_element_type=F32).astype(BF16)
-    for at, out_ref in zip(places(y, c), outs):
-        for zl in range(0, NZ, 2):
-            w = jnp.concatenate([weights_in(w_in_ref, sib_ref, c, at * NZ + z) for z in (zl, zl + 1)], axis=0)
-            out = lax.dot_general(pg, w, CONTRACT_LAST, preferred_element_type=F32).astype(BF16)
-            for j in range(2):
-                out_ref[zl + j] = out[:, j * COLS:(j + 1) * COLS]
+    pg_ref[...] = pg
+    partials(w_in_ref, sib_ref, pg, places(*position())[3], out_ref)
+
+
+def near_kernel(w_in_ref, sib_ref, pg_ref, *outs):
+    pg = pg_ref[...]
+    for at, out_ref in zip(places(*position()), outs):
+        partials(w_in_ref, sib_ref, pg, at, out_ref)
 
 
 def relay_kernel(mine_ref, passed_ref, out_ref):
@@ -279,9 +298,8 @@
     )
     rows = held(NZ, KEPT, COLS)
     parts = keep(mine), keep(across(sent))
-    to_own, to_first, to_second, to_last = run(
-        middle_kernel, (rows, rows, rows, rows), 0, w_in, keep(in_sib), *parts
-    )
+    pg, to_last = run(far_kernel, (held(KEPT, NC * HID), rows), 0, w_in, keep(in_sib), *parts)
+    to_own, to_first, to_second = run(near_kernel, (rows, rows, rows), 0, w_in, keep(in_sib), keep(pg))
     passed, from_second = partner(to_last, 1), partner(to_second, 1)
     relayed = run(relay_kernel, rows, 0, keep(to_first), keep(passed))
     from_first = partner(relayed, 0)

time: 141 us -> 140 us (level)
    pallas_call x13 -> x14, Pallas kernels: 14.3 us -> 14.4 us  [run(): pl.pallas_call(kernel, out_shape=outs, in_specs=specs, out_specs=out_spec...]
  transfers between devices with their start and end apart: 17 -> 17, of which waited for: 10 -> 10; matrix products, arithmetic and copies ran while one was open for 0% -> 0% of each run, Pallas kernels for 6% -> 7%
where the time goes in v6:
time: 140 us
  starting transfers between devices  65.2 us (47%)
  waiting for transfers between devices  41.8 us (30%)
  blocking collectives  17.3 us (12%)
  Pallas kernels  14.4 us (10%)
    ppermute x9, starting transfers between devices, partner(): lax.ppermute(value, ('y', 'c'), [(i * NC + c, to[c][which][i] * NC + c) f...  27.3 us
    all_to_all x1, starting transfers between devices, on_device(): received = lax.all_to_all(send, ('zh', 'x'), 0, 0, tiled=True)  18.1 us
    all_gather x1, blocking collectives, on_device(): own = lax.all_gather(received, 'zl', axis=0, tiled=True)  17.3 us
    ppermute x9, waiting for transfers between devices, partner(): lax.ppermute(value, ('y', 'c'), [(i * NC + c, to[c][which][i] * NC + c) f...  15.4 us
    pallas_call x14, Pallas kernels, run(): pl.pallas_call(kernel, out_shape=outs, in_specs=specs, out_specs=out_spec...  14.4 us
    all_to_all x1, waiting for transfers between devices, on_device(): back = lax.all_to_all(total, ('zh', 'x'), 0, 0, tiled=True)  10.9 us
    ppermute x5, starting transfers between devices, across(): return lax.ppermute(value, 'c', [(0, 1), (1, 0)])  10.7 us
    all_to_all x1, waiting for transfers between devices, on_device(): received = lax.all_to_all(send, ('zh', 'x'), 0, 0, tiled=True)  9.3 us
  transfers between devices with their start and end apart: 17, of which 10 were waited for; matrix products, arithmetic and copies ran while one was open for 0% of the time, Pallas kernels for 7%

profile of v6, /device:TPU:2, one launch (start us, length us, event | category | flops | bytes accessed | tf_op | source)
XLA Modules:
  0.0 139.6 jit_solution(449518321488790166)
XLA Ops:
  0.6 1.9 %shard_map.85.after_ref = bf16[16,40,128]{2,1,0:T(8,128)(2,1)} custom-call(s32[2,128]{1,0:T(2,128)} %bitcast.17, f32[2,128]{1,0:T(2,128)} %bitcast.19, bf16[128,128]{1,0:T(8,128)(2,1)} %tok_ref.1, bf16[128,128]{1,0:T(8,128)(2,1)} %dy_ref.1), custom_call_target="tpu_custom_call" | custom-call | tf_op jit(solution)/shard_map/pallas_call | solution.py:257
  2.5 18.1 %all-to-all-start = ((bf16[16,40,128]{2,1,0:T(8,128)(2,1)}), bf16[16,40,128]{2,1,0:T(8,128)(2,1)S(1)}, u32[]{:S(2)}, u32[]{:S(2)}) async-start(bf16[16,40,128]{2,1,0:T(8,128)(2,1)} %shard_map.85.after_ref), calls=%async_computation | async-start | bytes 327680 | tf_op jit(solution)/shard_map/all_to_all | solution.py:283
  20.6 2.2 %shard_map.86 = (bf16[16,128,128]{2,1,0:T(8,128)(2,1)}, bf16[16,128,128]{2,1,0:T(8,128)(2,1)}) custom-call(bf16[16,2,128,128]{3,2,1,0:T(8,128)(2,1)} %bitcast.7, bf16[128,4096]{1,0:T(8,128)(2,1)} %bitcast.13, bf16[16,40,128]{2,1,0:T(8,128)(2,1)} %shard_map.85.after_ref), custom_call_target="tpu_custom_call" | custom-call | tf_op jit(solution)/shard_map/pallas_call | solution.py:257
  22.8 1.9 %collective-permute-start = (bf16[16,128,128]{2,1,0:T(8,128)(2,1)}, bf16[16,128,128]{2,1,0:T(8,128)(2,1)S(1)}, u32[]{:S(2)}, u32[]{:S(2)}) collective-permute-start(bf16[16,128,128]{2,1,0:T(8,128)(2,1)} %get-tuple-element.21), channel_id=1, source_target_pairs={{0,16},{16,0},{1,17},{17,1},{2,18},{18,2},{3,19},{19,3},{4,20},{20... | collective-permute-start | bytes 1572872 | tf_op jit(solution)/shard_map/ppermute | solution.py:269
  24.7 0.0 copy-start
  24.8 0.0 copy-start.1
  24.8 2.5 %collective-permute-start.1 = (bf16[16,128,128]{2,1,0:T(8,128)(2,1)}, bf16[16,128,128]{2,1,0:T(8,128)(2,1)S(1)}, u32[]{:S(2)}, u32[]{:S(2)}) collective-permute-start(bf16[16,128,128]{2,1,0:T(8,128)(2,1)} %get-tuple-element.22), channel_id=1, source_target_pairs={{0,16},{16,0},{1,17},{17,1},{2,18},{18,2},{3,19},{19,3},{4,20},{20... | collective-permute-start | bytes 1572872 | tf_op jit(solution)/shard_map/ppermute | solution.py:269
  27.3 9.3 %all-to-all-done = bf16[16,40,128]{2,1,0:T(8,128)(2,1)S(1)} async-done(((bf16[16,40,128]{2,1,0:T(8,128)(2,1)}), bf16[16,40,128]{2,1,0:T(8,128)(2,1)S(1)}, u32[]{:S(2)}, u32[]{:S(2)}) %all-to-all-start) | async-done | bytes 163872 | tf_op jit(solution)/shard_map/all_to_all | solution.py:283
  36.6 17.3 %all_gather.3.own.refs_0_ = bf16[64,40,128]{2,1,0:T(8,128)(2,1)S(1)} all-gather(bf16[16,40,128]{2,1,0:T(8,128)(2,1)S(1)} %all-to-all-done), channel_id=1, replica_groups=mesh['y'=4,'zl'=4,'c'=2,'zh'=4,'x'=4] {'zl'}, dimensions={0}, use_global_device_ids=true | all-gather | bytes 819200 | tf_op jit(solution)/shard_map/all_gather | solution.py:284
  53.9 0.0 collective-permute-done.wis.sib_ref
  53.9 0.0 collective-permute-done.1.wos
  54.0 0.1 fusion
  54.0 4.9 %collective-permute-start.4 = (bf16[32,40,128]{2,1,0:T(8,128)(2,1)S(1)}, bf16[32,40,128]{2,1,0:T(8,128)(2,1)S(1)}, u32[]{:S(2)}, u32[]{:S(2)}) collective-permute-start(bf16[32,40,128]{2,1,0:T(8,128)(2,1)S(1)} %get-tuple-element.39), channel_id=1, source_target_pairs={{0,384},{16,144},{128,256},{144,16},{256,128},{272,400},{384,0},{4... | collective-permute-start | bytes 983048 | tf_op jit(solution)/shard_map/ppermute | solution.py:265
  58.9 2.0 %collective-permute-start.2 = (bf16[32,40,128]{2,1,0:T(8,128)(2,1)S(1)}, bf16[32,40,128]{2,1,0:T(8,128)(2,1)S(1)}, u32[]{:S(2)}, u32[]{:S(2)}) collective-permute-start(bf16[32,40,128]{2,1,0:T(8,128)(2,1)S(1)} %get-tuple-element.40), channel_id=1, source_target_pairs={{0,128},{16,400},{128,0},{144,272},{256,384},{272,144},{384,256},{... | collective-permute-start | bytes 983048 | tf_op jit(solution)/shard_map/ppermute | solution.py:265
  61.0 3.8 %collective-permute-start.7 = (bf16[32,40,128]{2,1,0:T(8,128)(2,1)S(1)}, bf16[32,40,128]{2,1,0:T(8,128)(2,1)S(1)}, u32[]{:S(2)}, u32[]{:S(2)}) collective-permute-start(bf16[32,40,128]{2,1,0:T(8,128)(2,1)S(1)} %get-tuple-element.39), channel_id=1, source_target_pairs={{0,128},{16,400},{128,0},{144,272},{256,384},{272,144},{384,256},{... | collective-permute-start | bytes 983048 | tf_op jit(solution)/shard_map/ppermute | solution.py:265
  64.8 2.1 %collective-permute-start.6 = (bf16[32,40,128]{2,1,0:T(8,128)(2,1)S(1)}, bf16[32,40,128]{2,1,0:T(8,128)(2,1)S(1)}, u32[]{:S(2)}, u32[]{:S(2)}) collective-permute-start(bf16[32,40,128]{2,1,0:T(8,128)(2,1)S(1)} %get-tuple-element.40), channel_id=1, source_target_pairs={{0,384},{16,144},{128,256},{144,16},{256,128},{272,400},{384,0},{4... | collective-permute-start | bytes 983048 | tf_op jit(solution)/shard_map/ppermute | solution.py:265
  66.9 0.8 collective-permute-done.4.second_b.refs_4_
  67.8 2.3 %collective-permute-start.5 = (bf16[32,40,128]{2,1,0:T(8,128)(2,1)S(1)}, bf16[32,40,128]{2,1,0:T(8,128)(2,1)S(1)}, u32[]{:S(2)}, u32[]{:S(2)}) collective-permute-start(bf16[32,40,128]{2,1,0:T(8,128)(2,1)S(1)} %collective-permute-done.4.second_b.refs_4_), channel_id=1, source_target_pairs={{0,128},{16,400},{128,0},{144,272},{256,384},{272,144},{384,256},{... | collective-permute-start | bytes 983048 | tf_op jit(solution)/shard_map/ppermute | solution.py:265
  70.0 1.4 collective-permute-done.2.first_a.refs_1_
  71.4 3.2 %collective-permute-start.3 = (bf16[32,40,128]{2,1,0:T(8,128)(2,1)S(1)}, bf16[32,40,128]{2,1,0:T(8,128)(2,1)S(1)}, u32[]{:S(2)}, u32[]{:S(2)}) collective-permute-start(bf16[32,40,128]{2,1,0:T(8,128)(2,1)S(1)} %collective-permute-done.2.first_a.refs_1_), channel_id=1, source_target_pairs={{0,384},{16,144},{128,256},{144,16},{256,128},{272,400},{384,0},{4... | collective-permute-start | bytes 983048 | tf_op jit(solution)/shard_map/ppermute | solution.py:265
  74.6 3.5 %collective-permute-done.7.first_b.refs_2_ = bf16[32,40,128]{2,1,0:T(8,128)(2,1)S(1)} collective-permute-done((bf16[32,40,128]{2,1,0:T(8,128)(2,1)S(1)}, bf16[32,40,128]{2,1,0:T(8,128)(2,1)S(1)}, u32[]{:S(2)}, u32[]{:S(2)}) %collective-permute-start.7) | collective-permute-done | bytes 327712 | tf_op jit(solution)/shard_map/ppermute | solution.py:265
  78.2 0.9 shard_map.87.before_ref
  79.0 0.0 collective-permute-done.6.second_a.refs_3_
  79.0 0.5 shard_map.88.before_ref
  79.6 2.1 %collective-permute-done.5.last_b.refs_6_ = bf16[32,40,128]{2,1,0:T(8,128)(2,1)S(1)} collective-permute-done((bf16[32,40,128]{2,1,0:T(8,128)(2,1)S(1)}, bf16[32,40,128]{2,1,0:T(8,128)(2,1)S(1)}, u32[]{:S(2)}, u32[]{:S(2)}) %collective-permute-start.5) | collective-permute-done | bytes 327712 | tf_op jit(solution)/shard_map/ppermute | solution.py:265
  81.7 0.5 shard_map.89
  82.2 1.9 %collective-permute-start.8 = (bf16[640,256]{1,0:T(8,128)(2,1)S(1)}, bf16[640,256]{1,0:T(8,128)(2,1)S(1)}, u32[]{:S(2)}, u32[]{:S(2)}) collective-permute-start(bf16[640,256]{1,0:T(8,128)(2,1)S(1)} %get-tuple-element.27), channel_id=1, source_target_pairs={{0,16},{16,0},{1,17},{17,1},{2,18},{18,2},{3,19},{19,3},{4,20},{20... | collective-permute-start | bytes 983048 | tf_op jit(solution)/shard_map/ppermute | solution.py:269
  84.1 1.6 %collective-permute-done.8.part_sib_ref = bf16[640,256]{1,0:T(8,128)(2,1)S(1)} collective-permute-done((bf16[640,256]{1,0:T(8,128)(2,1)S(1)}, bf16[640,256]{1,0:T(8,128)(2,1)S(1)}, u32[]{:S(2)}, u32[]{:S(2)}) %collective-permute-start.8) | collective-permute-done | bytes 327712 | tf_op jit(solution)/shard_map/ppermute | solution.py:269
  85.7 0.8 shard_map.90
  86.6 3.1 %collective-permute-start.9 = (bf16[4,320,128]{2,1,0:T(8,128)(2,1)S(1)}, bf16[4,320,128]{2,1,0:T(8,128)(2,1)S(1)}, u32[]{:S(2)}, u32[]{:S(2)}) collective-permute-start(bf16[4,320,128]{2,1,0:T(8,128)(2,1)S(1)} %get-tuple-element.31), channel_id=1, source_target_pairs={{0,384},{16,144},{128,256},{144,16},{256,128},{272,400},{384,0},{4... | collective-permute-start | bytes 983048 | tf_op jit(solution)/shard_map/ppermute | solution.py:265
  89.7 0.5 shard_map.91
  90.2 3.9 %collective-permute-start.11 = (bf16[4,320,128]{2,1,0:T(8,128)(2,1)S(1)}, bf16[4,320,128]{2,1,0:T(8,128)(2,1)S(1)}, u32[]{:S(2)}, u32[]{:S(2)}) collective-permute-start(bf16[4,320,128]{2,1,0:T(8,128)(2,1)S(1)} %get-tuple-element.32), channel_id=1, source_target_pairs={{0,384},{16,144},{128,256},{144,16},{256,128},{272,400},{384,0},{4... | collective-permute-start | bytes 983048 | tf_op jit(solution)/shard_map/ppermute | solution.py:265
  94.1 2.6 %collective-permute-done.9.passed_ref = bf16[4,320,128]{2,1,0:T(8,128)(2,1)S(1)} collective-permute-done((bf16[4,320,128]{2,1,0:T(8,128)(2,1)S(1)}, bf16[4,320,128]{2,1,0:T(8,128)(2,1)S(1)}, u32[]{:S(2)}, u32[]{:S(2)}) %collective-permute-start.9) | collective-permute-done | bytes 327712 | tf_op jit(solution)/shard_map/ppermute | solution.py:265
  96.8 0.1 shard_map.92.refs_7_
  96.8 1.9 %collective-permute-start.10 = (bf16[4,320,128]{2,1,0:T(8,128)(2,1)S(1)}, bf16[4,320,128]{2,1,0:T(8,128)(2,1)S(1)}, u32[]{:S(2)}, u32[]{:S(2)}) collective-permute-start(bf16[4,320,128]{2,1,0:T(8,128)(2,1)S(1)} %shard_map.92.refs_7_), channel_id=1, source_target_pairs={{0,128},{16,400},{128,0},{144,272},{256,384},{272,144},{384,256},{... | collective-permute-start | bytes 983048 | tf_op jit(solution)/shard_map/ppermute | solution.py:265
  98.8 2.0 %shard_map.93 = (bf16[16,128,128]{2,1,0:T(8,128)(2,1)S(1)}, bf16[128,2048]{1,0:T(8,128)(2,1)S(1)}, bf16[16,128,128]{2,1,0:T(8,128)(2,1)S(1)}, bf16[16,128,128]{2,1,0:T(8,128)(2,1)S(1)}) custom-call(f32[640,256]{1,0:T(8,128)S(1)} %get-tuple-element.26.part_ref, bf16[640,256]{1,0:T(8,128)(2,1)S(1)} %collective-permute-done.8.part_sib_ref, ...), custom_call_target="tpu_custom_call" | custom-call | tf_op jit(solution)/shard_map/pallas_call | solution.py:257
  100.8 5.0 %collective-permute-done.10.first_ref = bf16[4,320,128]{2,1,0:T(8,128)(2,1)S(1)} collective-permute-done((bf16[4,320,128]{2,1,0:T(8,128)(2,1)S(1)}, bf16[4,320,128]{2,1,0:T(8,128)(2,1)S(1)}, u32[]{:S(2)}, u32[]{:S(2)}) %collective-permute-start.10) | collective-permute-done | bytes 327712 | tf_op jit(solution)/shard_map/ppermute | solution.py:265
  105.8 0.8 shard_map.94
  106.6 3.5 %all-to-all-start.1 = ((bf16[4,320,128]{2,1,0:T(8,128)(2,1)}), bf16[4,320,128]{2,1,0:T(8,128)(2,1)S(1)}, u32[]{:S(2)}, u32[]{:S(2)}) async-start(bf16[4,320,128]{2,1,0:T(8,128)(2,1)} %shard_map.94), calls=%async_computation.1 | async-start | bytes 655360 | tf_op jit(solution)/shard_map/all_to_all | solution.py:310
  110.1 1.9 %collective-permute-start.13 = (bf16[16,128,128]{2,1,0:T(8,128)(2,1)S(1)}, bf16[16,128,128]{2,1,0:T(8,128)(2,1)S(1)}, u32[]{:S(2)}, u32[]{:S(2)}) collective-permute-start(bf16[16,128,128]{2,1,0:T(8,128)(2,1)S(1)} %get-tuple-element.36), channel_id=1, source_target_pairs={{0,16},{16,0},{1,17},{17,1},{2,18},{18,2},{3,19},{19,3},{4,20},{20... | collective-permute-start | bytes 1572872 | tf_op jit(solution)/shard_map/ppermute | solution.py:269
  112.0 2.4 %collective-permute-start.12 = (bf16[16,128,128]{2,1,0:T(8,128)(2,1)S(1)}, bf16[16,128,128]{2,1,0:T(8,128)(2,1)S(1)}, u32[]{:S(2)}, u32[]{:S(2)}) collective-permute-start(bf16[16,128,128]{2,1,0:T(8,128)(2,1)S(1)} %get-tuple-element.33.after_ref), channel_id=1, source_target_pairs={{0,16},{16,0},{1,17},{17,1},{2,18},{18,2},{3,19},{19,3},{4,20},{20... | collective-permute-start | bytes 1572872 | tf_op jit(solution)/shard_map/ppermute | solution.py:269
  114.5 4.5 %all-to-all-done.1.parts_ref = bf16[4,320,128]{2,1,0:T(8,128)(2,1)S(1)} async-done(((bf16[4,320,128]{2,1,0:T(8,128)(2,1)}), bf16[4,320,128]{2,1,0:T(8,128)(2,1)S(1)}, u32[]{:S(2)}, u32[]{:S(2)}) %all-to-all-start.1) | async-done | bytes 327712 | tf_op jit(solution)/shard_map/all_to_all | solution.py:310
  119.0 0.7 shard_map.95.after_ref
  119.7 5.6 %all-to-all-start.2 = ((bf16[16,20,128]{2,1,0:T(8,128)(2,1)}), bf16[16,20,128]{2,1,0:T(8,128)(2,1)S(1)}, u32[]{:S(2)}, u32[]{:S(2)}) async-start(bf16[16,20,128]{2,1,0:T(8,128)(2,1)} %shard_map.95.after_ref), calls=%async_computation.2 | async-start | bytes 196608 | tf_op jit(solution)/shard_map/all_to_all | solution.py:313
  125.2 1.6 %shard_map.98 = (bf16[4096,128]{1,0:T(8,128)(2,1)}, bf16[128,4096]{1,0:T(8,128)(2,1)}) custom-call(bf16[16,128,128]{2,1,0:T(8,128)(2,1)S(1)} %get-tuple-element.34.in_mine, bf16[128,2048]{1,0:T(8,128)(2,1)S(1)} %get-tuple-element.35.out_mine, bf16[16,128,128]{2,1,0:T(8,128)(2,1)S(1)} %collective-permute-done.12.in_sib, ...), custom_call_target="tpu_custom_call" | custom-call | tf_op jit(solution)/shard_map/pallas_call | solution.py:257
  126.9 1.0 shard_map.96.table_ref
  127.9 10.9 %all-to-all-done.2.back_ref = bf16[16,20,128]{2,1,0:T(8,128)(2,1)S(1)} async-done(((bf16[16,20,128]{2,1,0:T(8,128)(2,1)}), bf16[16,20,128]{2,1,0:T(8,128)(2,1)S(1)}, u32[]{:S(2)}, u32[]{:S(2)}) %all-to-all-start.2) | async-done | bytes 81952 | tf_op jit(solution)/shard_map/all_to_all | solution.py:313
  138.8 0.8 shard_map.97
  (6 shorter events, 0.0 us)
Async XLA Ops:
  2.5 34.1 %all-to-all-start = ((bf16[16,40,128]{2,1,0:T(8,128)(2,1)}), bf16[16,40,128]{2,1,0:T(8,128)(2,1)S(1)}, u32[]{:S(2)}, u32[]{:S(2)}) async-start(bf16[16,40,128]{2,1,0:T(8,128)(2,1)} %shard_map.85.after_ref), calls=%async_computation | async-start | bytes 327680 | tf_op jit(solution)/shard_map/all_to_all | solution.py:283
  22.8 31.1 %collective-permute-start = (bf16[16,128,128]{2,1,0:T(8,128)(2,1)}, bf16[16,128,128]{2,1,0:T(8,128)(2,1)S(1)}, u32[]{:S(2)}, u32[]{:S(2)}) collective-permute-start(bf16[16,128,128]{2,1,0:T(8,128)(2,1)} %get-tuple-element.21), channel_id=1, source_target_pairs={{0,16},{16,0},{1,17},{17,1},{2,18},{18,2},{3,19},{19,3},{4,20},{20... | collective-permute-start | bytes 1572872 | tf_op jit(solution)/shard_map/ppermute | solution.py:269
  24.7 53.4 %copy-start = (bf16[1,4096,128]{2,1,0:T(8,128)(2,1)S(1)}, bf16[1,4096,128]{2,1,0:T(8,128)(2,1)}, u32[]{:S(2)}) copy-start(bf16[1,4096,128]{2,1,0:T(8,128)(2,1)} %param.10) | copy-start | bytes 3145732
  24.8 53.4 %copy-start.1 = (bf16[1,128,4096]{2,1,0:T(8,128)(2,1)S(1)}, bf16[1,128,4096]{2,1,0:T(8,128)(2,1)}, u32[]{:S(2)}) copy-start(bf16[1,128,4096]{2,1,0:T(8,128)(2,1)} %param.11) | copy-start | bytes 3145732
  24.8 29.2 %collective-permute-start.1 = (bf16[16,128,128]{2,1,0:T(8,128)(2,1)}, bf16[16,128,128]{2,1,0:T(8,128)(2,1)S(1)}, u32[]{:S(2)}, u32[]{:S(2)}) collective-permute-start(bf16[16,128,128]{2,1,0:T(8,128)(2,1)} %get-tuple-element.22), channel_id=1, source_target_pairs={{0,16},{16,0},{1,17},{17,1},{2,18},{18,2},{3,19},{19,3},{4,20},{20... | collective-permute-start | bytes 1572872 | tf_op jit(solution)/shard_map/ppermute | solution.py:269
  54.0 13.8 %collective-permute-start.4 = (bf16[32,40,128]{2,1,0:T(8,128)(2,1)S(1)}, bf16[32,40,128]{2,1,0:T(8,128)(2,1)S(1)}, u32[]{:S(2)}, u32[]{:S(2)}) collective-permute-start(bf16[32,40,128]{2,1,0:T(8,128)(2,1)S(1)} %get-tuple-element.39), channel_id=1, source_target_pairs={{0,384},{16,144},{128,256},{144,16},{256,128},{272,400},{384,0},{4... | collective-permute-start | bytes 983048 | tf_op jit(solution)/shard_map/ppermute | solution.py:265
  58.9 12.5 %collective-permute-start.2 = (bf16[32,40,128]{2,1,0:T(8,128)(2,1)S(1)}, bf16[32,40,128]{2,1,0:T(8,128)(2,1)S(1)}, u32[]{:S(2)}, u32[]{:S(2)}) collective-permute-start(bf16[32,40,128]{2,1,0:T(8,128)(2,1)S(1)} %get-tuple-element.40), channel_id=1, source_target_pairs={{0,128},{16,400},{128,0},{144,272},{256,384},{272,144},{384,256},{... | collective-permute-start | bytes 983048 | tf_op jit(solution)/shard_map/ppermute | solution.py:265
  61.0 17.2 %collective-permute-start.7 = (bf16[32,40,128]{2,1,0:T(8,128)(2,1)S(1)}, bf16[32,40,128]{2,1,0:T(8,128)(2,1)S(1)}, u32[]{:S(2)}, u32[]{:S(2)}) collective-permute-start(bf16[32,40,128]{2,1,0:T(8,128)(2,1)S(1)} %get-tuple-element.39), channel_id=1, source_target_pairs={{0,128},{16,400},{128,0},{144,272},{256,384},{272,144},{384,256},{... | collective-permute-start | bytes 983048 | tf_op jit(solution)/shard_map/ppermute | solution.py:265
  64.8 14.2 %collective-permute-start.6 = (bf16[32,40,128]{2,1,0:T(8,128)(2,1)S(1)}, bf16[32,40,128]{2,1,0:T(8,128)(2,1)S(1)}, u32[]{:S(2)}, u32[]{:S(2)}) collective-permute-start(bf16[32,40,128]{2,1,0:T(8,128)(2,1)S(1)} %get-tuple-element.40), channel_id=1, source_target_pairs={{0,384},{16,144},{128,256},{144,16},{256,128},{272,400},{384,0},{4... | collective-permute-start | bytes 983048 | tf_op jit(solution)/shard_map/ppermute | solution.py:265
  67.8 13.9 %collective-permute-start.5 = (bf16[32,40,128]{2,1,0:T(8,128)(2,1)S(1)}, bf16[32,40,128]{2,1,0:T(8,128)(2,1)S(1)}, u32[]{:S(2)}, u32[]{:S(2)}) collective-permute-start(bf16[32,40,128]{2,1,0:T(8,128)(2,1)S(1)} %collective-permute-done.4.second_b.refs_4_), channel_id=1, source_target_pairs={{0,128},{16,400},{128,0},{144,272},{256,384},{272,144},{384,256},{... | collective-permute-start | bytes 983048 | tf_op jit(solution)/shard_map/ppermute | solution.py:265
  71.4 10.2 %collective-permute-start.3 = (bf16[32,40,128]{2,1,0:T(8,128)(2,1)S(1)}, bf16[32,40,128]{2,1,0:T(8,128)(2,1)S(1)}, u32[]{:S(2)}, u32[]{:S(2)}) collective-permute-start(bf16[32,40,128]{2,1,0:T(8,128)(2,1)S(1)} %collective-permute-done.2.first_a.refs_1_), channel_id=1, source_target_pairs={{0,384},{16,144},{128,256},{144,16},{256,128},{272,400},{384,0},{4... | collective-permute-start | bytes 983048 | tf_op jit(solution)/shard_map/ppermute | solution.py:265
  82.2 3.5 %collective-permute-start.8 = (bf16[640,256]{1,0:T(8,128)(2,1)S(1)}, bf16[640,256]{1,0:T(8,128)(2,1)S(1)}, u32[]{:S(2)}, u32[]{:S(2)}) collective-permute-start(bf16[640,256]{1,0:T(8,128)(2,1)S(1)} %get-tuple-element.27), channel_id=1, source_target_pairs={{0,16},{16,0},{1,17},{17,1},{2,18},{18,2},{3,19},{19,3},{4,20},{20... | collective-permute-start | bytes 983048 | tf_op jit(solution)/shard_map/ppermute | solution.py:269
  86.6 10.2 %collective-permute-start.9 = (bf16[4,320,128]{2,1,0:T(8,128)(2,1)S(1)}, bf16[4,320,128]{2,1,0:T(8,128)(2,1)S(1)}, u32[]{:S(2)}, u32[]{:S(2)}) collective-permute-start(bf16[4,320,128]{2,1,0:T(8,128)(2,1)S(1)} %get-tuple-element.31), channel_id=1, source_target_pairs={{0,384},{16,144},{128,256},{144,16},{256,128},{272,400},{384,0},{4... | collective-permute-start | bytes 983048 | tf_op jit(solution)/shard_map/ppermute | solution.py:265
  90.2 10.6 %collective-permute-start.11 = (bf16[4,320,128]{2,1,0:T(8,128)(2,1)S(1)}, bf16[4,320,128]{2,1,0:T(8,128)(2,1)S(1)}, u32[]{:S(2)}, u32[]{:S(2)}) collective-permute-start(bf16[4,320,128]{2,1,0:T(8,128)(2,1)S(1)} %get-tuple-element.32), channel_id=1, source_target_pairs={{0,384},{16,144},{128,256},{144,16},{256,128},{272,400},{384,0},{4... | collective-permute-start | bytes 983048 | tf_op jit(solution)/shard_map/ppermute | solution.py:265
  96.8 9.0 %collective-permute-start.10 = (bf16[4,320,128]{2,1,0:T(8,128)(2,1)S(1)}, bf16[4,320,128]{2,1,0:T(8,128)(2,1)S(1)}, u32[]{:S(2)}, u32[]{:S(2)}) collective-permute-start(bf16[4,320,128]{2,1,0:T(8,128)(2,1)S(1)} %shard_map.92.refs_7_), channel_id=1, source_target_pairs={{0,128},{16,400},{128,0},{144,272},{256,384},{272,144},{384,256},{... | collective-permute-start | bytes 983048 | tf_op jit(solution)/shard_map/ppermute | solution.py:265
  106.6 12.3 %all-to-all-start.1 = ((bf16[4,320,128]{2,1,0:T(8,128)(2,1)}), bf16[4,320,128]{2,1,0:T(8,128)(2,1)S(1)}, u32[]{:S(2)}, u32[]{:S(2)}) async-start(bf16[4,320,128]{2,1,0:T(8,128)(2,1)} %shard_map.94), calls=%async_computation.1 | async-start | bytes 655360 | tf_op jit(solution)/shard_map/all_to_all | solution.py:310
  110.1 15.1 %collective-permute-start.13 = (bf16[16,128,128]{2,1,0:T(8,128)(2,1)S(1)}, bf16[16,128,128]{2,1,0:T(8,128)(2,1)S(1)}, u32[]{:S(2)}, u32[]{:S(2)}) collective-permute-start(bf16[16,128,128]{2,1,0:T(8,128)(2,1)S(1)} %get-tuple-element.36), channel_id=1, source_target_pairs={{0,16},{16,0},{1,17},{17,1},{2,18},{18,2},{3,19},{19,3},{4,20},{20... | collective-permute-start | bytes 1572872 | tf_op jit(solution)/shard_map/ppermute | solution.py:269
  112.0 13.2 %collective-permute-start.12 = (bf16[16,128,128]{2,1,0:T(8,128)(2,1)S(1)}, bf16[16,128,128]{2,1,0:T(8,128)(2,1)S(1)}, u32[]{:S(2)}, u32[]{:S(2)}) collective-permute-start(bf16[16,128,128]{2,1,0:T(8,128)(2,1)S(1)} %get-tuple-element.33.after_ref), channel_id=1, source_target_pairs={{0,16},{16,0},{1,17},{17,1},{2,18},{18,2},{3,19},{19,3},{4,20},{20... | collective-permute-start | bytes 1572872 | tf_op jit(solution)/shard_map/ppermute | solution.py:269
  119.7 19.1 %all-to-all-start.2 = ((bf16[16,20,128]{2,1,0:T(8,128)(2,1)}), bf16[16,20,128]{2,1,0:T(8,128)(2,1)S(1)}, u32[]{:S(2)}, u32[]{:S(2)}) async-start(bf16[16,20,128]{2,1,0:T(8,128)(2,1)} %shard_map.95.after_ref), calls=%async_computation.2 | async-start | bytes 196608 | tf_op jit(solution)/shard_map/all_to_all | solution.py:313

commit v7 on v6

--- a/solution.py
+++ b/solution.py
@@ -18,7 +18,6 @@
 F32 = jnp.float32
 VMEM = pltpu.CompilerParams(vmem_limit_bytes=14 * 1024 * 1024)
 CONTRACT_LAST = (((1,), (1,)), ((), ()))
-CONTRACT_FIRST = (((0,), (0,)), ((), ()))
 
 
 def slot_table(ids, rows_each, slot_of):
@@ -73,7 +72,7 @@
 def table_kernel(ids_ref, after_ref, table_ref):
     del after_ref
     table, _, _ = slot_table(ids_ref[...], CAP, lambda q: q)
-    table_ref[...] = table.astype(BF16)
+    table_ref[...] = table.astype(BF16).T
 
 
 def position():
@@ -164,10 +163,7 @@
 
 def far_kernel(w_in_ref, sib_ref, part_ref, part_sib_ref, pg_ref, out_ref):
     pre_grad, _ = activations(part_ref, part_sib_ref)
-    block = lax.broadcasted_iota(jnp.int32, (EXPERTS, CAP, ROWS), 0).reshape(KEPT, ROWS)
-    within = lax.broadcasted_iota(jnp.int32, (EXPERTS, CAP, ROWS), 1).reshape(KEPT, ROWS)
-    keep = (lax.broadcasted_iota(jnp.int32, (KEPT, ROWS), 1) == block * MSG + within).astype(BF16)
-    pg = jnp.dot(keep, pre_grad, preferred_element_type=F32).astype(BF16)
+    pg = pre_grad.astype(F32).reshape(EXPERTS, MSG, NC * HID)[:, :CAP].reshape(KEPT, NC * HID).astype(BF16)
     pg_ref[...] = pg
     partials(w_in_ref, sib_ref, pg, places(*position())[3], out_ref)
 
@@ -227,7 +223,7 @@
 
 def combine_kernel(table_ref, back_ref, out_ref):
     rows = back_ref[...].astype(F32).reshape(KEPT, COLS).astype(BF16)
-    out_ref[...] = lax.dot_general(table_ref[...], rows, CONTRACT_FIRST, preferred_element_type=F32).astype(BF16)
+    out_ref[...] = jnp.dot(table_ref[...], rows, preferred_element_type=F32).astype(BF16)
 
 
 SMEM = pl.BlockSpec(memory_space=pltpu.SMEM)
@@ -309,7 +305,7 @@
     summed = run(total_kernel, rows, 0, keep(to_own), keep(from_first), keep(from_second), in_other, unread=1)
     collected = lax.all_to_all(summed, "zl", 0, 0, tiled=True)
     total = run(gathered_kernel, held(EXPERTS, CAP, COLS), 0, keep(collected))
-    table = run(table_kernel, held(KEPT, TOK), 0, ids, total, unread=1)
+    table = run(table_kernel, held(TOK, KEPT), 0, ids, total, unread=1)
     back = lax.all_to_all(total, ("zh", "x"), 0, 0, tiled=True)
     tokens_grad = run(combine_kernel, shape(TOK, COLS), 0, keep(table), keep(back))
     w_in_grad, w_out_grad = run(

time: 140 us -> 140 us (level)
  no operation moved by 1% of the time
where the time goes in v7:
time: 140 us; the launch traced here: 139 us
  starting transfers between devices  65.2 us (47%)
  waiting for transfers between devices  41.7 us (30%)
  blocking collectives  17.3 us (12%)
  Pallas kernels  14.1 us (10%)
    ppermute x9, starting transfers between devices, partner(): lax.ppermute(value, ('y', 'c'), [(i * NC + c, to[c][which][i] * NC + c) f...  27.3 us
    all_to_all x1, starting transfers between devices, on_device(): received = lax.all_to_all(send, ('zh', 'x'), 0, 0, tiled=True)  18.1 us
    all_gather x1, blocking collectives, on_device(): own = lax.all_gather(received, 'zl', axis=0, tiled=True)  17.3 us
    ppermute x9, waiting for transfers between devices, partner(): lax.ppermute(value, ('y', 'c'), [(i * NC + c, to[c][which][i] * NC + c) f...  15.4 us
    pallas_call x14, Pallas kernels, run(): pl.pallas_call(kernel, out_shape=outs, in_specs=specs, out_specs=out_spec...  14.1 us
    all_to_all x1, waiting for transfers between devices, on_device(): back = lax.all_to_all(total, ('zh', 'x'), 0, 0, tiled=True)  10.9 us
    ppermute x5, starting transfers between devices, across(): return lax.ppermute(value, 'c', [(0, 1), (1, 0)])  10.7 us
    all_to_all x1, waiting for transfers between devices, on_device(): received = lax.all_to_all(send, ('zh', 'x'), 0, 0, tiled=True)  9.3 us
  transfers between devices with their start and end apart: 17, of which 10 were waited for; matrix products, arithmetic and copies ran while one was open for 0% of the time, Pallas kernels for 7%

profile of v7, /device:TPU:2, one launch (start us, length us, event | category | flops | bytes accessed | tf_op | source)
XLA Modules:
  0.0 139.3 jit_solution(6569101647343842076)
XLA Ops:
  0.6 1.9 %shard_map.85.after_ref = bf16[16,40,128]{2,1,0:T(8,128)(2,1)} custom-call(s32[2,128]{1,0:T(2,128)} %bitcast.17, f32[2,128]{1,0:T(2,128)} %bitcast.19, bf16[128,128]{1,0:T(8,128)(2,1)} %tok_ref.1, bf16[128,128]{1,0:T(8,128)(2,1)} %dy_ref.1), custom_call_target="tpu_custom_call" | custom-call | tf_op jit(solution)/shard_map/pallas_call | solution.py:253
  2.5 18.1 %all-to-all-start = ((bf16[16,40,128]{2,1,0:T(8,128)(2,1)}), bf16[16,40,128]{2,1,0:T(8,128)(2,1)S(1)}, u32[]{:S(2)}, u32[]{:S(2)}) async-start(bf16[16,40,128]{2,1,0:T(8,128)(2,1)} %shard_map.85.after_ref), calls=%async_computation | async-start | bytes 327680 | tf_op jit(solution)/shard_map/all_to_all | solution.py:279
  20.6 2.2 %shard_map.86 = (bf16[16,128,128]{2,1,0:T(8,128)(2,1)}, bf16[16,128,128]{2,1,0:T(8,128)(2,1)}) custom-call(bf16[16,2,128,128]{3,2,1,0:T(8,128)(2,1)} %bitcast.7, bf16[128,4096]{1,0:T(8,128)(2,1)} %bitcast.13, bf16[16,40,128]{2,1,0:T(8,128)(2,1)} %shard_map.85.after_ref), custom_call_target="tpu_custom_call" | custom-call | tf_op jit(solution)/shard_map/pallas_call | solution.py:253
  22.8 1.9 %collective-permute-start = (bf16[16,128,128]{2,1,0:T(8,128)(2,1)}, bf16[16,128,128]{2,1,0:T(8,128)(2,1)S(1)}, u32[]{:S(2)}, u32[]{:S(2)}) collective-permute-start(bf16[16,128,128]{2,1,0:T(8,128)(2,1)} %get-tuple-element.21), channel_id=1, source_target_pairs={{0,16},{16,0},{1,17},{17,1},{2,18},{18,2},{3,19},{19,3},{4,20},{20... | collective-permute-start | bytes 1572872 | tf_op jit(solution)/shard_map/ppermute | solution.py:265
  24.7 0.0 copy-start
  24.8 0.0 copy-start.1
  24.8 2.5 %collective-permute-start.1 = (bf16[16,128,128]{2,1,0:T(8,128)(2,1)}, bf16[16,128,128]{2,1,0:T(8,128)(2,1)S(1)}, u32[]{:S(2)}, u32[]{:S(2)}) collective-permute-start(bf16[16,128,128]{2,1,0:T(8,128)(2,1)} %get-tuple-element.22), channel_id=1, source_target_pairs={{0,16},{16,0},{1,17},{17,1},{2,18},{18,2},{3,19},{19,3},{4,20},{20... | collective-permute-start | bytes 1572872 | tf_op jit(solution)/shard_map/ppermute | solution.py:265
  27.3 9.3 %all-to-all-done = bf16[16,40,128]{2,1,0:T(8,128)(2,1)S(1)} async-done(((bf16[16,40,128]{2,1,0:T(8,128)(2,1)}), bf16[16,40,128]{2,1,0:T(8,128)(2,1)S(1)}, u32[]{:S(2)}, u32[]{:S(2)}) %all-to-all-start) | async-done | bytes 163872 | tf_op jit(solution)/shard_map/all_to_all | solution.py:279
  36.6 17.3 %all_gather.3.own.refs_0_ = bf16[64,40,128]{2,1,0:T(8,128)(2,1)S(1)} all-gather(bf16[16,40,128]{2,1,0:T(8,128)(2,1)S(1)} %all-to-all-done), channel_id=1, replica_groups=mesh['y'=4,'zl'=4,'c'=2,'zh'=4,'x'=4] {'zl'}, dimensions={0}, use_global_device_ids=true | all-gather | bytes 819200 | tf_op jit(solution)/shard_map/all_gather | solution.py:280
  53.9 0.0 collective-permute-done.wis.sib_ref
  53.9 0.0 collective-permute-done.1.wos
  54.0 0.1 fusion
  54.0 4.9 %collective-permute-start.4 = (bf16[32,40,128]{2,1,0:T(8,128)(2,1)S(1)}, bf16[32,40,128]{2,1,0:T(8,128)(2,1)S(1)}, u32[]{:S(2)}, u32[]{:S(2)}) collective-permute-start(bf16[32,40,128]{2,1,0:T(8,128)(2,1)S(1)} %get-tuple-element.39), channel_id=1, source_target_pairs={{0,384},{16,144},{128,256},{144,16},{256,128},{272,400},{384,0},{4... | collective-permute-start | bytes 983048 | tf_op jit(solution)/shard_map/ppermute | solution.py:261
  58.9 2.0 %collective-permute-start.2 = (bf16[32,40,128]{2,1,0:T(8,128)(2,1)S(1)}, bf16[32,40,128]{2,1,0:T(8,128)(2,1)S(1)}, u32[]{:S(2)}, u32[]{:S(2)}) collective-permute-start(bf16[32,40,128]{2,1,0:T(8,128)(2,1)S(1)} %get-tuple-element.40), channel_id=1, source_target_pairs={{0,128},{16,400},{128,0},{144,272},{256,384},{272,144},{384,256},{... | collective-permute-start | bytes 983048 | tf_op jit(solution)/shard_map/ppermute | solution.py:261
  61.0 3.8 %collective-permute-start.7 = (bf16[32,40,128]{2,1,0:T(8,128)(2,1)S(1)}, bf16[32,40,128]{2,1,0:T(8,128)(2,1)S(1)}, u32[]{:S(2)}, u32[]{:S(2)}) collective-permute-start(bf16[32,40,128]{2,1,0:T(8,128)(2,1)S(1)} %get-tuple-element.39), channel_id=1, source_target_pairs={{0,128},{16,400},{128,0},{144,272},{256,384},{272,144},{384,256},{... | collective-permute-start | bytes 983048 | tf_op jit(solution)/shard_map/ppermute | solution.py:261
  64.8 2.1 %collective-permute-start.6 = (bf16[32,40,128]{2,1,0:T(8,128)(2,1)S(1)}, bf16[32,40,128]{2,1,0:T(8,128)(2,1)S(1)}, u32[]{:S(2)}, u32[]{:S(2)}) collective-permute-start(bf16[32,40,128]{2,1,0:T(8,128)(2,1)S(1)} %get-tuple-element.40), channel_id=1, source_target_pairs={{0,384},{16,144},{128,256},{144,16},{256,128},{272,400},{384,0},{4... | collective-permute-start | bytes 983048 | tf_op jit(solution)/shard_map/ppermute | solution.py:261
  66.9 0.8 collective-permute-done.4.second_b.refs_4_
  67.8 2.3 %collective-permute-start.5 = (bf16[32,40,128]{2,1,0:T(8,128)(2,1)S(1)}, bf16[32,40,128]{2,1,0:T(8,128)(2,1)S(1)}, u32[]{:S(2)}, u32[]{:S(2)}) collective-permute-start(bf16[32,40,128]{2,1,0:T(8,128)(2,1)S(1)} %collective-permute-done.4.second_b.refs_4_), channel_id=1, source_target_pairs={{0,128},{16,400},{128,0},{144,272},{256,384},{272,144},{384,256},{... | collective-permute-start | bytes 983048 | tf_op jit(solution)/shard_map/ppermute | solution.py:261
  70.0 1.4 collective-permute-done.2.first_a.refs_1_
  71.4 3.2 %collective-permute-start.3 = (bf16[32,40,128]{2,1,0:T(8,128)(2,1)S(1)}, bf16[32,40,128]{2,1,0:T(8,128)(2,1)S(1)}, u32[]{:S(2)}, u32[]{:S(2)}) collective-permute-start(bf16[32,40,128]{2,1,0:T(8,128)(2,1)S(1)} %collective-permute-done.2.first_a.refs_1_), channel_id=1, source_target_pairs={{0,384},{16,144},{128,256},{144,16},{256,128},{272,400},{384,0},{4... | collective-permute-start | bytes 983048 | tf_op jit(solution)/shard_map/ppermute | solution.py:261
  74.6 3.5 %collective-permute-done.7.first_b.refs_2_ = bf16[32,40,128]{2,1,0:T(8,128)(2,1)S(1)} collective-permute-done((bf16[32,40,128]{2,1,0:T(8,128)(2,1)S(1)}, bf16[32,40,128]{2,1,0:T(8,128)(2,1)S(1)}, u32[]{:S(2)}, u32[]{:S(2)}) %collective-permute-start.7) | collective-permute-done | bytes 327712 | tf_op jit(solution)/shard_map/ppermute | solution.py:261
  78.2 0.9 shard_map.87.before_ref
  79.0 0.0 collective-permute-done.6.second_a.refs_3_
  79.0 0.5 shard_map.88.before_ref
  79.6 2.1 %collective-permute-done.5.last_b.refs_6_ = bf16[32,40,128]{2,1,0:T(8,128)(2,1)S(1)} collective-permute-done((bf16[32,40,128]{2,1,0:T(8,128)(2,1)S(1)}, bf16[32,40,128]{2,1,0:T(8,128)(2,1)S(1)}, u32[]{:S(2)}, u32[]{:S(2)}) %collective-permute-start.5) | collective-permute-done | bytes 327712 | tf_op jit(solution)/shard_map/ppermute | solution.py:261
  81.7 0.5 shard_map.89
  82.2 1.9 %collective-permute-start.8 = (bf16[640,256]{1,0:T(8,128)(2,1)S(1)}, bf16[640,256]{1,0:T(8,128)(2,1)S(1)}, u32[]{:S(2)}, u32[]{:S(2)}) collective-permute-start(bf16[640,256]{1,0:T(8,128)(2,1)S(1)} %get-tuple-element.27), channel_id=1, source_target_pairs={{0,16},{16,0},{1,17},{17,1},{2,18},{18,2},{3,19},{19,3},{4,20},{20... | collective-permute-start | bytes 983048 | tf_op jit(solution)/shard_map/ppermute | solution.py:265
  84.1 1.6 %collective-permute-done.8.part_sib_ref = bf16[640,256]{1,0:T(8,128)(2,1)S(1)} collective-permute-done((bf16[640,256]{1,0:T(8,128)(2,1)S(1)}, bf16[640,256]{1,0:T(8,128)(2,1)S(1)}, u32[]{:S(2)}, u32[]{:S(2)}) %collective-permute-start.8) | collective-permute-done | bytes 327712 | tf_op jit(solution)/shard_map/ppermute | solution.py:265
  85.7 0.6 shard_map.90
  86.3 3.1 %collective-permute-start.9 = (bf16[4,320,128]{2,1,0:T(8,128)(2,1)S(1)}, bf16[4,320,128]{2,1,0:T(8,128)(2,1)S(1)}, u32[]{:S(2)}, u32[]{:S(2)}) collective-permute-start(bf16[4,320,128]{2,1,0:T(8,128)(2,1)S(1)} %get-tuple-element.31), channel_id=1, source_target_pairs={{0,384},{16,144},{128,256},{144,16},{256,128},{272,400},{384,0},{4... | collective-permute-start | bytes 983048 | tf_op jit(solution)/shard_map/ppermute | solution.py:261
  89.4 0.5 shard_map.91
  89.9 3.9 %collective-permute-start.11 = (bf16[4,320,128]{2,1,0:T(8,128)(2,1)S(1)}, bf16[4,320,128]{2,1,0:T(8,128)(2,1)S(1)}, u32[]{:S(2)}, u32[]{:S(2)}) collective-permute-start(bf16[4,320,128]{2,1,0:T(8,128)(2,1)S(1)} %get-tuple-element.32), channel_id=1, source_target_pairs={{0,384},{16,144},{128,256},{144,16},{256,128},{272,400},{384,0},{4... | collective-permute-start | bytes 983048 | tf_op jit(solution)/shard_map/ppermute | solution.py:261
  93.8 2.6 %collective-permute-done.9.passed_ref = bf16[4,320,128]{2,1,0:T(8,128)(2,1)S(1)} collective-permute-done((bf16[4,320,128]{2,1,0:T(8,128)(2,1)S(1)}, bf16[4,320,128]{2,1,0:T(8,128)(2,1)S(1)}, u32[]{:S(2)}, u32[]{:S(2)}) %collective-permute-start.9) | collective-permute-done | bytes 327712 | tf_op jit(solution)/shard_map/ppermute | solution.py:261
  96.5 0.1 shard_map.92.refs_7_
  96.5 1.9 %collective-permute-start.10 = (bf16[4,320,128]{2,1,0:T(8,128)(2,1)S(1)}, bf16[4,320,128]{2,1,0:T(8,128)(2,1)S(1)}, u32[]{:S(2)}, u32[]{:S(2)}) collective-permute-start(bf16[4,320,128]{2,1,0:T(8,128)(2,1)S(1)} %shard_map.92.refs_7_), channel_id=1, source_target_pairs={{0,128},{16,400},{128,0},{144,272},{256,384},{272,144},{384,256},{... | collective-permute-start | bytes 983048 | tf_op jit(solution)/shard_map/ppermute | solution.py:261
  98.5 2.0 %shard_map.93 = (bf16[16,128,128]{2,1,0:T(8,128)(2,1)S(1)}, bf16[128,2048]{1,0:T(8,128)(2,1)S(1)}, bf16[16,128,128]{2,1,0:T(8,128)(2,1)S(1)}, bf16[16,128,128]{2,1,0:T(8,128)(2,1)S(1)}) custom-call(f32[640,256]{1,0:T(8,128)S(1)} %get-tuple-element.26.part_ref, bf16[640,256]{1,0:T(8,128)(2,1)S(1)} %collective-permute-done.8.part_sib_ref, ...), custom_call_target="tpu_custom_call" | custom-call | tf_op jit(solution)/shard_map/pallas_call | solution.py:253
  100.5 5.0 %collective-permute-done.10.first_ref = bf16[4,320,128]{2,1,0:T(8,128)(2,1)S(1)} collective-permute-done((bf16[4,320,128]{2,1,0:T(8,128)(2,1)S(1)}, bf16[4,320,128]{2,1,0:T(8,128)(2,1)S(1)}, u32[]{:S(2)}, u32[]{:S(2)}) %collective-permute-start.10) | collective-permute-done | bytes 327712 | tf_op jit(solution)/shard_map/ppermute | solution.py:261
  105.5 0.8 shard_map.94
  106.4 3.5 %all-to-all-start.1 = ((bf16[4,320,128]{2,1,0:T(8,128)(2,1)}), bf16[4,320,128]{2,1,0:T(8,128)(2,1)S(1)}, u32[]{:S(2)}, u32[]{:S(2)}) async-start(bf16[4,320,128]{2,1,0:T(8,128)(2,1)} %shard_map.94), calls=%async_computation.1 | async-start | bytes 655360 | tf_op jit(solution)/shard_map/all_to_all | solution.py:306
  109.8 1.9 %collective-permute-start.13 = (bf16[16,128,128]{2,1,0:T(8,128)(2,1)S(1)}, bf16[16,128,128]{2,1,0:T(8,128)(2,1)S(1)}, u32[]{:S(2)}, u32[]{:S(2)}) collective-permute-start(bf16[16,128,128]{2,1,0:T(8,128)(2,1)S(1)} %get-tuple-element.36), channel_id=1, source_target_pairs={{0,16},{16,0},{1,17},{17,1},{2,18},{18,2},{3,19},{19,3},{4,20},{20... | collective-permute-start | bytes 1572872 | tf_op jit(solution)/shard_map/ppermute | solution.py:265
  111.7 2.4 %collective-permute-start.12 = (bf16[16,128,128]{2,1,0:T(8,128)(2,1)S(1)}, bf16[16,128,128]{2,1,0:T(8,128)(2,1)S(1)}, u32[]{:S(2)}, u32[]{:S(2)}) collective-permute-start(bf16[16,128,128]{2,1,0:T(8,128)(2,1)S(1)} %get-tuple-element.33.after_ref), channel_id=1, source_target_pairs={{0,16},{16,0},{1,17},{17,1},{2,18},{18,2},{3,19},{19,3},{4,20},{20... | collective-permute-start | bytes 1572872 | tf_op jit(solution)/shard_map/ppermute | solution.py:265
  114.2 4.5 %all-to-all-done.1.parts_ref = bf16[4,320,128]{2,1,0:T(8,128)(2,1)S(1)} async-done(((bf16[4,320,128]{2,1,0:T(8,128)(2,1)}), bf16[4,320,128]{2,1,0:T(8,128)(2,1)S(1)}, u32[]{:S(2)}, u32[]{:S(2)}) %all-to-all-start.1) | async-done | bytes 327712 | tf_op jit(solution)/shard_map/all_to_all | solution.py:306
  118.7 0.7 shard_map.95.after_ref
  119.4 5.6 %all-to-all-start.2 = ((bf16[16,20,128]{2,1,0:T(8,128)(2,1)}), bf16[16,20,128]{2,1,0:T(8,128)(2,1)S(1)}, u32[]{:S(2)}, u32[]{:S(2)}) async-start(bf16[16,20,128]{2,1,0:T(8,128)(2,1)} %shard_map.95.after_ref), calls=%async_computation.2 | async-start | bytes 196608 | tf_op jit(solution)/shard_map/all_to_all | solution.py:309
  124.9 1.6 %shard_map.98 = (bf16[4096,128]{1,0:T(8,128)(2,1)}, bf16[128,4096]{1,0:T(8,128)(2,1)}) custom-call(bf16[16,128,128]{2,1,0:T(8,128)(2,1)S(1)} %get-tuple-element.34.in_mine, bf16[128,2048]{1,0:T(8,128)(2,1)S(1)} %get-tuple-element.35.out_mine, bf16[16,128,128]{2,1,0:T(8,128)(2,1)S(1)} %collective-permute-done.12.in_sib, ...), custom_call_target="tpu_custom_call" | custom-call | tf_op jit(solution)/shard_map/pallas_call | solution.py:253
  126.6 1.0 shard_map.96.table_ref
  127.6 10.9 %all-to-all-done.2.back_ref = bf16[16,20,128]{2,1,0:T(8,128)(2,1)S(1)} async-done(((bf16[16,20,128]{2,1,0:T(8,128)(2,1)}), bf16[16,20,128]{2,1,0:T(8,128)(2,1)S(1)}, u32[]{:S(2)}, u32[]{:S(2)}) %all-to-all-start.2) | async-done | bytes 81952 | tf_op jit(solution)/shard_map/all_to_all | solution.py:309
  138.5 0.8 shard_map.97
  (6 shorter events, 0.0 us)
Async XLA Ops:
  2.5 34.1 %all-to-all-start = ((bf16[16,40,128]{2,1,0:T(8,128)(2,1)}), bf16[16,40,128]{2,1,0:T(8,128)(2,1)S(1)}, u32[]{:S(2)}, u32[]{:S(2)}) async-start(bf16[16,40,128]{2,1,0:T(8,128)(2,1)} %shard_map.85.after_ref), calls=%async_computation | async-start | bytes 327680 | tf_op jit(solution)/shard_map/all_to_all | solution.py:279
  22.8 31.1 %collective-permute-start = (bf16[16,128,128]{2,1,0:T(8,128)(2,1)}, bf16[16,128,128]{2,1,0:T(8,128)(2,1)S(1)}, u32[]{:S(2)}, u32[]{:S(2)}) collective-permute-start(bf16[16,128,128]{2,1,0:T(8,128)(2,1)} %get-tuple-element.21), channel_id=1, source_target_pairs={{0,16},{16,0},{1,17},{17,1},{2,18},{18,2},{3,19},{19,3},{4,20},{20... | collective-permute-start | bytes 1572872 | tf_op jit(solution)/shard_map/ppermute | solution.py:265
  24.7 53.4 %copy-start = (bf16[1,4096,128]{2,1,0:T(8,128)(2,1)S(1)}, bf16[1,4096,128]{2,1,0:T(8,128)(2,1)}, u32[]{:S(2)}) copy-start(bf16[1,4096,128]{2,1,0:T(8,128)(2,1)} %param.10) | copy-start | bytes 3145732
  24.8 53.4 %copy-start.1 = (bf16[1,128,4096]{2,1,0:T(8,128)(2,1)S(1)}, bf16[1,128,4096]{2,1,0:T(8,128)(2,1)}, u32[]{:S(2)}) copy-start(bf16[1,128,4096]{2,1,0:T(8,128)(2,1)} %param.11) | copy-start | bytes 3145732
  24.8 29.2 %collective-permute-start.1 = (bf16[16,128,128]{2,1,0:T(8,128)(2,1)}, bf16[16,128,128]{2,1,0:T(8,128)(2,1)S(1)}, u32[]{:S(2)}, u32[]{:S(2)}) collective-permute-start(bf16[16,128,128]{2,1,0:T(8,128)(2,1)} %get-tuple-element.22), channel_id=1, source_target_pairs={{0,16},{16,0},{1,17},{17,1},{2,18},{18,2},{3,19},{19,3},{4,20},{20... | collective-permute-start | bytes 1572872 | tf_op jit(solution)/shard_map/ppermute | solution.py:265
  54.0 13.8 %collective-permute-start.4 = (bf16[32,40,128]{2,1,0:T(8,128)(2,1)S(1)}, bf16[32,40,128]{2,1,0:T(8,128)(2,1)S(1)}, u32[]{:S(2)}, u32[]{:S(2)}) collective-permute-start(bf16[32,40,128]{2,1,0:T(8,128)(2,1)S(1)} %get-tuple-element.39), channel_id=1, source_target_pairs={{0,384},{16,144},{128,256},{144,16},{256,128},{272,400},{384,0},{4... | collective-permute-start | bytes 983048 | tf_op jit(solution)/shard_map/ppermute | solution.py:261
  58.9 12.5 %collective-permute-start.2 = (bf16[32,40,128]{2,1,0:T(8,128)(2,1)S(1)}, bf16[32,40,128]{2,1,0:T(8,128)(2,1)S(1)}, u32[]{:S(2)}, u32[]{:S(2)}) collective-permute-start(bf16[32,40,128]{2,1,0:T(8,128)(2,1)S(1)} %get-tuple-element.40), channel_id=1, source_target_pairs={{0,128},{16,400},{128,0},{144,272},{256,384},{272,144},{384,256},{... | collective-permute-start | bytes 983048 | tf_op jit(solution)/shard_map/ppermute | solution.py:261
  61.0 17.2 %collective-permute-start.7 = (bf16[32,40,128]{2,1,0:T(8,128)(2,1)S(1)}, bf16[32,40,128]{2,1,0:T(8,128)(2,1)S(1)}, u32[]{:S(2)}, u32[]{:S(2)}) collective-permute-start(bf16[32,40,128]{2,1,0:T(8,128)(2,1)S(1)} %get-tuple-element.39), channel_id=1, source_target_pairs={{0,128},{16,400},{128,0},{144,272},{256,384},{272,144},{384,256},{... | collective-permute-start | bytes 983048 | tf_op jit(solution)/shard_map/ppermute | solution.py:261
  64.8 14.2 %collective-permute-start.6 = (bf16[32,40,128]{2,1,0:T(8,128)(2,1)S(1)}, bf16[32,40,128]{2,1,0:T(8,128)(2,1)S(1)}, u32[]{:S(2)}, u32[]{:S(2)}) collective-permute-start(bf16[32,40,128]{2,1,0:T(8,128)(2,1)S(1)} %get-tuple-element.40), channel_id=1, source_target_pairs={{0,384},{16,144},{128,256},{144,16},{256,128},{272,400},{384,0},{4... | collective-permute-start | bytes 983048 | tf_op jit(solution)/shard_map/ppermute | solution.py:261
  67.8 13.9 %collective-permute-start.5 = (bf16[32,40,128]{2,1,0:T(8,128)(2,1)S(1)}, bf16[32,40,128]{2,1,0:T(8,128)(2,1)S(1)}, u32[]{:S(2)}, u32[]{:S(2)}) collective-permute-start(bf16[32,40,128]{2,1,0:T(8,128)(2,1)S(1)} %collective-permute-done.4.second_b.refs_4_), channel_id=1, source_target_pairs={{0,128},{16,400},{128,0},{144,272},{256,384},{272,144},{384,256},{... | collective-permute-start | bytes 983048 | tf_op jit(solution)/shard_map/ppermute | solution.py:261
  71.4 10.2 %collective-permute-start.3 = (bf16[32,40,128]{2,1,0:T(8,128)(2,1)S(1)}, bf16[32,40,128]{2,1,0:T(8,128)(2,1)S(1)}, u32[]{:S(2)}, u32[]{:S(2)}) collective-permute-start(bf16[32,40,128]{2,1,0:T(8,128)(2,1)S(1)} %collective-permute-done.2.first_a.refs_1_), channel_id=1, source_target_pairs={{0,384},{16,144},{128,256},{144,16},{256,128},{272,400},{384,0},{4... | collective-permute-start | bytes 983048 | tf_op jit(solution)/shard_map/ppermute | solution.py:261
  82.2 3.5 %collective-permute-start.8 = (bf16[640,256]{1,0:T(8,128)(2,1)S(1)}, bf16[640,256]{1,0:T(8,128)(2,1)S(1)}, u32[]{:S(2)}, u32[]{:S(2)}) collective-permute-start(bf16[640,256]{1,0:T(8,128)(2,1)S(1)} %get-tuple-element.27), channel_id=1, source_target_pairs={{0,16},{16,0},{1,17},{17,1},{2,18},{18,2},{3,19},{19,3},{4,20},{20... | collective-permute-start | bytes 983048 | tf_op jit(solution)/shard_map/ppermute | solution.py:265
  86.3 10.2 %collective-permute-start.9 = (bf16[4,320,128]{2,1,0:T(8,128)(2,1)S(1)}, bf16[4,320,128]{2,1,0:T(8,128)(2,1)S(1)}, u32[]{:S(2)}, u32[]{:S(2)}) collective-permute-start(bf16[4,320,128]{2,1,0:T(8,128)(2,1)S(1)} %get-tuple-element.31), channel_id=1, source_target_pairs={{0,384},{16,144},{128,256},{144,16},{256,128},{272,400},{384,0},{4... | collective-permute-start | bytes 983048 | tf_op jit(solution)/shard_map/ppermute | solution.py:261
  89.9 10.6 %collective-permute-start.11 = (bf16[4,320,128]{2,1,0:T(8,128)(2,1)S(1)}, bf16[4,320,128]{2,1,0:T(8,128)(2,1)S(1)}, u32[]{:S(2)}, u32[]{:S(2)}) collective-permute-start(bf16[4,320,128]{2,1,0:T(8,128)(2,1)S(1)} %get-tuple-element.32), channel_id=1, source_target_pairs={{0,384},{16,144},{128,256},{144,16},{256,128},{272,400},{384,0},{4... | collective-permute-start | bytes 983048 | tf_op jit(solution)/shard_map/ppermute | solution.py:261
  96.5 9.0 %collective-permute-start.10 = (bf16[4,320,128]{2,1,0:T(8,128)(2,1)S(1)}, bf16[4,320,128]{2,1,0:T(8,128)(2,1)S(1)}, u32[]{:S(2)}, u32[]{:S(2)}) collective-permute-start(bf16[4,320,128]{2,1,0:T(8,128)(2,1)S(1)} %shard_map.92.refs_7_), channel_id=1, source_target_pairs={{0,128},{16,400},{128,0},{144,272},{256,384},{272,144},{384,256},{... | collective-permute-start | bytes 983048 | tf_op jit(solution)/shard_map/ppermute | solution.py:261
  106.4 12.3 %all-to-all-start.1 = ((bf16[4,320,128]{2,1,0:T(8,128)(2,1)}), bf16[4,320,128]{2,1,0:T(8,128)(2,1)S(1)}, u32[]{:S(2)}, u32[]{:S(2)}) async-start(bf16[4,320,128]{2,1,0:T(8,128)(2,1)} %shard_map.94), calls=%async_computation.1 | async-start | bytes 655360 | tf_op jit(solution)/shard_map/all_to_all | solution.py:306
  109.8 15.1 %collective-permute-start.13 = (bf16[16,128,128]{2,1,0:T(8,128)(2,1)S(1)}, bf16[16,128,128]{2,1,0:T(8,128)(2,1)S(1)}, u32[]{:S(2)}, u32[]{:S(2)}) collective-permute-start(bf16[16,128,128]{2,1,0:T(8,128)(2,1)S(1)} %get-tuple-element.36), channel_id=1, source_target_pairs={{0,16},{16,0},{1,17},{17,1},{2,18},{18,2},{3,19},{19,3},{4,20},{20... | collective-permute-start | bytes 1572872 | tf_op jit(solution)/shard_map/ppermute | solution.py:265
  111.7 13.2 %collective-permute-start.12 = (bf16[16,128,128]{2,1,0:T(8,128)(2,1)S(1)}, bf16[16,128,128]{2,1,0:T(8,128)(2,1)S(1)}, u32[]{:S(2)}, u32[]{:S(2)}) collective-permute-start(bf16[16,128,128]{2,1,0:T(8,128)(2,1)S(1)} %get-tuple-element.33.after_ref), channel_id=1, source_target_pairs={{0,16},{16,0},{1,17},{17,1},{2,18},{18,2},{3,19},{19,3},{4,20},{20... | collective-permute-start | bytes 1572872 | tf_op jit(solution)/shard_map/ppermute | solution.py:265
  119.4 19.1 %all-to-all-start.2 = ((bf16[16,20,128]{2,1,0:T(8,128)(2,1)}), bf16[16,20,128]{2,1,0:T(8,128)(2,1)S(1)}, u32[]{:S(2)}, u32[]{:S(2)}) async-start(bf16[16,20,128]{2,1,0:T(8,128)(2,1)} %shard_map.95.after_ref), calls=%async_computation.2 | async-start | bytes 196608 | tf_op jit(solution)/shard_map/all_to_all | solution.py:309

commit v8 on v7

--- a/solution.py
+++ b/solution.py
@@ -48,10 +48,12 @@
     table = jnp.broadcast_to(place[:, None, :], shape) == slot
     weight = jnp.where(table, jnp.broadcast_to(gate[:, None, :], shape), 0.0)
     scale = jnp.sum(weight, axis=2, keepdims=True).reshape(ROWS, 1)
-    pick = jnp.where(table, 1.0, 0.0).reshape(ROWS, TOK).astype(BF16)
-    rows_in = jnp.dot(pick, tok_ref[...], preferred_element_type=F32)
-    rows_dy = jnp.dot(pick, dy_ref[...], preferred_element_type=F32)
-    out = jnp.where(row.reshape(ROWS, COLS) < CAP, rows_in, scale * rows_dy)
+    is_in = row.reshape(ROWS, TOK) < CAP
+    pick = jnp.where(table, 1.0, 0.0).reshape(ROWS, TOK)
+    pick = joined(jnp.where(is_in, pick, 0.0), jnp.where(is_in, 0.0, pick)).astype(BF16)
+    source = jnp.concatenate([tok_ref[...], dy_ref[...]], axis=0)
+    out = jnp.dot(pick, source, preferred_element_type=F32)
+    out = jnp.where(is_in, out, scale * out)
     out_ref[...] = out.astype(BF16).reshape(EXPERTS, MSG, COLS)
 
 

time: 140 us -> 140 us (level)
  no operation moved by 1% of the time
where the time goes in v8:
time: 140 us; the launch traced here: 139 us
  starting transfers between devices  65.1 us (46%)
  waiting for transfers between devices  41.7 us (30%)
  blocking collectives  17.3 us (12%)
  Pallas kernels  14.1 us (10%)
    ppermute x9, starting transfers between devices, partner(): lax.ppermute(value, ('y', 'c'), [(i * NC + c, to[c][which][i] * NC + c) f...  27.3 us
    all_to_all x1, starting transfers between devices, on_device(): received = lax.all_to_all(send, ('zh', 'x'), 0, 0, tiled=True)  18.1 us
    all_gather x1, blocking collectives, on_device(): own = lax.all_gather(received, 'zl', axis=0, tiled=True)  17.3 us
    ppermute x9, waiting for transfers between devices, partner(): lax.ppermute(value, ('y', 'c'), [(i * NC + c, to[c][which][i] * NC + c) f...  15.4 us
    pallas_call x14, Pallas kernels, run(): pl.pallas_call(kernel, out_shape=outs, in_specs=specs, out_specs=out_spec...  14.1 us
    all_to_all x1, waiting for transfers between devices, on_device(): back = lax.all_to_all(total, ('zh', 'x'), 0, 0, tiled=True)  10.9 us
    ppermute x5, starting transfers between devices, across(): return lax.ppermute(value, 'c', [(0, 1), (1, 0)])  10.7 us
    all_to_all x1, waiting for transfers between devices, on_device(): received = lax.all_to_all(send, ('zh', 'x'), 0, 0, tiled=True)  9.31 us
  transfers between devices with their start and end apart: 17, of which 10 were waited for; matrix products, arithmetic and copies ran while one was open for 0% of the time, Pallas kernels for 7%

profile of v8, /device:TPU:2, one launch (start us, length us, event | category | flops | bytes accessed | tf_op | source)
XLA Modules:
  0.0 139.3 jit_solution(4756873132472566529)
XLA Ops:
  0.6 1.8 %shard_map.85.after_ref = bf16[16,40,128]{2,1,0:T(8,128)(2,1)} custom-call(s32[2,128]{1,0:T(2,128)} %bitcast.17, f32[2,128]{1,0:T(2,128)} %bitcast.19, bf16[128,128]{1,0:T(8,128)(2,1)} %tok_ref.1, bf16[128,128]{1,0:T(8,128)(2,1)} %dy_ref.1), custom_call_target="tpu_custom_call" | custom-call | tf_op jit(solution)/shard_map/pallas_call | solution.py:255
  2.5 18.1 %all-to-all-start = ((bf16[16,40,128]{2,1,0:T(8,128)(2,1)}), bf16[16,40,128]{2,1,0:T(8,128)(2,1)S(1)}, u32[]{:S(2)}, u32[]{:S(2)}) async-start(bf16[16,40,128]{2,1,0:T(8,128)(2,1)} %shard_map.85.after_ref), calls=%async_computation | async-start | bytes 327680 | tf_op jit(solution)/shard_map/all_to_all | solution.py:281
  20.6 2.2 %shard_map.86 = (bf16[16,128,128]{2,1,0:T(8,128)(2,1)}, bf16[16,128,128]{2,1,0:T(8,128)(2,1)}) custom-call(bf16[16,2,128,128]{3,2,1,0:T(8,128)(2,1)} %bitcast.7, bf16[128,4096]{1,0:T(8,128)(2,1)} %bitcast.13, bf16[16,40,128]{2,1,0:T(8,128)(2,1)} %shard_map.85.after_ref), custom_call_target="tpu_custom_call" | custom-call | tf_op jit(solution)/shard_map/pallas_call | solution.py:255
  22.8 1.9 %collective-permute-start = (bf16[16,128,128]{2,1,0:T(8,128)(2,1)}, bf16[16,128,128]{2,1,0:T(8,128)(2,1)S(1)}, u32[]{:S(2)}, u32[]{:S(2)}) collective-permute-start(bf16[16,128,128]{2,1,0:T(8,128)(2,1)} %get-tuple-element.21), channel_id=1, source_target_pairs={{0,16},{16,0},{1,17},{17,1},{2,18},{18,2},{3,19},{19,3},{4,20},{20... | collective-permute-start | bytes 1572872 | tf_op jit(solution)/shard_map/ppermute | solution.py:267
  24.7 0.0 copy-start
  24.8 0.0 copy-start.1
  24.8 2.5 %collective-permute-start.1 = (bf16[16,128,128]{2,1,0:T(8,128)(2,1)}, bf16[16,128,128]{2,1,0:T(8,128)(2,1)S(1)}, u32[]{:S(2)}, u32[]{:S(2)}) collective-permute-start(bf16[16,128,128]{2,1,0:T(8,128)(2,1)} %get-tuple-element.22), channel_id=1, source_target_pairs={{0,16},{16,0},{1,17},{17,1},{2,18},{18,2},{3,19},{19,3},{4,20},{20... | collective-permute-start | bytes 1572872 | tf_op jit(solution)/shard_map/ppermute | solution.py:267
  27.3 9.3 %all-to-all-done = bf16[16,40,128]{2,1,0:T(8,128)(2,1)S(1)} async-done(((bf16[16,40,128]{2,1,0:T(8,128)(2,1)}), bf16[16,40,128]{2,1,0:T(8,128)(2,1)S(1)}, u32[]{:S(2)}, u32[]{:S(2)}) %all-to-all-start) | async-done | bytes 163872 | tf_op jit(solution)/shard_map/all_to_all | solution.py:281
  36.6 17.3 %all_gather.3.own.refs_0_ = bf16[64,40,128]{2,1,0:T(8,128)(2,1)S(1)} all-gather(bf16[16,40,128]{2,1,0:T(8,128)(2,1)S(1)} %all-to-all-done), channel_id=1, replica_groups=mesh['y'=4,'zl'=4,'c'=2,'zh'=4,'x'=4] {'zl'}, dimensions={0}, use_global_device_ids=true | all-gather | bytes 819200 | tf_op jit(solution)/shard_map/all_gather | solution.py:282
  53.9 0.1 fusion
  54.0 4.9 %collective-permute-start.4 = (bf16[32,40,128]{2,1,0:T(8,128)(2,1)S(1)}, bf16[32,40,128]{2,1,0:T(8,128)(2,1)S(1)}, u32[]{:S(2)}, u32[]{:S(2)}) collective-permute-start(bf16[32,40,128]{2,1,0:T(8,128)(2,1)S(1)} %get-tuple-element.39), channel_id=1, source_target_pairs={{0,384},{16,144},{128,256},{144,16},{256,128},{272,400},{384,0},{4... | collective-permute-start | bytes 983048 | tf_op jit(solution)/shard_map/ppermute | solution.py:263
  58.9 2.0 %collective-permute-start.2 = (bf16[32,40,128]{2,1,0:T(8,128)(2,1)S(1)}, bf16[32,40,128]{2,1,0:T(8,128)(2,1)S(1)}, u32[]{:S(2)}, u32[]{:S(2)}) collective-permute-start(bf16[32,40,128]{2,1,0:T(8,128)(2,1)S(1)} %get-tuple-element.40), channel_id=1, source_target_pairs={{0,128},{16,400},{128,0},{144,272},{256,384},{272,144},{384,256},{... | collective-permute-start | bytes 983048 | tf_op jit(solution)/shard_map/ppermute | solution.py:263
  61.0 3.8 %collective-permute-start.7 = (bf16[32,40,128]{2,1,0:T(8,128)(2,1)S(1)}, bf16[32,40,128]{2,1,0:T(8,128)(2,1)S(1)}, u32[]{:S(2)}, u32[]{:S(2)}) collective-permute-start(bf16[32,40,128]{2,1,0:T(8,128)(2,1)S(1)} %get-tuple-element.39), channel_id=1, source_target_pairs={{0,128},{16,400},{128,0},{144,272},{256,384},{272,144},{384,256},{... | collective-permute-start | bytes 983048 | tf_op jit(solution)/shard_map/ppermute | solution.py:263
  64.8 2.1 %collective-permute-start.6 = (bf16[32,40,128]{2,1,0:T(8,128)(2,1)S(1)}, bf16[32,40,128]{2,1,0:T(8,128)(2,1)S(1)}, u32[]{:S(2)}, u32[]{:S(2)}) collective-permute-start(bf16[32,40,128]{2,1,0:T(8,128)(2,1)S(1)} %get-tuple-element.40), channel_id=1, source_target_pairs={{0,384},{16,144},{128,256},{144,16},{256,128},{272,400},{384,0},{4... | collective-permute-start | bytes 983048 | tf_op jit(solution)/shard_map/ppermute | solution.py:263
  66.9 0.8 collective-permute-done.4.second_b.refs_4_
  67.8 2.3 %collective-permute-start.5 = (bf16[32,40,128]{2,1,0:T(8,128)(2,1)S(1)}, bf16[32,40,128]{2,1,0:T(8,128)(2,1)S(1)}, u32[]{:S(2)}, u32[]{:S(2)}) collective-permute-start(bf16[32,40,128]{2,1,0:T(8,128)(2,1)S(1)} %collective-permute-done.4.second_b.refs_4_), channel_id=1, source_target_pairs={{0,128},{16,400},{128,0},{144,272},{256,384},{272,144},{384,256},{... | collective-permute-start | bytes 983048 | tf_op jit(solution)/shard_map/ppermute | solution.py:263
  70.0 1.4 collective-permute-done.2.first_a.refs_1_
  71.4 3.2 %collective-permute-start.3 = (bf16[32,40,128]{2,1,0:T(8,128)(2,1)S(1)}, bf16[32,40,128]{2,1,0:T(8,128)(2,1)S(1)}, u32[]{:S(2)}, u32[]{:S(2)}) collective-permute-start(bf16[32,40,128]{2,1,0:T(8,128)(2,1)S(1)} %collective-permute-done.2.first_a.refs_1_), channel_id=1, source_target_pairs={{0,384},{16,144},{128,256},{144,16},{256,128},{272,400},{384,0},{4... | collective-permute-start | bytes 983048 | tf_op jit(solution)/shard_map/ppermute | solution.py:263
  74.6 3.5 %collective-permute-done.7.first_b.refs_2_ = bf16[32,40,128]{2,1,0:T(8,128)(2,1)S(1)} collective-permute-done((bf16[32,40,128]{2,1,0:T(8,128)(2,1)S(1)}, bf16[32,40,128]{2,1,0:T(8,128)(2,1)S(1)}, u32[]{:S(2)}, u32[]{:S(2)}) %collective-permute-start.7) | collective-permute-done | bytes 327712 | tf_op jit(solution)/shard_map/ppermute | solution.py:263
  78.2 0.9 shard_map.87.before_ref
  79.0 0.0 collective-permute-done.6.second_a.refs_3_
  79.0 0.5 shard_map.88.before_ref
  79.6 2.1 %collective-permute-done.5.last_b.refs_6_ = bf16[32,40,128]{2,1,0:T(8,128)(2,1)S(1)} collective-permute-done((bf16[32,40,128]{2,1,0:T(8,128)(2,1)S(1)}, bf16[32,40,128]{2,1,0:T(8,128)(2,1)S(1)}, u32[]{:S(2)}, u32[]{:S(2)}) %collective-permute-start.5) | collective-permute-done | bytes 327712 | tf_op jit(solution)/shard_map/ppermute | solution.py:263
  81.7 0.0 collective-permute-done.3.last_a.refs_5_
  81.7 0.5 shard_map.89
  82.2 1.9 %collective-permute-start.8 = (bf16[640,256]{1,0:T(8,128)(2,1)S(1)}, bf16[640,256]{1,0:T(8,128)(2,1)S(1)}, u32[]{:S(2)}, u32[]{:S(2)}) collective-permute-start(bf16[640,256]{1,0:T(8,128)(2,1)S(1)} %get-tuple-element.27), channel_id=1, source_target_pairs={{0,16},{16,0},{1,17},{17,1},{2,18},{18,2},{3,19},{19,3},{4,20},{20... | collective-permute-start | bytes 983048 | tf_op jit(solution)/shard_map/ppermute | solution.py:267
  84.1 1.6 %collective-permute-done.8.part_sib_ref = bf16[640,256]{1,0:T(8,128)(2,1)S(1)} collective-permute-done((bf16[640,256]{1,0:T(8,128)(2,1)S(1)}, bf16[640,256]{1,0:T(8,128)(2,1)S(1)}, u32[]{:S(2)}, u32[]{:S(2)}) %collective-permute-start.8) | collective-permute-done | bytes 327712 | tf_op jit(solution)/shard_map/ppermute | solution.py:267
  85.7 0.6 shard_map.90
  86.3 3.1 %collective-permute-start.9 = (bf16[4,320,128]{2,1,0:T(8,128)(2,1)S(1)}, bf16[4,320,128]{2,1,0:T(8,128)(2,1)S(1)}, u32[]{:S(2)}, u32[]{:S(2)}) collective-permute-start(bf16[4,320,128]{2,1,0:T(8,128)(2,1)S(1)} %get-tuple-element.31), channel_id=1, source_target_pairs={{0,384},{16,144},{128,256},{144,16},{256,128},{272,400},{384,0},{4... | collective-permute-start | bytes 983048 | tf_op jit(solution)/shard_map/ppermute | solution.py:263
  89.4 0.5 shard_map.91
  89.9 3.9 %collective-permute-start.11 = (bf16[4,320,128]{2,1,0:T(8,128)(2,1)S(1)}, bf16[4,320,128]{2,1,0:T(8,128)(2,1)S(1)}, u32[]{:S(2)}, u32[]{:S(2)}) collective-permute-start(bf16[4,320,128]{2,1,0:T(8,128)(2,1)S(1)} %get-tuple-element.32), channel_id=1, source_target_pairs={{0,384},{16,144},{128,256},{144,16},{256,128},{272,400},{384,0},{4... | collective-permute-start | bytes 983048 | tf_op jit(solution)/shard_map/ppermute | solution.py:263
  93.8 2.6 %collective-permute-done.9.passed_ref = bf16[4,320,128]{2,1,0:T(8,128)(2,1)S(1)} collective-permute-done((bf16[4,320,128]{2,1,0:T(8,128)(2,1)S(1)}, bf16[4,320,128]{2,1,0:T(8,128)(2,1)S(1)}, u32[]{:S(2)}, u32[]{:S(2)}) %collective-permute-start.9) | collective-permute-done | bytes 327712 | tf_op jit(solution)/shard_map/ppermute | solution.py:263
  96.5 0.1 shard_map.92.refs_7_
  96.5 1.9 %collective-permute-start.10 = (bf16[4,320,128]{2,1,0:T(8,128)(2,1)S(1)}, bf16[4,320,128]{2,1,0:T(8,128)(2,1)S(1)}, u32[]{:S(2)}, u32[]{:S(2)}) collective-permute-start(bf16[4,320,128]{2,1,0:T(8,128)(2,1)S(1)} %shard_map.92.refs_7_), channel_id=1, source_target_pairs={{0,128},{16,400},{128,0},{144,272},{256,384},{272,144},{384,256},{... | collective-permute-start | bytes 983048 | tf_op jit(solution)/shard_map/ppermute | solution.py:263
  98.5 2.0 %shard_map.93 = (bf16[16,128,128]{2,1,0:T(8,128)(2,1)S(1)}, bf16[128,2048]{1,0:T(8,128)(2,1)S(1)}, bf16[16,128,128]{2,1,0:T(8,128)(2,1)S(1)}, bf16[16,128,128]{2,1,0:T(8,128)(2,1)S(1)}) custom-call(f32[640,256]{1,0:T(8,128)S(1)} %get-tuple-element.26.part_ref, bf16[640,256]{1,0:T(8,128)(2,1)S(1)} %collective-permute-done.8.part_sib_ref, ...), custom_call_target="tpu_custom_call" | custom-call | tf_op jit(solution)/shard_map/pallas_call | solution.py:255
  100.5 0.0 collective-permute-done.11.second_ref
  100.5 5.0 %collective-permute-done.10.first_ref = bf16[4,320,128]{2,1,0:T(8,128)(2,1)S(1)} collective-permute-done((bf16[4,320,128]{2,1,0:T(8,128)(2,1)S(1)}, bf16[4,320,128]{2,1,0:T(8,128)(2,1)S(1)}, u32[]{:S(2)}, u32[]{:S(2)}) %collective-permute-start.10) | collective-permute-done | bytes 327712 | tf_op jit(solution)/shard_map/ppermute | solution.py:263
  105.5 0.8 shard_map.94
  106.4 3.5 %all-to-all-start.1 = ((bf16[4,320,128]{2,1,0:T(8,128)(2,1)}), bf16[4,320,128]{2,1,0:T(8,128)(2,1)S(1)}, u32[]{:S(2)}, u32[]{:S(2)}) async-start(bf16[4,320,128]{2,1,0:T(8,128)(2,1)} %shard_map.94), calls=%async_computation.1 | async-start | bytes 655360 | tf_op jit(solution)/shard_map/all_to_all | solution.py:308
  109.8 1.9 %collective-permute-start.13 = (bf16[16,128,128]{2,1,0:T(8,128)(2,1)S(1)}, bf16[16,128,128]{2,1,0:T(8,128)(2,1)S(1)}, u32[]{:S(2)}, u32[]{:S(2)}) collective-permute-start(bf16[16,128,128]{2,1,0:T(8,128)(2,1)S(1)} %get-tuple-element.36), channel_id=1, source_target_pairs={{0,16},{16,0},{1,17},{17,1},{2,18},{18,2},{3,19},{19,3},{4,20},{20... | collective-permute-start | bytes 1572872 | tf_op jit(solution)/shard_map/ppermute | solution.py:267
  111.7 2.4 %collective-permute-start.12 = (bf16[16,128,128]{2,1,0:T(8,128)(2,1)S(1)}, bf16[16,128,128]{2,1,0:T(8,128)(2,1)S(1)}, u32[]{:S(2)}, u32[]{:S(2)}) collective-permute-start(bf16[16,128,128]{2,1,0:T(8,128)(2,1)S(1)} %get-tuple-element.33.after_ref), channel_id=1, source_target_pairs={{0,16},{16,0},{1,17},{17,1},{2,18},{18,2},{3,19},{19,3},{4,20},{20... | collective-permute-start | bytes 1572872 | tf_op jit(solution)/shard_map/ppermute | solution.py:267
  114.2 4.5 %all-to-all-done.1.parts_ref = bf16[4,320,128]{2,1,0:T(8,128)(2,1)S(1)} async-done(((bf16[4,320,128]{2,1,0:T(8,128)(2,1)}), bf16[4,320,128]{2,1,0:T(8,128)(2,1)S(1)}, u32[]{:S(2)}, u32[]{:S(2)}) %all-to-all-start.1) | async-done | bytes 327712 | tf_op jit(solution)/shard_map/all_to_all | solution.py:308
  118.7 0.7 shard_map.95.after_ref
  119.4 5.6 %all-to-all-start.2 = ((bf16[16,20,128]{2,1,0:T(8,128)(2,1)}), bf16[16,20,128]{2,1,0:T(8,128)(2,1)S(1)}, u32[]{:S(2)}, u32[]{:S(2)}) async-start(bf16[16,20,128]{2,1,0:T(8,128)(2,1)} %shard_map.95.after_ref), calls=%async_computation.2 | async-start | bytes 196608 | tf_op jit(solution)/shard_map/all_to_all | solution.py:311
  124.9 1.6 %shard_map.98 = (bf16[4096,128]{1,0:T(8,128)(2,1)}, bf16[128,4096]{1,0:T(8,128)(2,1)}) custom-call(bf16[16,128,128]{2,1,0:T(8,128)(2,1)S(1)} %get-tuple-element.34.in_mine, bf16[128,2048]{1,0:T(8,128)(2,1)S(1)} %get-tuple-element.35.out_mine, bf16[16,128,128]{2,1,0:T(8,128)(2,1)S(1)} %collective-permute-done.12.in_sib, ...), custom_call_target="tpu_custom_call" | custom-call | tf_op jit(solution)/shard_map/pallas_call | solution.py:255
  126.6 1.0 shard_map.96.table_ref
  127.6 10.9 %all-to-all-done.2.back_ref = bf16[16,20,128]{2,1,0:T(8,128)(2,1)S(1)} async-done(((bf16[16,20,128]{2,1,0:T(8,128)(2,1)}), bf16[16,20,128]{2,1,0:T(8,128)(2,1)S(1)}, u32[]{:S(2)}, u32[]{:S(2)}) %all-to-all-start.2) | async-done | bytes 81952 | tf_op jit(solution)/shard_map/all_to_all | solution.py:311
  138.5 0.8 shard_map.97
  (6 shorter events, 0.0 us)
Async XLA Ops:
  2.5 34.1 %all-to-all-start = ((bf16[16,40,128]{2,1,0:T(8,128)(2,1)}), bf16[16,40,128]{2,1,0:T(8,128)(2,1)S(1)}, u32[]{:S(2)}, u32[]{:S(2)}) async-start(bf16[16,40,128]{2,1,0:T(8,128)(2,1)} %shard_map.85.after_ref), calls=%async_computation | async-start | bytes 327680 | tf_op jit(solution)/shard_map/all_to_all | solution.py:281
  22.8 31.1 %collective-permute-start = (bf16[16,128,128]{2,1,0:T(8,128)(2,1)}, bf16[16,128,128]{2,1,0:T(8,128)(2,1)S(1)}, u32[]{:S(2)}, u32[]{:S(2)}) collective-permute-start(bf16[16,128,128]{2,1,0:T(8,128)(2,1)} %get-tuple-element.21), channel_id=1, source_target_pairs={{0,16},{16,0},{1,17},{17,1},{2,18},{18,2},{3,19},{19,3},{4,20},{20... | collective-permute-start | bytes 1572872 | tf_op jit(solution)/shard_map/ppermute | solution.py:267
  24.7 53.4 %copy-start = (bf16[1,4096,128]{2,1,0:T(8,128)(2,1)S(1)}, bf16[1,4096,128]{2,1,0:T(8,128)(2,1)}, u32[]{:S(2)}) copy-start(bf16[1,4096,128]{2,1,0:T(8,128)(2,1)} %param.10) | copy-start | bytes 3145732
  24.8 53.4 %copy-start.1 = (bf16[1,128,4096]{2,1,0:T(8,128)(2,1)S(1)}, bf16[1,128,4096]{2,1,0:T(8,128)(2,1)}, u32[]{:S(2)}) copy-start(bf16[1,128,4096]{2,1,0:T(8,128)(2,1)} %param.11) | copy-start | bytes 3145732
  24.8 29.2 %collective-permute-start.1 = (bf16[16,128,128]{2,1,0:T(8,128)(2,1)}, bf16[16,128,128]{2,1,0:T(8,128)(2,1)S(1)}, u32[]{:S(2)}, u32[]{:S(2)}) collective-permute-start(bf16[16,128,128]{2,1,0:T(8,128)(2,1)} %get-tuple-element.22), channel_id=1, source_target_pairs={{0,16},{16,0},{1,17},{17,1},{2,18},{18,2},{3,19},{19,3},{4,20},{20... | collective-permute-start | bytes 1572872 | tf_op jit(solution)/shard_map/ppermute | solution.py:267
  54.0 13.8 %collective-permute-start.4 = (bf16[32,40,128]{2,1,0:T(8,128)(2,1)S(1)}, bf16[32,40,128]{2,1,0:T(8,128)(2,1)S(1)}, u32[]{:S(2)}, u32[]{:S(2)}) collective-permute-start(bf16[32,40,128]{2,1,0:T(8,128)(2,1)S(1)} %get-tuple-element.39), channel_id=1, source_target_pairs={{0,384},{16,144},{128,256},{144,16},{256,128},{272,400},{384,0},{4... | collective-permute-start | bytes 983048 | tf_op jit(solution)/shard_map/ppermute | solution.py:263
  58.9 12.5 %collective-permute-start.2 = (bf16[32,40,128]{2,1,0:T(8,128)(2,1)S(1)}, bf16[32,40,128]{2,1,0:T(8,128)(2,1)S(1)}, u32[]{:S(2)}, u32[]{:S(2)}) collective-permute-start(bf16[32,40,128]{2,1,0:T(8,128)(2,1)S(1)} %get-tuple-element.40), channel_id=1, source_target_pairs={{0,128},{16,400},{128,0},{144,272},{256,384},{272,144},{384,256},{... | collective-permute-start | bytes 983048 | tf_op jit(solution)/shard_map/ppermute | solution.py:263
  61.0 17.2 %collective-permute-start.7 = (bf16[32,40,128]{2,1,0:T(8,128)(2,1)S(1)}, bf16[32,40,128]{2,1,0:T(8,128)(2,1)S(1)}, u32[]{:S(2)}, u32[]{:S(2)}) collective-permute-start(bf16[32,40,128]{2,1,0:T(8,128)(2,1)S(1)} %get-tuple-element.39), channel_id=1, source_target_pairs={{0,128},{16,400},{128,0},{144,272},{256,384},{272,144},{384,256},{... | collective-permute-start | bytes 983048 | tf_op jit(solution)/shard_map/ppermute | solution.py:263
  64.8 14.2 %collective-permute-start.6 = (bf16[32,40,128]{2,1,0:T(8,128)(2,1)S(1)}, bf16[32,40,128]{2,1,0:T(8,128)(2,1)S(1)}, u32[]{:S(2)}, u32[]{:S(2)}) collective-permute-start(bf16[32,40,128]{2,1,0:T(8,128)(2,1)S(1)} %get-tuple-element.40), channel_id=1, source_target_pairs={{0,384},{16,144},{128,256},{144,16},{256,128},{272,400},{384,0},{4... | collective-permute-start | bytes 983048 | tf_op jit(solution)/shard_map/ppermute | solution.py:263
  67.8 13.9 %collective-permute-start.5 = (bf16[32,40,128]{2,1,0:T(8,128)(2,1)S(1)}, bf16[32,40,128]{2,1,0:T(8,128)(2,1)S(1)}, u32[]{:S(2)}, u32[]{:S(2)}) collective-permute-start(bf16[32,40,128]{2,1,0:T(8,128)(2,1)S(1)} %collective-permute-done.4.second_b.refs_4_), channel_id=1, source_target_pairs={{0,128},{16,400},{128,0},{144,272},{256,384},{272,144},{384,256},{... | collective-permute-start | bytes 983048 | tf_op jit(solution)/shard_map/ppermute | solution.py:263
  71.4 10.3 %collective-permute-start.3 = (bf16[32,40,128]{2,1,0:T(8,128)(2,1)S(1)}, bf16[32,40,128]{2,1,0:T(8,128)(2,1)S(1)}, u32[]{:S(2)}, u32[]{:S(2)}) collective-permute-start(bf16[32,40,128]{2,1,0:T(8,128)(2,1)S(1)} %collective-permute-done.2.first_a.refs_1_), channel_id=1, source_target_pairs={{0,384},{16,144},{128,256},{144,16},{256,128},{272,400},{384,0},{4... | collective-permute-start | bytes 983048 | tf_op jit(solution)/shard_map/ppermute | solution.py:263
  82.2 3.5 %collective-permute-start.8 = (bf16[640,256]{1,0:T(8,128)(2,1)S(1)}, bf16[640,256]{1,0:T(8,128)(2,1)S(1)}, u32[]{:S(2)}, u32[]{:S(2)}) collective-permute-start(bf16[640,256]{1,0:T(8,128)(2,1)S(1)} %get-tuple-element.27), channel_id=1, source_target_pairs={{0,16},{16,0},{1,17},{17,1},{2,18},{18,2},{3,19},{19,3},{4,20},{20... | collective-permute-start | bytes 983048 | tf_op jit(solution)/shard_map/ppermute | solution.py:267
  86.3 10.2 %collective-permute-start.9 = (bf16[4,320,128]{2,1,0:T(8,128)(2,1)S(1)}, bf16[4,320,128]{2,1,0:T(8,128)(2,1)S(1)}, u32[]{:S(2)}, u32[]{:S(2)}) collective-permute-start(bf16[4,320,128]{2,1,0:T(8,128)(2,1)S(1)} %get-tuple-element.31), channel_id=1, source_target_pairs={{0,384},{16,144},{128,256},{144,16},{256,128},{272,400},{384,0},{4... | collective-permute-start | bytes 983048 | tf_op jit(solution)/shard_map/ppermute | solution.py:263
  89.9 10.6 %collective-permute-start.11 = (bf16[4,320,128]{2,1,0:T(8,128)(2,1)S(1)}, bf16[4,320,128]{2,1,0:T(8,128)(2,1)S(1)}, u32[]{:S(2)}, u32[]{:S(2)}) collective-permute-start(bf16[4,320,128]{2,1,0:T(8,128)(2,1)S(1)} %get-tuple-element.32), channel_id=1, source_target_pairs={{0,384},{16,144},{128,256},{144,16},{256,128},{272,400},{384,0},{4... | collective-permute-start | bytes 983048 | tf_op jit(solution)/shard_map/ppermute | solution.py:263
  96.5 9.0 %collective-permute-start.10 = (bf16[4,320,128]{2,1,0:T(8,128)(2,1)S(1)}, bf16[4,320,128]{2,1,0:T(8,128)(2,1)S(1)}, u32[]{:S(2)}, u32[]{:S(2)}) collective-permute-start(bf16[4,320,128]{2,1,0:T(8,128)(2,1)S(1)} %shard_map.92.refs_7_), channel_id=1, source_target_pairs={{0,128},{16,400},{128,0},{144,272},{256,384},{272,144},{384,256},{... | collective-permute-start | bytes 983048 | tf_op jit(solution)/shard_map/ppermute | solution.py:263
  106.4 12.3 %all-to-all-start.1 = ((bf16[4,320,128]{2,1,0:T(8,128)(2,1)}), bf16[4,320,128]{2,1,0:T(8,128)(2,1)S(1)}, u32[]{:S(2)}, u32[]{:S(2)}) async-start(bf16[4,320,128]{2,1,0:T(8,128)(2,1)} %shard_map.94), calls=%async_computation.1 | async-start | bytes 655360 | tf_op jit(solution)/shard_map/all_to_all | solution.py:308
  109.8 15.1 %collective-permute-start.13 = (bf16[16,128,128]{2,1,0:T(8,128)(2,1)S(1)}, bf16[16,128,128]{2,1,0:T(8,128)(2,1)S(1)}, u32[]{:S(2)}, u32[]{:S(2)}) collective-permute-start(bf16[16,128,128]{2,1,0:T(8,128)(2,1)S(1)} %get-tuple-element.36), channel_id=1, source_target_pairs={{0,16},{16,0},{1,17},{17,1},{2,18},{18,2},{3,19},{19,3},{4,20},{20... | collective-permute-start | bytes 1572872 | tf_op jit(solution)/shard_map/ppermute | solution.py:267
  111.7 13.2 %collective-permute-start.12 = (bf16[16,128,128]{2,1,0:T(8,128)(2,1)S(1)}, bf16[16,128,128]{2,1,0:T(8,128)(2,1)S(1)}, u32[]{:S(2)}, u32[]{:S(2)}) collective-permute-start(bf16[16,128,128]{2,1,0:T(8,128)(2,1)S(1)} %get-tuple-element.33.after_ref), channel_id=1, source_target_pairs={{0,16},{16,0},{1,17},{17,1},{2,18},{18,2},{3,19},{19,3},{4,20},{20... | collective-permute-start | bytes 1572872 | tf_op jit(solution)/shard_map/ppermute | solution.py:267
  119.4 19.1 %all-to-all-start.2 = ((bf16[16,20,128]{2,1,0:T(8,128)(2,1)}), bf16[16,20,128]{2,1,0:T(8,128)(2,1)S(1)}, u32[]{:S(2)}, u32[]{:S(2)}) async-start(bf16[16,20,128]{2,1,0:T(8,128)(2,1)} %shard_map.95.after_ref), calls=%async_computation.2 | async-start | bytes 196608 | tf_op jit(solution)/shard_map/all_to_all | solution.py:311
